TPU v7x, 32 devices: a whole 2x2x4 slice. The times are simulated.
32 devices in a mesh: aux: 2 (over y), ao: 16 (over z, x, core).
Axes of the slice: x: 2, y: 2, z: 4, core: 2. Of those that a mesh axis runs over, the one named last changes fastest.
Arguments:
- blocks: bfloat16 [64, 4000, 4000], P('aux', 'ao'), may hold values from -6 to 6
- block_scale: float32 [64, 160], P('aux', 'ao'), may hold values from 0.3 to 3
- coeff: bfloat16 [4000, 380], P('ao'), may hold values from -0.09375 to 0.09375
- rot_coeff: bfloat16 [4000, 380], P('ao'), may hold values from -0.09375 to 0.09375
- occupation: float32 [380], replicated, may hold values from 0.2 to 2
Outputs:
- sigma: float32 [4000, 380], P('ao')
All inputs are finite; a program needn't handle non-finite values.
Results may differ from a plain program's by a relative error of at most 0.005.
Values may be sent and summed in bfloat16 or wider, within the bound.
No kernel may reach another device: no remote copies, remote signals or barrier semaphores. Data moves between devices by JAX's collectives and lax.ppermute only.
A program may use at most 256 MiB of HBM per device.

v0:
```python
import jax
import jax.numpy as jnp
from jax import lax
from jax.sharding import PartitionSpec as P

NAUX = 64
NI = 380


def body(blocks, block_scale, coeff, rot_coeff, occupation):
    groups = lax.axis_size("ao")
    whole_c, whole_r = (
        lax.all_gather(coeff, "ao", axis=0, tiled=True),
        lax.all_gather(rot_coeff, "ao", axis=0, tiled=True),
    )
    both = jnp.concatenate([whole_c, whole_r], axis=1)
    naux_loc, rows, naos = blocks.shape
    nint = coeff.shape[1]
    half = jnp.dot(blocks.reshape(naux_loc * rows, naos), both, preferred_element_type=jnp.float32)
    half = half.reshape(naux_loc, rows, 2 * nint)
    factor = jnp.repeat(block_scale, rows // block_scale.shape[1], axis=1)[:, :, None]
    half = half * factor
    h_occ = half[:, :, :nint].astype(jnp.bfloat16)
    h_rot = half[:, :, nint:].astype(jnp.bfloat16)
    weighted = coeff.astype(jnp.float32) * occupation[None, :]
    gamma_part = jnp.sum(h_rot.astype(jnp.float32) * weighted[None, :, :], axis=(1, 2))
    gamma = lax.psum(gamma_part, "ao")
    padding = -nint % groups
    padded = jnp.pad(h_rot, ((0, 0), (0, 0), (0, padding)))
    local_y = jnp.einsum(
        "pmi,mj->ipj",
        lax.all_to_all(padded, "ao", split_axis=2, concat_axis=1, tiled=True),
        whole_c,
        preferred_element_type=jnp.float32,
    )
    ymo = lax.all_gather(local_y.astype(jnp.bfloat16), "ao", axis=0, tiled=True)[:nint]
    flat_occ = h_occ.transpose(1, 0, 2).reshape(rows, naux_loc * nint)
    kterm = jnp.einsum(
        "mq,iq->mi",
        flat_occ,
        ymo.reshape(nint, naux_loc * nint),
        preferred_element_type=jnp.float32,
    )
    jterm = jnp.einsum("p,pmi->mi", gamma, h_occ.astype(jnp.float32))
    partial_sigma = 2.0 * jterm - kterm
    total = lax.psum(partial_sigma, "aux")
    return total / jnp.sqrt(jnp.float32(NAUX * NI))


def solution(mesh):
    in_specs = (P("aux", "ao", None), P("aux", "ao"), P("ao", None), P("ao", None), P())
    out_specs = P("ao", None)
    return jax.shard_map(body, mesh=mesh, in_specs=in_specs, out_specs=out_specs, check_vma=False)
```

profile of v0, /device:TPU:28, one launch (start us, length us, event | category | flops | bytes accessed | tf_op | source)
XLA Modules:
  0.0 684.4 jit_solution(1730372805657573513)
XLA Ops:
  6.5 0.0 all-gather.10.cloned.1.call-start
  6.5 0.7 all-gather.10.cloned.1.call-update
  7.3 0.0 all-gather.8.cloned.1.call-start
  7.3 0.7 all-gather.8.cloned.1.call-update
  8.0 92.0 %copy.13 = bf16[32,250,4000]{1,0,2:T(8,128)(2,1)} copy(bf16[32,250,4000]{2,0,1:T(8,128)(2,1)} %param.5) | data formatting | bytes 128000000 | tf_op args[0]
  100.0 0.0 copy-start.4
  100.0 120.8 %reshape.11 = bf16[8000,4000]{0,1:T(8,128)(2,1)} reshape(bf16[32,250,4000]{1,0,2:T(8,128)(2,1)} %copy.13) | data formatting | bytes 128000000 | tf_op jit(solution)/shard_map/reshape | solution.py:19
  220.8 0.0 copy-done.4
  220.8 0.1 copy.14
  220.9 0.1 broadcast_in_dim.2
  221.1 0.1 mul.32
  221.2 0.0 all-gather.10.cloned.1.call-done
  221.2 3.4 reshape.16
  224.6 0.0 all-gather.8.cloned.1.call-done
  224.6 4.9 reshape.14
  229.5 61.4 %convolution_bitcast_fusion = f32[8000,760]{0,1:T(8,128)} fusion(bf16[8000,4000]{0,1:T(8,128)(2,1)} %reshape.11, bf16[4000,380]{1,0:T(8,128)(2,1)S(1)} %reshape.16, bf16[4000,380]{1,0:T(8,128)(2,1)} %reshape.14), kind=kOutput, calls=%fused_computation.1 | convolution fusion | flops 48652161024 | bytes 94400000 | tf_op jit(solution)/shard_map/dot_general | solution.py:19
  290.8 38.4 %reshape.12 = f32[32,250,760]{1,0,2:T(8,128)} reshape(f32[8000,760]{0,1:T(8,128)} %convolution_bitcast_fusion) | data formatting | bytes 48640000 | tf_op jit(solution)/shard_map/reshape | solution.py:20
  329.3 24.9 %copy.15 = f32[32,250,760]{2,1,0:T(8,128)} copy(f32[32,250,760]{1,0,2:T(8,128)} %reshape.12) | data formatting | bytes 48640000 | tf_op jit(solution)/shard_map/reshape | solution.py:20
  354.1 9.4 %multiply_convert_fusion = bf16[32,250,760]{2,1,0:T(8,128)(2,1)S(1)} fusion(f32[32,250,760]{2,1,0:T(8,128)} %copy.15, f32[32,250]{1,0:T(8,128)S(1)} %mul.32), kind=kLoop, calls=%fused_computation | loop fusion | flops 12160000 | bytes 36512000 | tf_op jit(solution)/shard_map/convert.1
  363.5 0.0 copy-start
  363.5 8.3 %fusion.22 = (bf16[32,250,380]{2,1,0:T(8,128)(2,1)}, bf16[32,250,380]{2,1,0:T(8,128)(2,1)}) fusion(bf16[32,250,760]{2,1,0:T(8,128)(2,1)S(1)} %multiply_convert_fusion), kind=kLoop, calls=%fused_computation.21 | loop fusion | bytes 24320000 | tf_op jit(solution)/shard_map/slice | solution.py:23
  371.8 0.2 copy-done
  372.0 9.0 %copy.22 = bf16[32,250,380]{1,0,2:T(8,128)(2,1)} copy(bf16[32,250,380]{2,1,0:T(8,128)(2,1)} %get-tuple-element.6) | data formatting | bytes 12160000
  381.0 7.2 %pad.4.clone = bf16[32,250,384]{1,0,2:T(8,128)(2,1)} pad(bf16[32,250,380]{1,0,2:T(8,128)(2,1)} %copy.22, bf16[]{:T(256)} %constant.8.clone.1), padding=0_0x0_0x0_4 | pad | bytes 12224002 | tf_op jit(solution)/shard_map/jit(_pad)/pad | solution.py:29
  388.2 0.0 copy-start.1
  388.2 6.3 all-to-all-start
  394.6 0.0 all-gather.6.cloned.1.call-start
  394.6 0.0 copy-done.1
  394.6 2.8 reshape.19
  397.4 125.0 %all-to-all-done = bf16[32,250,384]{1,0,2:T(8,128)(2,1)} async-done(((bf16[32,250,384]{1,0,2:T(8,128)(2,1)}), bf16[32,250,384]{1,0,2:T(8,128)(2,1)}, u32[]{:S(2)}, u32[]{:S(2)}) %all-to-all-start) | async-done | bytes 6144032 | tf_op jit(solution)/shard_map/all_to_all | solution.py:32
  522.4 9.0 %copy.18 = bf16[32,16,250,24]{2,1,3,0:T(8,128)(2,1)} copy(bf16[32,16,250,24]{2,0,3,1:T(8,128)(2,1)} %bitcast.8) | data formatting | bytes 12288000 | tf_op jit(solution)/shard_map/all_to_all | solution.py:32
  531.4 0.0 copy-start.2
  531.4 14.1 %all_to_all.16 = bf16[32,4000,24]{1,2,0:T(8,128)(2,1)} reshape(bf16[32,16,250,24]{2,1,3,0:T(8,128)(2,1)} %copy.18) | data formatting | bytes 12288000 | tf_op jit(solution)/shard_map/all_to_all | solution.py:32
  545.5 0.0 copy-done.2
  545.5 0.0 copy-start.5
  545.5 6.4 fusion.8
  552.0 0.0 all-gather.6.cloned.1.call-update
  552.0 0.3 all-reduce.3.cloned.1.call-start
  552.2 0.0 copy-done.3
  552.3 0.0 copy-done.5
  552.3 8.2 %multiply_reduce_fusion = f32[32]{0:T(128)S(1)} fusion(f32[250,380]{1,0:T(8,128)S(1)} %convert_multiply_fusion, bf16[32,250,760]{2,1,0:T(8,128)(2,1)} %copy-done), kind=kLoop, calls=%fused_computation.2 | loop fusion | flops 9119968 | bytes 6460128 | tf_op jit(solution)/shard_map/reduce_sum | solution.py:26
  560.5 33.0 %psum.14 = bf16[32]{0:T(256)(128)(2,1)S(1)} all-reduce(f32[32]{0:T(128)S(1)} %multiply_reduce_fusion), channel_id=1, replica_groups=mesh['aux'=2,'ao'=16] {'ao'}, use_global_device_ids=true, to_apply=%region_1.0 | all-reduce | flops 32 | bytes 192 | tf_op jit(solution)/shard_map/psum | solution.py:27
  593.5 6.3 fusion.6
  599.8 41.5 %all-gather.6.cloned.1.call-done = bf16[384,32,380]{2,0,1:T(8,128)(2,1)} async-done(((bf16[24,32,380]{2,0,1:T(8,128)(2,1)}), bf16[384,32,380]{2,0,1:T(8,128)(2,1)}) %all-gather.6.cloned.1.call-update) | async-done | bytes 9338896 | tf_op jit(solution)/shard_map/all_gather | solution.py:36
  641.3 9.7 %fusion.14 = f32[250,380]{1,0:T(8,128)} fusion(bf16[384,32,380]{2,0,1:T(8,128)(2,1)} %all-gather.6.cloned.1.call-done, f32[1,250,380]{2,0,1:T(1,128)S(1)} %fusion.6, bf16[32,250,760]{2,1,0:T(8,128)(2,1)} %copy-done), kind=kOutput, calls=%fused_computation.14 | convolution fusion | flops 2310589952 | bytes 16488640 | tf_op jit(solution)/shard_map/mq,iq->mi/dot_general | solution.py:38
  651.0 0.0 all-reduce.3.cloned.1.call-update
  651.0 25.0 %all-reduce.3.cloned.1.call-done = f32[250,380]{1,0:T(8,128)} async-done(((f32[250,380]{1,0:T(8,128)}), f32[250,380]{1,0:T(8,128)}) %all-reduce.3.cloned.1.call-update) | async-done | bytes 380016 | tf_op jit(solution)/shard_map/psum | solution.py:46
  676.1 1.8 broadcast_multiply_fusion
  (2 shorter events, 0.0 us)
Async XLA Ops:
  6.5 214.7 %all-gather.10.cloned.1.call-start = ((), (), s32[]{:S(2)}) async-start(), calls=%async_computation.4 | async-start | bytes 3342336 | tf_op jit(solution)/shard_map/all_gather | solution.py:14
  7.3 217.3 %all-gather.8.cloned.1.call-start = ((), (), s32[]{:S(2)}) async-start(), calls=%async_computation.3 | async-start | bytes 3342336 | tf_op jit(solution)/shard_map/all_gather | solution.py:13
  100.0 120.8 %copy-start.4 = (f32[32,10]{0,1:T(8,128)S(1)}, f32[32,10]{0,1:T(8,128)}, u32[]{:S(2)}) copy-start(f32[32,10]{0,1:T(8,128)} %param.6) | copy-start | bytes 3844
  363.5 8.5 %copy-start = (bf16[32,250,760]{2,1,0:T(8,128)(2,1)}, bf16[32,250,760]{2,1,0:T(8,128)(2,1)S(1)}, u32[]{:S(2)}) copy-start(bf16[32,250,760]{2,1,0:T(8,128)(2,1)S(1)} %multiply_convert_fusion) | copy-start | bytes 36480004
  388.2 6.4 copy-start.1
  388.2 134.2 %all-to-all-start = ((bf16[32,250,384]{1,0,2:T(8,128)(2,1)}), bf16[32,250,384]{1,0,2:T(8,128)(2,1)}, u32[]{:S(2)}, u32[]{:S(2)}) async-start(bf16[32,250,384]{1,0,2:T(8,128)(2,1)} %pad.4.clone), calls=%async_computation | async-start | bytes 12582912 | tf_op jit(solution)/shard_map/all_to_all | solution.py:32
  394.6 246.7 %all-gather.6.cloned.1.call-start = ((), (), s32[]{:S(2)}) async-start(), calls=%async_computation.1 | async-start | bytes 10027008 | tf_op jit(solution)/shard_map/all_gather | solution.py:36
  531.4 14.1 %copy-start.2 = (bf16[4000,380,1]{1,0,2:T(8,128)(2,1)S(1)}, bf16[4000,380,1]{1,0,2:T(8,128)(2,1)}, u32[]{:S(2)}) copy-start(bf16[4000,380,1]{1,0,2:T(8,128)(2,1)} %reshape.19) | copy-start | bytes 9120004
  545.5 6.7 copy-start.3
  545.5 6.7 copy-start.5
  552.0 124.1 %all-reduce.3.cloned.1.call-start = ((), (), s32[]{:S(2)}) async-start(), calls=%async_computation.2 | async-start | bytes 786432 | tf_op jit(solution)/shard_map/psum | solution.py:46
Sparse Core Ops, SparseCore 0:
  9.6 44.9 all-gather.9
  56.9 43.9 all-gather.7
  552.1 89.1 all-gather.5
  651.2 24.8 all-reduce.2
where the time goes:
time: 694 us; the launch traced here: 684 us
  local copies, waits for them, and re-layouts  335 us (48%)
  waiting for transfers between devices  193 us (28%)
  matrix products  83.8 us (12%)
  blocking collectives  33 us (5%)
  other arithmetic  19.4 us (3%)
  between operations  13.2 us (2%)
    all_to_all x1, waiting for transfers between devices, body(): lax.all_to_all(padded, 'ao', split_axis=2, concat_axis=1, tiled=True)  125 us
    reshape x1, local copies, waits for them, and re-layouts, body(): blocks.reshape(naux_loc * rows, naos)  121 us
    unnamed x18, local copies, waits for them, and re-layouts  112 us
    reshape x2, local copies, waits for them, and re-layouts, body(): half = half.reshape(naux_loc, rows, 2 * nint)  63.3 us
    dot_general x1, matrix products, body(): jnp.dot(blocks.reshape(naux_loc * rows, naos), both, preferred_element_ty...  61.4 us
    all_gather x1, waiting for transfers between devices, body(): lax.all_gather(local_y.astype(jnp.bfloat16), 'ao', axis=0, tiled=True)  41.5 us
    psum x1, blocking collectives, body(): gamma = lax.psum(gamma_part, 'ao')  33 us
    psum x1, waiting for transfers between devices, body(): total = lax.psum(partial_sigma, 'aux')  25 us
  transfers between devices with their start and end apart: 5, of which 3 were waited for; matrix products, arithmetic and copies ran while one was open for 34% of the time, Pallas kernels for 0%

commit v1 on v0

v1 whole, which is shorter than its diff:
```python
import functools
import math

import jax
import jax.numpy as jnp
from jax import lax
from jax.experimental import pallas as pl
from jax.experimental.pallas import tpu as pltpu
from jax.sharding import PartitionSpec as P

BF16, F32 = jnp.bfloat16, jnp.float32
VMEM_BYTES = 50 * 2**20
LANES = 128


def up_to(value, step):
    return -(-value // step) * step


def layout_of(groups):
    core = 2 if groups % 2 == 0 else 1
    chips = groups // core
    x = 1
    while 4 * x * x <= chips and chips % (2 * x) == 0:
        x *= 2
    return chips // x, x, core


def rows_times(b_ref, m_ref, scale_ref, h_ref):
    mub, paux, naos = b_ref.shape
    step = pl.program_id(0)
    h = jnp.dot(b_ref[...].reshape(mub * paux, naos), m_ref[...], preferred_element_type=F32)
    h = h.reshape(mub, paux, -1) * scale_ref[...]
    h = h.reshape(mub * paux, -1).astype(BF16).astype(F32)
    first = pl.multiple_of(step * (mub * paux), 8)
    for t in range(h_ref.shape[0]):
        h_ref[t, pl.ds(first, mub * paux), :] = h[:, t * LANES : (t + 1) * LANES]


def rows_of(h_ref, p, paux):
    rows = h_ref.shape[1] // paux
    return jnp.concatenate(
        [h_ref[t, pl.ds(p, rows, stride=paux), :] for t in range(h_ref.shape[0])], axis=1
    )


def rot_kernel(paux, fan, subs, me_ref, b_ref, m_ref, scale_ref, ct_ref, w_ref, *rest):
    outs, gamma_ref, h_ref = rest[:-2], rest[-2], rest[-1]
    rows_times(b_ref, m_ref, scale_ref, h_ref)

    @pl.when(pl.program_id(0) == pl.num_programs(0) - 1)
    def _():
        each = paux // fan
        per = each // subs
        me = me_ref[0]
        for d in range(fan):
            base = jnp.bitwise_xor(me, d) * each
            for j in range(each):
                p = base + j
                hp = rows_of(h_ref, p, paux)
                gamma_ref[pl.ds(p, 1)] = jnp.sum(hp * w_ref[...], axis=0, keepdims=True)[None]
                y = jnp.dot(ct_ref[...], hp.astype(BF16), preferred_element_type=F32)
                outs[d * subs + j // per][j % per] = y.astype(BF16)


def occ_kernel(paux, b_ref, m_ref, scale_ref, out_ref, h_ref):
    rows_times(b_ref, m_ref, scale_ref, h_ref)

    @pl.when(pl.program_id(0) == pl.num_programs(0) - 1)
    def _():
        for p in range(paux):
            out_ref[p] = rows_of(h_ref, p, paux).astype(BF16)


def sigma_kernel(fan, each, per, first, me_ref, gamma_ref, base_ref, *rest):
    h_refs, y_refs, out_ref = rest[:fan], rest[fan:-1], rest[-1]
    step = pl.program_id(0)

    @pl.when(step == 0)
    def _():
        out_ref[...] = base_ref[...]

    acc = out_ref[...]
    for d in range(fan):
        p = jnp.bitwise_xor(me_ref[0], d) * each + first + step
        h = h_refs[d][0]
        acc = acc + (2.0 * gamma_ref[p]) * h.astype(F32)
        acc = acc - jnp.dot(h, y_refs[d][0], preferred_element_type=F32)
    out_ref[...] = acc


def block_specs(rows, nscale, paux, naos, width, chunk):
    mub = rows // nscale
    return [
        pl.BlockSpec((mub, paux, naos), lambda s, *_: (s, chunk, 0)),
        pl.BlockSpec((naos, width), lambda s, *_: (0, 0), pipeline_mode=pl.Buffered(1)),
        pl.BlockSpec((1, paux, 1), lambda s, *_: (s, chunk, 0)),
    ]


def rot_part(me, blocks, matrix, scale, ct, weighted, chunk, paux, fan, subs):
    rows, _, naos = blocks.shape
    nscale, width = scale.shape[0], matrix.shape[1]
    per = paux // fan // subs
    piece = jax.ShapeDtypeStruct((per, width, width), BF16)
    whole = lambda shape: pl.BlockSpec(shape, lambda s, *_: (0,) * len(shape))
    return pl.pallas_call(
        functools.partial(rot_kernel, paux, fan, subs),
        grid_spec=pltpu.PrefetchScalarGridSpec(
            num_scalar_prefetch=1,
            grid=(nscale,),
            in_specs=block_specs(rows, nscale, paux, naos, width, chunk)
            + [whole(ct.shape), whole(weighted.shape)],
            out_specs=[whole(piece.shape)] * (fan * subs) + [whole((paux, 1, width))],
            scratch_shapes=[pltpu.VMEM((width // LANES, rows * paux, LANES), F32)],
        ),
        out_shape=[piece] * (fan * subs) + [jax.ShapeDtypeStruct((paux, 1, width), F32)],
        compiler_params=pltpu.CompilerParams(vmem_limit_bytes=VMEM_BYTES),
        cost_estimate=pl.CostEstimate(
            flops=2 * rows * paux * naos * width, bytes_accessed=2 * rows * paux * naos, transcendentals=0
        ),
    )(me, blocks, matrix, scale, ct, weighted)


def occ_part(blocks, matrix, scale, chunk, paux):
    rows, _, naos = blocks.shape
    nscale, width = scale.shape[0], matrix.shape[1]
    return pl.pallas_call(
        functools.partial(occ_kernel, paux),
        grid=(nscale,),
        in_specs=block_specs(rows, nscale, paux, naos, width, chunk),
        out_specs=pl.BlockSpec((paux, rows, width), lambda s: (0, 0, 0)),
        out_shape=jax.ShapeDtypeStruct((paux, rows, width), BF16),
        scratch_shapes=[pltpu.VMEM((width // LANES, rows * paux, LANES), F32)],
        compiler_params=pltpu.CompilerParams(vmem_limit_bytes=VMEM_BYTES),
        cost_estimate=pl.CostEstimate(
            flops=2 * rows * paux * naos * width, bytes_accessed=2 * rows * paux * naos, transcendentals=0
        ),
    )(blocks, matrix, scale)


def sigma_part(me, gamma, base, h_occ, pieces, each, first):
    fan = len(pieces)
    per, width, _ = pieces[0].shape
    rows = h_occ.shape[1]

    def pick(d):
        return lambda s, me_ref: (jnp.bitwise_xor(me_ref[0], d) * each + first + s, 0, 0)

    return pl.pallas_call(
        functools.partial(sigma_kernel, fan, each, per, first),
        grid_spec=pltpu.PrefetchScalarGridSpec(
            num_scalar_prefetch=1,
            grid=(per,),
            in_specs=[
                pl.BlockSpec(memory_space=pltpu.SMEM),
                pl.BlockSpec((rows, width), lambda s, *_: (0, 0)),
            ]
            + [pl.BlockSpec((1, rows, width), pick(d)) for d in range(fan)]
            + [pl.BlockSpec((1, width, width), lambda s, *_: (s, 0, 0))] * fan,
            out_specs=pl.BlockSpec((rows, width), lambda s, *_: (0, 0)),
        ),
        out_shape=jax.ShapeDtypeStruct((rows, width), F32),
        compiler_params=pltpu.CompilerParams(vmem_limit_bytes=VMEM_BYTES),
        cost_estimate=pl.CostEstimate(
            flops=2 * fan * per * rows * width * width,
            bytes_accessed=4 * fan * per * width * width,
            transcendentals=0,
        ),
    )(me, gamma, base, *([h_occ] * fan), *pieces)


def body(blocks, block_scale, coeff, rot_coeff, occupation):
    groups, parts = lax.axis_size("ao"), lax.axis_size("aux")
    nz, nx, ncore = layout_of(groups)
    fan = nx * ncore
    naux, rows, naos = blocks.shape
    nint = coeff.shape[1]
    width = up_to(nint, LANES)
    index = lax.axis_index("ao")
    z = index // fan
    me = jnp.reshape(index % fan, (1,)).astype(jnp.int32)

    def swap(value, bit):
        return lax.ppermute(value, "ao", [(i, i ^ bit) for i in range(groups)])

    def along_z(value, pairs):
        return lax.ppermute(
            value, "ao", [(a * fan + i, b * fan + i) for a, b in pairs for i in range(fan)]
        )

    def sum_z(value):
        half = nz // 2
        inward = [[(k, k + 1), (nz - 1 - k, nz - 2 - k)] for k in range(half - 1)]
        for pairs in inward:
            value = value + along_z(value, pairs)
        if nz > 1:
            value = value + along_z(value, [(half - 1, half), (half, half - 1)])
        for pairs in reversed(inward):
            got = along_z(value, [(b, a) for a, b in pairs])
            outer = functools.reduce(jnp.logical_or, [z == a for a, _ in pairs])
            value = jnp.where(outer, got, value)
        return value

    def reduce_all(pieces):
        bit = 1
        bits = []
        live = list(range(fan))
        while bit < fan:
            bits.append(bit)
            sent = {d: swap(pieces[d], bit) for d in live if d & bit}
            live = [d for d in live if not d & bit]
            pieces = {d: pieces[d] + sent[d | bit] for d in live}
            bit *= 2
        total = {0: sum_z(pieces[0])}
        for bit in reversed(bits):
            total.update({d | bit: swap(v, bit) for d, v in list(total.items())})
        return [total[d] for d in range(fan)]

    def gathered(local):
        whole = lax.all_gather(local, "ao", axis=0, tiled=True)
        return jnp.pad(whole, ((0, 0), (0, width - nint)))

    paux = 16 if naux % 16 == 0 else naux
    chunks = naux // paux
    each = paux // fan
    subs = 2 if each % 2 == 0 else 1
    per = each // subs

    by_rows = blocks.transpose(1, 0, 2)
    scale = block_scale.T[:, :, None]
    ct = jnp.pad(coeff.T, ((0, width - nint), (0, 0)))
    weighted = jnp.pad(coeff.astype(F32) * occupation[None, :], ((0, 0), (0, width - nint)))
    whole_r = gathered(rot_coeff)
    whole_c = gathered(coeff)

    pieces, gammas = [], []
    for c in range(chunks):
        *out, g = rot_part(me, by_rows, whole_r, scale, ct, weighted, c, paux, fan, subs)
        pieces.append(out)
        gammas.append(g)
    gamma = lax.psum(jnp.sum(jnp.concatenate(gammas, axis=0), axis=(1, 2)), "ao")
    totals = [
        [reduce_all({d: pieces[c][d * subs + u] for d in range(fan)}) for u in range(subs)]
        for c in range(chunks)
    ]
    h_occ = [occ_part(by_rows, whole_c, scale, c, paux) for c in range(chunks)]
    sigma = jnp.zeros((rows, width), F32)
    for c in range(chunks):
        for u in range(subs):
            sigma = sigma_part(
                me, gamma[c * paux : (c + 1) * paux], sigma, h_occ[c], totals[c][u], each, u * per
            )
    bit = 1
    while bit < parts:
        sigma = sigma + lax.ppermute(sigma, "aux", [(i, i ^ bit) for i in range(parts)])
        bit *= 2
    return sigma[:, :nint] / math.sqrt(naux * parts * nint)


def solution(mesh):
    in_specs = (P("aux", "ao", None), P("aux", "ao"), P("ao", None), P("ao", None), P())
    out_specs = P("ao", None)
    return jax.shard_map(body, mesh=mesh, in_specs=in_specs, out_specs=out_specs, check_vma=False)
```

time: 694 us -> 381 us (0.55)
  the two profiles are of different devices: /device:TPU:28 before, /device:TPU:0 now
where the time goes in v1:
time: 381 us; the launch traced here: 379 us
  waiting for transfers between devices  152 us (40%)
  Pallas kernels  118 us (31%)
  starting transfers between devices  32.8 us (9%)
  blocking collectives  32.1 us (8%)
  local copies, waits for them, and re-layouts  19.8 us (5%)
  between operations  13.8 us (4%)
  other arithmetic  10.6 us (3%)
    ppermute x12, waiting for transfers between devices, along_z(): lax.ppermute(value, 'ao', [(a * fan + i, b * fan + i) for a, b in pairs f...  56.9 us
    pallas_call x2, Pallas kernels, rot_part(): pl.pallas_call(functools.partial(rot_kernel, paux, fan, subs), grid_spec=...  55.1 us
    pallas_call x2, Pallas kernels, occ_part(): pl.pallas_call(functools.partial(occ_kernel, paux), grid=(nscale,), in_sp...  51 us
    all_gather x2, waiting for transfers between devices, gathered(): whole = lax.all_gather(local, 'ao', axis=0, tiled=True)  46.6 us
    ppermute x24, waiting for transfers between devices, swap(): return lax.ppermute(value, 'ao', [(i, i ^ bit) for i in range(groups)])  39.9 us
    psum x1, blocking collectives, body(): lax.psum(jnp.sum(jnp.concatenate(gammas, axis=0), axis=(1, 2)), 'ao')  32.1 us
    ppermute x12, starting transfers between devices, along_z(): lax.ppermute(value, 'ao', [(a * fan + i, b * fan + i) for a, b in pairs f...  21.5 us
    unnamed x23, local copies, waits for them, and re-layouts  12.7 us
  transfers between devices with their start and end apart: 39, of which 15 were waited for; matrix products, arithmetic and copies ran while one was open for 7% of the time, Pallas kernels for 30%

profile of v1, /device:TPU:0, one launch (start us, length us, event | category | flops | bytes accessed | tf_op | source)
XLA Modules:
  0.0 378.6 jit_solution(12560468241395358273)
XLA Ops:
  8.0 1.1 copy.12
  11.0 46.6 %all-gather.5.cloned.1.call-done = bf16[16,250,380]{2,1,0:T(8,128)(2,1)} async-done(((bf16[1,250,380]{2,1,0:T(8,128)(2,1)}), bf16[16,250,380]{2,1,0:T(8,128)(2,1)}) %all-gather.5.cloned.1.call-update) | async-done | bytes 3040016 | tf_op jit(solution)/shard_map/all_gather | solution.py:221
  57.6 4.8 %reshape.6 = bf16[4000,380]{1,0:T(8,128)(2,1)} reshape(bf16[16,250,380]{2,1,0:T(8,128)(2,1)} %all-gather.5.cloned.1.call-done) | data formatting | bytes 6080000
  62.3 3.9 %pad.15.m_ref = bf16[4000,384]{1,0:T(8,128)(2,1)} pad(bf16[4000,380]{1,0:T(8,128)(2,1)} %reshape.6, bf16[]{:T(256)} %constant.35.clone.1), padding=0_0x0_4 | pad | bytes 6112002 | tf_op jit(solution)/shard_map/jit(_pad)/pad | solution.py:222
  66.2 27.5 %shard_map.56 = (bf16[2,384,384]{2,1,0:T(8,128)(2,1)S(1)}, bf16[2,384,384]{2,1,0:T(8,128)(2,1)S(1)}, bf16[2,384,384]{2,1,0:T(8,128)(2,1)S(1)}, bf16[2,384,384]{2...) custom-call(s32[1]{0:T(128)} %bitcast.me_ref, ...), custom_call_target="tpu_custom_call" | custom-call | flops 12288000000 | bytes 32000000 | tf_op jit(solution)/shard_map/pallas_call | solution.py:107
  93.9 27.6 %shard_map.55 = (bf16[2,384,384]{2,1,0:T(8,128)(2,1)S(1)}, bf16[2,384,384]{2,1,0:T(8,128)(2,1)S(1)}, bf16[2,384,384]{2,1,0:T(8,128)(2,1)S(1)}, bf16[2,384,384]{2...) custom-call(s32[1]{0:T(128)} %bitcast.me_ref, ...), custom_call_target="tpu_custom_call" | custom-call | flops 12288000000 | bytes 32000000 | tf_op jit(solution)/shard_map/pallas_call | solution.py:107
  123.8 1.1 collective-permute-start.29
  125.5 1.1 collective-permute-start.2
  126.8 1.0 collective-permute-start.11
  128.2 11.7 %collective-permute-done.29 = bf16[2,384,384]{2,1,0:T(8,128)(2,1)S(1)} collective-permute-done((bf16[2,384,384]{2,1,0:T(8,128)(2,1)S(1)}, bf16[2,384,384]{2,1,0:T(8,128)(2,1)S(1)}, u32[]{:S(2)}, u32[]{:S(2)}) %collective-permute-start.29) | collective-permute-done | bytes 589856 | tf_op jit(solution)/shard_map/ppermute | solution.py:185
  139.9 1.0 collective-permute-start.20
  141.1 11.5 %collective-permute-done.2 = bf16[2,384,384]{2,1,0:T(8,128)(2,1)S(1)} collective-permute-done((bf16[2,384,384]{2,1,0:T(8,128)(2,1)S(1)}, bf16[2,384,384]{2,1,0:T(8,128)(2,1)S(1)}, u32[]{:S(2)}, u32[]{:S(2)}) %collective-permute-start.2) | collective-permute-done | bytes 589856 | tf_op jit(solution)/shard_map/ppermute | solution.py:185
  152.6 3.8 %collective-permute-start.30 = (bf16[2,384,384]{2,1,0:T(8,128)(2,1)S(1)}, bf16[2,384,384]{2,1,0:T(8,128)(2,1)S(1)}, u32[]{:S(2)}, u32[]{:S(2)}) collective-permute-start(bf16[2,384,384]{2,1,0:T(8,128)(2,1)S(1)} %add_add_fusion), channel_id=1, source_target_pairs={{0,4},{1,5},{2,6},{3,7},{12,8},{13,9},{14,10},{15,11},{16,20},{17,... | collective-permute-start | bytes 1769480 | tf_op jit(solution)/shard_map/ppermute | solution.py:188
  156.5 1.3 collective-permute-start.3
  157.9 7.4 %collective-permute-done.11 = bf16[2,384,384]{2,1,0:T(8,128)(2,1)S(1)} collective-permute-done((bf16[2,384,384]{2,1,0:T(8,128)(2,1)S(1)}, bf16[2,384,384]{2,1,0:T(8,128)(2,1)S(1)}, u32[]{:S(2)}, u32[]{:S(2)}) %collective-permute-start.11) | collective-permute-done | bytes 589856 | tf_op jit(solution)/shard_map/ppermute | solution.py:185
  165.3 3.8 %collective-permute-start.12 = (bf16[2,384,384]{2,1,0:T(8,128)(2,1)S(1)}, bf16[2,384,384]{2,1,0:T(8,128)(2,1)S(1)}, u32[]{:S(2)}, u32[]{:S(2)}) collective-permute-start(bf16[2,384,384]{2,1,0:T(8,128)(2,1)S(1)} %add_add_fusion.2), channel_id=1, source_target_pairs={{0,4},{1,5},{2,6},{3,7},{12,8},{13,9},{14,10},{15,11},{16,20},{17,... | collective-permute-start | bytes 1769480 | tf_op jit(solution)/shard_map/ppermute | solution.py:188
  169.2 8.0 %collective-permute-done.20 = bf16[2,384,384]{2,1,0:T(8,128)(2,1)S(1)} collective-permute-done((bf16[2,384,384]{2,1,0:T(8,128)(2,1)S(1)}, bf16[2,384,384]{2,1,0:T(8,128)(2,1)S(1)}, u32[]{:S(2)}, u32[]{:S(2)}) %collective-permute-start.20) | collective-permute-done | bytes 589856 | tf_op jit(solution)/shard_map/ppermute | solution.py:185
  177.3 3.8 %collective-permute-start.21 = (bf16[2,384,384]{2,1,0:T(8,128)(2,1)S(1)}, bf16[2,384,384]{2,1,0:T(8,128)(2,1)S(1)}, u32[]{:S(2)}, u32[]{:S(2)}) collective-permute-start(bf16[2,384,384]{2,1,0:T(8,128)(2,1)S(1)} %add_add_fusion.1), channel_id=1, source_target_pairs={{0,4},{1,5},{2,6},{3,7},{12,8},{13,9},{14,10},{15,11},{16,20},{17,... | collective-permute-start | bytes 1769480 | tf_op jit(solution)/shard_map/ppermute | solution.py:188
  183.6 11.8 %collective-permute-done.12 = bf16[2,384,384]{2,1,0:T(8,128)(2,1)S(1)} collective-permute-done((bf16[2,384,384]{2,1,0:T(8,128)(2,1)S(1)}, bf16[2,384,384]{2,1,0:T(8,128)(2,1)S(1)}, u32[]{:S(2)}, u32[]{:S(2)}) %collective-permute-start.12) | collective-permute-done | bytes 589856 | tf_op jit(solution)/shard_map/ppermute | solution.py:188
  196.3 9.5 %collective-permute-done.21 = bf16[2,384,384]{2,1,0:T(8,128)(2,1)S(1)} collective-permute-done((bf16[2,384,384]{2,1,0:T(8,128)(2,1)S(1)}, bf16[2,384,384]{2,1,0:T(8,128)(2,1)S(1)}, u32[]{:S(2)}, u32[]{:S(2)}) %collective-permute-start.21) | collective-permute-done | bytes 589856 | tf_op jit(solution)/shard_map/ppermute | solution.py:188
  206.0 1.5 collective-permute-start.22
  207.6 1.3 collective-permute-start.32
  209.1 1.3 collective-permute-start.5
  210.4 1.0 add.88
  211.4 1.3 collective-permute-start.14
  212.7 1.2 add.93
  213.9 1.3 collective-permute-start.23
  215.2 12.1 %collective-permute-done.32 = bf16[2,384,384]{2,1,0:T(8,128)(2,1)} collective-permute-done((bf16[2,384,384]{2,1,0:T(8,128)(2,1)S(1)}, bf16[2,384,384]{2,1,0:T(8,128)(2,1)}, u32[]{:S(2)}, u32[]{:S(2)}) %collective-permute-start.32) | collective-permute-done | bytes 589856 | tf_op jit(solution)/shard_map/ppermute | solution.py:188
  227.3 1.1 broadcast_select_fusion.rest_4_
  228.9 11.0 %collective-permute-done.5 = bf16[2,384,384]{2,1,0:T(8,128)(2,1)} collective-permute-done((bf16[2,384,384]{2,1,0:T(8,128)(2,1)S(1)}, bf16[2,384,384]{2,1,0:T(8,128)(2,1)}, u32[]{:S(2)}, u32[]{:S(2)}) %collective-permute-start.5) | collective-permute-done | bytes 589856 | tf_op jit(solution)/shard_map/ppermute | solution.py:188
  239.9 1.1 broadcast_select_fusion.3.rest_4_
  241.6 4.7 %reshape.8 = bf16[4000,380]{1,0:T(8,128)(2,1)} reshape(bf16[16,250,380]{2,1,0:T(8,128)(2,1)} %all-gather.7.cloned.1.call-done) | data formatting | bytes 6080000
  246.3 2.2 pad.18.m_ref
  248.5 4.0 %collective-permute-done.14 = bf16[2,384,384]{2,1,0:T(8,128)(2,1)} collective-permute-done((bf16[2,384,384]{2,1,0:T(8,128)(2,1)}, bf16[2,384,384]{2,1,0:T(8,128)(2,1)}, u32[]{:S(2)}, u32[]{:S(2)}) %collective-permute-start.14) | collective-permute-done | bytes 589856 | tf_op jit(solution)/shard_map/ppermute | solution.py:188
  252.5 1.1 broadcast_select_fusion.2.rest_4_
  254.2 7.7 %collective-permute-done.23 = bf16[2,384,384]{2,1,0:T(8,128)(2,1)} collective-permute-done((bf16[2,384,384]{2,1,0:T(8,128)(2,1)S(1)}, bf16[2,384,384]{2,1,0:T(8,128)(2,1)}, u32[]{:S(2)}, u32[]{:S(2)}) %collective-permute-start.23) | collective-permute-done | bytes 589856 | tf_op jit(solution)/shard_map/ppermute | solution.py:188
  261.9 1.1 broadcast_select_fusion.1.rest_4_
  263.9 25.5 %shard_map.57.rest_0_.rest_1_.rest_2_.rest_3_ = bf16[16,250,384]{2,1,0:T(8,128)(2,1)} custom-call(bf16[250,32,4000]{2,1,0:T(8,128)(2,1)} %bitcast.10, bf16[4000,384]{1,0:T(8,128)(2,1)S(1)} %pad.18.m_ref, f32[10,32,1]{2,1,0:T(8,128)S(1)} %copy.13.scale_ref), custom_call_target="tpu_custom_call" | custom-call | flops 12288000000 | bytes 32000000 | tf_op jit(solution)/shard_map/pallas_call | solution.py:128
  290.8 25.5 %shard_map.60.rest_0_.rest_1_.rest_2_.rest_3_ = bf16[16,250,384]{2,1,0:T(8,128)(2,1)} custom-call(bf16[250,32,4000]{2,1,0:T(8,128)(2,1)} %bitcast.11, bf16[4000,384]{1,0:T(8,128)(2,1)S(1)} %pad.18.m_ref, f32[10,32,1]{2,1,0:T(8,128)S(1)} %copy.13.scale_ref), custom_call_target="tpu_custom_call" | custom-call | flops 12288000000 | bytes 32000000 | tf_op jit(solution)/shard_map/pallas_call | solution.py:128
  316.6 32.1 %psum.7 = f32[32]{0:T(128)S(1)} all-reduce(f32[32]{0:T(128)S(1)} %maximum_reduce_fusion), channel_id=1, replica_groups=mesh['aux'=2,'ao'=16] {'ao'}, use_global_device_ids=true, to_apply=%region_1.2 | all-reduce | flops 32 | bytes 256 | tf_op jit(solution)/shard_map/psum | solution.py:242
  348.8 1.1 copy-done.3
  349.9 1.1 copy-done.5
  350.9 2.8 shard_map.58.base_ref
  353.8 2.9 shard_map.59.base_ref
  356.7 3.0 shard_map.61.base_ref
  359.7 2.9 shard_map.62
  362.6 1.5 collective-permute-start.36
  364.1 6.8 %collective-permute-done.36 = f32[250,384]{1,0:T(8,128)S(1)} collective-permute-done((f32[250,384]{1,0:T(8,128)S(1)}, f32[250,384]{1,0:T(8,128)S(1)}, u32[]{:S(2)}, u32[]{:S(2)}) %collective-permute-start.36) | collective-permute-done | bytes 384032 | tf_op jit(solution)/shard_map/ppermute | solution.py:256
  (94 shorter events, 16.1 us)
Async XLA Ops:
  6.5 51.0 %all-gather.5.cloned.1.call-start = ((), (), s32[]{:S(2)}) async-start(), calls=%async_computation | async-start | bytes 3342336 | tf_op jit(solution)/shard_map/all_gather | solution.py:221
  7.3 234.3 %all-gather.7.cloned.1.call-start = ((), (), s32[]{:S(2)}) async-start(), calls=%async_computation.1 | async-start | bytes 3342336 | tf_op jit(solution)/shard_map/all_gather | solution.py:221
  93.7 28.7 %copy-start.9 = (bf16[2,384,384]{2,1,0:T(8,128)(2,1)S(1)}, bf16[2,384,384]{2,1,0:T(8,128)(2,1)}, u32[]{:S(2)}) copy-start(bf16[2,384,384]{2,1,0:T(8,128)(2,1)} %get-tuple-element.36) | copy-start | bytes 1769476
  93.7 29.2 %copy-start.8 = (bf16[2,384,384]{2,1,0:T(8,128)(2,1)S(1)}, bf16[2,384,384]{2,1,0:T(8,128)(2,1)}, u32[]{:S(2)}) copy-start(bf16[2,384,384]{2,1,0:T(8,128)(2,1)} %get-tuple-element.39) | copy-start | bytes 1769476
  93.7 28.9 %collective-permute-start.28 = (bf16[2,384,384]{2,1,0:T(8,128)(2,1)}, bf16[2,384,384]{2,1,0:T(8,128)(2,1)S(1)}, u32[]{:S(2)}, u32[]{:S(2)}) collective-permute-start(bf16[2,384,384]{2,1,0:T(8,128)(2,1)} %get-tuple-element.40), channel_id=1, source_target_pairs={{0,1},{1,0},{2,3},{3,2},{4,5},{5,4},{6,7},{7,6},{8,9},{9,8},{10,11... | collective-permute-start | bytes 1769480 | tf_op jit(solution)/shard_map/ppermute | solution.py:185
  121.6 5.0 %copy-start.7 = (bf16[2,384,384]{2,1,0:T(8,128)(2,1)S(1)}, bf16[2,384,384]{2,1,0:T(8,128)(2,1)}, u32[]{:S(2)}) copy-start(bf16[2,384,384]{2,1,0:T(8,128)(2,1)} %get-tuple-element.31) | copy-start | bytes 1769476
  121.6 2.2 collective-permute-start.1
  121.8 3.6 collective-permute-start.10
  122.1 4.6 %collective-permute-start.27 = (bf16[2,384,384]{2,1,0:T(8,128)(2,1)S(1)}, bf16[2,384,384]{2,1,0:T(8,128)(2,1)S(1)}, u32[]{:S(2)}, u32[]{:S(2)}) collective-permute-start(bf16[2,384,384]{2,1,0:T(8,128)(2,1)S(1)} %get-tuple-element.38), channel_id=1, source_target_pairs={{0,1},{1,0},{2,3},{3,2},{4,5},{5,4},{6,7},{7,6},{8,9},{9,8},{10,11... | collective-permute-start | bytes 1769480 | tf_op jit(solution)/shard_map/ppermute | solution.py:185
  122.3 4.4 %collective-permute-start.19 = (bf16[2,384,384]{2,1,0:T(8,128)(2,1)S(1)}, bf16[2,384,384]{2,1,0:T(8,128)(2,1)S(1)}, u32[]{:S(2)}, u32[]{:S(2)}) collective-permute-start(bf16[2,384,384]{2,1,0:T(8,128)(2,1)S(1)} %copy-done.9), channel_id=1, source_target_pairs={{0,1},{1,0},{2,3},{3,2},{4,5},{5,4},{6,7},{7,6},{8,9},{9,8},{10,11... | collective-permute-start | bytes 1769480 | tf_op jit(solution)/shard_map/ppermute | solution.py:185
  122.6 5.4 %collective-permute-start = (bf16[2,384,384]{2,1,0:T(8,128)(2,1)S(1)}, bf16[2,384,384]{2,1,0:T(8,128)(2,1)S(1)}, u32[]{:S(2)}, u32[]{:S(2)}) collective-permute-start(bf16[2,384,384]{2,1,0:T(8,128)(2,1)S(1)} %get-tuple-element.26), channel_id=1, source_target_pairs={{0,1},{1,0},{2,3},{3,2},{4,5},{5,4},{6,7},{7,6},{8,9},{9,8},{10,11... | collective-permute-start | bytes 1769480 | tf_op jit(solution)/shard_map/ppermute | solution.py:185
  123.8 16.2 %collective-permute-start.29 = (bf16[2,384,384]{2,1,0:T(8,128)(2,1)S(1)}, bf16[2,384,384]{2,1,0:T(8,128)(2,1)S(1)}, u32[]{:S(2)}, u32[]{:S(2)}) collective-permute-start(bf16[2,384,384]{2,1,0:T(8,128)(2,1)S(1)} %add.95), channel_id=1, source_target_pairs={{0,2},{1,3},{2,0},{3,1},{4,6},{5,7},{6,4},{7,5},{8,10},{9,11},{10,... | collective-permute-start | bytes 1769480 | tf_op jit(solution)/shard_map/ppermute | solution.py:185
  125.5 27.1 %collective-permute-start.2 = (bf16[2,384,384]{2,1,0:T(8,128)(2,1)S(1)}, bf16[2,384,384]{2,1,0:T(8,128)(2,1)S(1)}, u32[]{:S(2)}, u32[]{:S(2)}) collective-permute-start(bf16[2,384,384]{2,1,0:T(8,128)(2,1)S(1)} %add.80), channel_id=1, source_target_pairs={{0,2},{1,3},{2,0},{3,1},{4,6},{5,7},{6,4},{7,5},{8,10},{9,11},{10,... | collective-permute-start | bytes 1769480 | tf_op jit(solution)/shard_map/ppermute | solution.py:185
  126.7 29.8 %collective-permute-start.9 = (bf16[2,384,384]{2,1,0:T(8,128)(2,1)S(1)}, bf16[2,384,384]{2,1,0:T(8,128)(2,1)S(1)}, u32[]{:S(2)}, u32[]{:S(2)}) collective-permute-start(bf16[2,384,384]{2,1,0:T(8,128)(2,1)S(1)} %get-tuple-element.30), channel_id=1, source_target_pairs={{0,1},{1,0},{2,3},{3,2},{4,5},{5,4},{6,7},{7,6},{8,9},{9,8},{10,11... | collective-permute-start | bytes 1769480 | tf_op jit(solution)/shard_map/ppermute | solution.py:185
  126.8 38.4 %collective-permute-start.11 = (bf16[2,384,384]{2,1,0:T(8,128)(2,1)S(1)}, bf16[2,384,384]{2,1,0:T(8,128)(2,1)S(1)}, u32[]{:S(2)}, u32[]{:S(2)}) collective-permute-start(bf16[2,384,384]{2,1,0:T(8,128)(2,1)S(1)} %add.85), channel_id=1, source_target_pairs={{0,2},{1,3},{2,0},{3,1},{4,6},{5,7},{6,4},{7,5},{8,10},{9,11},{10,... | collective-permute-start | bytes 1769480 | tf_op jit(solution)/shard_map/ppermute | solution.py:185
  128.0 41.2 %collective-permute-start.18 = (bf16[2,384,384]{2,1,0:T(8,128)(2,1)S(1)}, bf16[2,384,384]{2,1,0:T(8,128)(2,1)S(1)}, u32[]{:S(2)}, u32[]{:S(2)}) collective-permute-start(bf16[2,384,384]{2,1,0:T(8,128)(2,1)S(1)} %get-tuple-element.34), channel_id=1, source_target_pairs={{0,1},{1,0},{2,3},{3,2},{4,5},{5,4},{6,7},{7,6},{8,9},{9,8},{10,11... | collective-permute-start | bytes 1769480 | tf_op jit(solution)/shard_map/ppermute | solution.py:185
  139.9 37.3 %collective-permute-start.20 = (bf16[2,384,384]{2,1,0:T(8,128)(2,1)S(1)}, bf16[2,384,384]{2,1,0:T(8,128)(2,1)S(1)}, u32[]{:S(2)}, u32[]{:S(2)}) collective-permute-start(bf16[2,384,384]{2,1,0:T(8,128)(2,1)S(1)} %add.90), channel_id=1, source_target_pairs={{0,2},{1,3},{2,0},{3,1},{4,6},{5,7},{6,4},{7,5},{8,10},{9,11},{10,... | collective-permute-start | bytes 1769480 | tf_op jit(solution)/shard_map/ppermute | solution.py:185
  152.6 28.5 %collective-permute-start.30 = (bf16[2,384,384]{2,1,0:T(8,128)(2,1)S(1)}, bf16[2,384,384]{2,1,0:T(8,128)(2,1)S(1)}, u32[]{:S(2)}, u32[]{:S(2)}) collective-permute-start(bf16[2,384,384]{2,1,0:T(8,128)(2,1)S(1)} %add_add_fusion), channel_id=1, source_target_pairs={{0,4},{1,5},{2,6},{3,7},{12,8},{13,9},{14,10},{15,11},{16,20},{17,... | collective-permute-start | bytes 1769480 | tf_op jit(solution)/shard_map/ppermute | solution.py:188
  156.5 26.3 %collective-permute-start.3 = (bf16[2,384,384]{2,1,0:T(8,128)(2,1)S(1)}, bf16[2,384,384]{2,1,0:T(8,128)(2,1)S(1)}, u32[]{:S(2)}, u32[]{:S(2)}) collective-permute-start(bf16[2,384,384]{2,1,0:T(8,128)(2,1)S(1)} %add_add_fusion.3), channel_id=1, source_target_pairs={{0,4},{1,5},{2,6},{3,7},{12,8},{13,9},{14,10},{15,11},{16,20},{17,... | collective-permute-start | bytes 1769480 | tf_op jit(solution)/shard_map/ppermute | solution.py:188
  165.3 30.1 %collective-permute-start.12 = (bf16[2,384,384]{2,1,0:T(8,128)(2,1)S(1)}, bf16[2,384,384]{2,1,0:T(8,128)(2,1)S(1)}, u32[]{:S(2)}, u32[]{:S(2)}) collective-permute-start(bf16[2,384,384]{2,1,0:T(8,128)(2,1)S(1)} %add_add_fusion.2), channel_id=1, source_target_pairs={{0,4},{1,5},{2,6},{3,7},{12,8},{13,9},{14,10},{15,11},{16,20},{17,... | collective-permute-start | bytes 1769480 | tf_op jit(solution)/shard_map/ppermute | solution.py:188
  177.3 28.5 %collective-permute-start.21 = (bf16[2,384,384]{2,1,0:T(8,128)(2,1)S(1)}, bf16[2,384,384]{2,1,0:T(8,128)(2,1)S(1)}, u32[]{:S(2)}, u32[]{:S(2)}) collective-permute-start(bf16[2,384,384]{2,1,0:T(8,128)(2,1)S(1)} %add_add_fusion.1), channel_id=1, source_target_pairs={{0,4},{1,5},{2,6},{3,7},{12,8},{13,9},{14,10},{15,11},{16,20},{17,... | collective-permute-start | bytes 1769480 | tf_op jit(solution)/shard_map/ppermute | solution.py:188
  181.3 26.2 %collective-permute-start.31 = (bf16[2,384,384]{2,1,0:T(8,128)(2,1)S(1)}, bf16[2,384,384]{2,1,0:T(8,128)(2,1)S(1)}, u32[]{:S(2)}, u32[]{:S(2)}) collective-permute-start(bf16[2,384,384]{2,1,0:T(8,128)(2,1)S(1)} %add.97), channel_id=1, source_target_pairs={{4,8},{5,9},{6,10},{7,11},{8,4},{9,5},{10,6},{11,7},{20,24},{21,25... | collective-permute-start | bytes 1769480 | tf_op jit(solution)/shard_map/ppermute | solution.py:188
  182.9 26.0 %collective-permute-start.4 = (bf16[2,384,384]{2,1,0:T(8,128)(2,1)S(1)}, bf16[2,384,384]{2,1,0:T(8,128)(2,1)S(1)}, u32[]{:S(2)}, u32[]{:S(2)}) collective-permute-start(bf16[2,384,384]{2,1,0:T(8,128)(2,1)S(1)} %add.82), channel_id=1, source_target_pairs={{4,8},{5,9},{6,10},{7,11},{8,4},{9,5},{10,6},{11,7},{20,24},{21,25... | collective-permute-start | bytes 1769480 | tf_op jit(solution)/shard_map/ppermute | solution.py:188
  195.6 14.8 %collective-permute-start.13 = (bf16[2,384,384]{2,1,0:T(8,128)(2,1)S(1)}, bf16[2,384,384]{2,1,0:T(8,128)(2,1)S(1)}, u32[]{:S(2)}, u32[]{:S(2)}) collective-permute-start(bf16[2,384,384]{2,1,0:T(8,128)(2,1)S(1)} %add.87), channel_id=1, source_target_pairs={{4,8},{5,9},{6,10},{7,11},{8,4},{9,5},{10,6},{11,7},{20,24},{21,25... | collective-permute-start | bytes 1769480 | tf_op jit(solution)/shard_map/ppermute | solution.py:188
  206.0 6.7 %collective-permute-start.22 = (bf16[2,384,384]{2,1,0:T(8,128)(2,1)S(1)}, bf16[2,384,384]{2,1,0:T(8,128)(2,1)}, u32[]{:S(2)}, u32[]{:S(2)}) collective-permute-start(bf16[2,384,384]{2,1,0:T(8,128)(2,1)S(1)} %add.92), channel_id=1, source_target_pairs={{4,8},{5,9},{6,10},{7,11},{8,4},{9,5},{10,6},{11,7},{20,24},{21,25... | collective-permute-start | bytes 1769480 | tf_op jit(solution)/shard_map/ppermute | solution.py:188
  207.6 19.7 %collective-permute-start.32 = (bf16[2,384,384]{2,1,0:T(8,128)(2,1)S(1)}, bf16[2,384,384]{2,1,0:T(8,128)(2,1)}, u32[]{:S(2)}, u32[]{:S(2)}) collective-permute-start(bf16[2,384,384]{2,1,0:T(8,128)(2,1)S(1)} %add.98), channel_id=1, source_target_pairs={{4,0},{5,1},{6,2},{7,3},{8,12},{9,13},{10,14},{11,15},{20,16},{21,... | collective-permute-start | bytes 1769480 | tf_op jit(solution)/shard_map/ppermute | solution.py:188
  209.1 30.8 %collective-permute-start.5 = (bf16[2,384,384]{2,1,0:T(8,128)(2,1)S(1)}, bf16[2,384,384]{2,1,0:T(8,128)(2,1)}, u32[]{:S(2)}, u32[]{:S(2)}) collective-permute-start(bf16[2,384,384]{2,1,0:T(8,128)(2,1)S(1)} %add.83), channel_id=1, source_target_pairs={{4,0},{5,1},{6,2},{7,3},{8,12},{9,13},{10,14},{11,15},{20,16},{21,... | collective-permute-start | bytes 1769480 | tf_op jit(solution)/shard_map/ppermute | solution.py:188
  211.4 41.2 %collective-permute-start.14 = (bf16[2,384,384]{2,1,0:T(8,128)(2,1)}, bf16[2,384,384]{2,1,0:T(8,128)(2,1)}, u32[]{:S(2)}, u32[]{:S(2)}) collective-permute-start(bf16[2,384,384]{2,1,0:T(8,128)(2,1)} %add.88), channel_id=1, source_target_pairs={{4,0},{5,1},{6,2},{7,3},{8,12},{9,13},{10,14},{11,15},{20,16},{21,... | collective-permute-start | bytes 1769480 | tf_op jit(solution)/shard_map/ppermute | solution.py:188
  213.9 32.4 %copy-start.6 = (bf16[2,384,384]{2,1,0:T(8,128)(2,1)}, bf16[2,384,384]{2,1,0:T(8,128)(2,1)S(1)}, u32[]{:S(2)}) copy-start(bf16[2,384,384]{2,1,0:T(8,128)(2,1)S(1)} %add.93) | copy-start | bytes 1769476
  213.9 48.0 %collective-permute-start.23 = (bf16[2,384,384]{2,1,0:T(8,128)(2,1)S(1)}, bf16[2,384,384]{2,1,0:T(8,128)(2,1)}, u32[]{:S(2)}, u32[]{:S(2)}) collective-permute-start(bf16[2,384,384]{2,1,0:T(8,128)(2,1)S(1)} %add.93), channel_id=1, source_target_pairs={{4,0},{5,1},{6,2},{7,3},{8,12},{9,13},{10,14},{11,15},{20,16},{21,... | collective-permute-start | bytes 1769480 | tf_op jit(solution)/shard_map/ppermute | solution.py:188
  228.4 34.7 %collective-permute-start.34 = (bf16[2,384,384]{2,1,0:T(8,128)(2,1)S(1)}, bf16[2,384,384]{2,1,0:T(8,128)(2,1)S(1)}, u32[]{:S(2)}, u32[]{:S(2)}) collective-permute-start(bf16[2,384,384]{2,1,0:T(8,128)(2,1)S(1)} %broadcast_select_fusion.rest_4_), channel_id=1, source_target_pairs={{0,2},{1,3},{2,0},{3,1},{4,6},{5,7},{6,4},{7,5},{8,10},{9,11},{10,... | collective-permute-start | bytes 1769480 | tf_op jit(solution)/shard_map/ppermute | solution.py:185
  241.0 22.7 %collective-permute-start.7 = (bf16[2,384,384]{2,1,0:T(8,128)(2,1)S(1)}, bf16[2,384,384]{2,1,0:T(8,128)(2,1)}, u32[]{:S(2)}, u32[]{:S(2)}) collective-permute-start(bf16[2,384,384]{2,1,0:T(8,128)(2,1)S(1)} %broadcast_select_fusion.3.rest_4_), channel_id=1, source_target_pairs={{0,2},{1,3},{2,0},{3,1},{4,6},{5,7},{6,4},{7,5},{8,10},{9,11},{10,... | collective-permute-start | bytes 1769480 | tf_op jit(solution)/shard_map/ppermute | solution.py:185
  253.7 36.0 %collective-permute-start.16 = (bf16[2,384,384]{2,1,0:T(8,128)(2,1)S(1)}, bf16[2,384,384]{2,1,0:T(8,128)(2,1)}, u32[]{:S(2)}, u32[]{:S(2)}) collective-permute-start(bf16[2,384,384]{2,1,0:T(8,128)(2,1)S(1)} %broadcast_select_fusion.2.rest_4_), channel_id=1, source_target_pairs={{0,2},{1,3},{2,0},{3,1},{4,6},{5,7},{6,4},{7,5},{8,10},{9,11},{10,... | collective-permute-start | bytes 1769480 | tf_op jit(solution)/shard_map/ppermute | solution.py:185
  254.2 35.8 %collective-permute-start.15 = (bf16[2,384,384]{2,1,0:T(8,128)(2,1)S(1)}, bf16[2,384,384]{2,1,0:T(8,128)(2,1)S(1)}, u32[]{:S(2)}, u32[]{:S(2)}) collective-permute-start(bf16[2,384,384]{2,1,0:T(8,128)(2,1)S(1)} %broadcast_select_fusion.2.rest_4_), channel_id=1, source_target_pairs={{0,1},{1,0},{2,3},{3,2},{4,5},{5,4},{6,7},{7,6},{8,9},{9,8},{10,11... | collective-permute-start | bytes 1769480 | tf_op jit(solution)/shard_map/ppermute | solution.py:185
  261.9 28.3 %collective-permute-start.6 = (bf16[2,384,384]{2,1,0:T(8,128)(2,1)S(1)}, bf16[2,384,384]{2,1,0:T(8,128)(2,1)S(1)}, u32[]{:S(2)}, u32[]{:S(2)}) collective-permute-start(bf16[2,384,384]{2,1,0:T(8,128)(2,1)S(1)} %broadcast_select_fusion.3.rest_4_), channel_id=1, source_target_pairs={{0,1},{1,0},{2,3},{3,2},{4,5},{5,4},{6,7},{7,6},{8,9},{9,8},{10,11... | collective-permute-start | bytes 1769480 | tf_op jit(solution)/shard_map/ppermute | solution.py:185
  263.1 26.3 %collective-permute-start.25 = (bf16[2,384,384]{2,1,0:T(8,128)(2,1)S(1)}, bf16[2,384,384]{2,1,0:T(8,128)(2,1)}, u32[]{:S(2)}, u32[]{:S(2)}) collective-permute-start(bf16[2,384,384]{2,1,0:T(8,128)(2,1)S(1)} %broadcast_select_fusion.1.rest_4_), channel_id=1, source_target_pairs={{0,2},{1,3},{2,0},{3,1},{4,6},{5,7},{6,4},{7,5},{8,10},{9,11},{10,... | collective-permute-start | bytes 1769480 | tf_op jit(solution)/shard_map/ppermute | solution.py:185
  263.7 26.8 %collective-permute-start.8 = (bf16[2,384,384]{2,1,0:T(8,128)(2,1)}, bf16[2,384,384]{2,1,0:T(8,128)(2,1)S(1)}, u32[]{:S(2)}, u32[]{:S(2)}) collective-permute-start(bf16[2,384,384]{2,1,0:T(8,128)(2,1)} %collective-permute-done.7.rest_6_), channel_id=1, source_target_pairs={{0,1},{1,0},{2,3},{3,2},{4,5},{5,4},{6,7},{7,6},{8,9},{9,8},{10,11... | collective-permute-start | bytes 1769480 | tf_op jit(solution)/shard_map/ppermute | solution.py:185
  289.4 70.2 %collective-permute-start.33 = (bf16[2,384,384]{2,1,0:T(8,128)(2,1)S(1)}, bf16[2,384,384]{2,1,0:T(8,128)(2,1)}, u32[]{:S(2)}, u32[]{:S(2)}) collective-permute-start(bf16[2,384,384]{2,1,0:T(8,128)(2,1)S(1)} %broadcast_select_fusion.rest_4_), channel_id=1, source_target_pairs={{0,1},{1,0},{2,3},{3,2},{4,5},{5,4},{6,7},{7,6},{8,9},{9,8},{10,11... | collective-permute-start | bytes 1769480 | tf_op jit(solution)/shard_map/ppermute | solution.py:185
  289.7 67.0 %collective-permute-start.24 = (bf16[2,384,384]{2,1,0:T(8,128)(2,1)S(1)}, bf16[2,384,384]{2,1,0:T(8,128)(2,1)}, u32[]{:S(2)}, u32[]{:S(2)}) collective-permute-start(bf16[2,384,384]{2,1,0:T(8,128)(2,1)S(1)} %broadcast_select_fusion.1.rest_4_), channel_id=1, source_target_pairs={{0,1},{1,0},{2,3},{3,2},{4,5},{5,4},{6,7},{7,6},{8,9},{9,8},{10,11... | collective-permute-start | bytes 1769480 | tf_op jit(solution)/shard_map/ppermute | solution.py:185
  290.0 26.3 %copy-start = (bf16[2,384,384]{2,1,0:T(8,128)(2,1)}, bf16[2,384,384]{2,1,0:T(8,128)(2,1)S(1)}, u32[]{:S(2)}) copy-start(bf16[2,384,384]{2,1,0:T(8,128)(2,1)S(1)} %collective-permute-done.15.rest_5_) | copy-start | bytes 1769476
  290.0 69.7 %collective-permute-start.35 = (bf16[2,384,384]{2,1,0:T(8,128)(2,1)S(1)}, bf16[2,384,384]{2,1,0:T(8,128)(2,1)}, u32[]{:S(2)}, u32[]{:S(2)}) collective-permute-start(bf16[2,384,384]{2,1,0:T(8,128)(2,1)S(1)} %collective-permute-done.34.rest_6_), channel_id=1, source_target_pairs={{0,1},{1,0},{2,3},{3,2},{4,5},{5,4},{6,7},{7,6},{8,9},{9,8},{10,11... | collective-permute-start | bytes 1769480 | tf_op jit(solution)/shard_map/ppermute | solution.py:185
  290.2 26.0 %copy-start.2 = (bf16[2,384,384]{2,1,0:T(8,128)(2,1)}, bf16[2,384,384]{2,1,0:T(8,128)(2,1)S(1)}, u32[]{:S(2)}) copy-start(bf16[2,384,384]{2,1,0:T(8,128)(2,1)S(1)} %collective-permute-done.6.rest_5_) | copy-start | bytes 1769476
  290.2 66.4 %collective-permute-start.26 = (bf16[2,384,384]{2,1,0:T(8,128)(2,1)}, bf16[2,384,384]{2,1,0:T(8,128)(2,1)}, u32[]{:S(2)}, u32[]{:S(2)}) collective-permute-start(bf16[2,384,384]{2,1,0:T(8,128)(2,1)} %collective-permute-done.25.rest_6_), channel_id=1, source_target_pairs={{0,1},{1,0},{2,3},{3,2},{4,5},{5,4},{6,7},{7,6},{8,9},{9,8},{10,11... | collective-permute-start | bytes 1769480 | tf_op jit(solution)/shard_map/ppermute | solution.py:185
  290.5 25.8 %copy-start.4 = (bf16[2,384,384]{2,1,0:T(8,128)(2,1)}, bf16[2,384,384]{2,1,0:T(8,128)(2,1)S(1)}, u32[]{:S(2)}) copy-start(bf16[2,384,384]{2,1,0:T(8,128)(2,1)S(1)} %collective-permute-done.8.rest_7_) | copy-start | bytes 1769476
  290.5 63.3 %collective-permute-start.17 = (bf16[2,384,384]{2,1,0:T(8,128)(2,1)}, bf16[2,384,384]{2,1,0:T(8,128)(2,1)}, u32[]{:S(2)}, u32[]{:S(2)}) collective-permute-start(bf16[2,384,384]{2,1,0:T(8,128)(2,1)} %collective-permute-done.16.rest_6_), channel_id=1, source_target_pairs={{0,1},{1,0},{2,3},{3,2},{4,5},{5,4},{6,7},{7,6},{8,9},{9,8},{10,11... | collective-permute-start | bytes 1769480 | tf_op jit(solution)/shard_map/ppermute | solution.py:185
  348.8 1.1 copy-start.3
  350.9 2.8 copy-start.1
  362.6 8.3 %collective-permute-start.36 = (f32[250,384]{1,0:T(8,128)S(1)}, f32[250,384]{1,0:T(8,128)S(1)}, u32[]{:S(2)}, u32[]{:S(2)}) collective-permute-start(f32[250,384]{1,0:T(8,128)S(1)} %shard_map.62), channel_id=1, source_target_pairs={{0,16},{16,0},{1,17},{17,1},{2,18},{18,2},{3,19},{19,3},{4,20},{20... | collective-permute-start | bytes 1152008 | tf_op jit(solution)/shard_map/ppermute | solution.py:256
  (1 other events, 1.1 us)
Sparse Core Ops, SparseCore 0:
  9.6 47.8 all-gather.4
  59.8 44.0 all-gather.6

commit v2 on v1

v2 whole, which is shorter than its diff:
```python
import functools
import math

import jax
import jax.numpy as jnp
from jax import lax
from jax.experimental import pallas as pl
from jax.experimental.pallas import tpu as pltpu
from jax.sharding import PartitionSpec as P

BF16, F32 = jnp.bfloat16, jnp.float32
VMEM_BYTES = 50 * 2**20
LANES = 128


def up_to(value, step):
    return -(-value // step) * step


def layout_of(groups):
    core = 2 if groups % 2 == 0 else 1
    chips = groups // core
    x = 1
    while 4 * x * x <= chips and chips % (2 * x) == 0:
        x *= 2
    return chips // x, x, core


def rows_times(b_ref, m_ref, scale_ref, h_ref):
    mub, paux, naos = b_ref.shape
    step = pl.program_id(0)
    h = jnp.dot(b_ref[...].reshape(mub * paux, naos), m_ref[...], preferred_element_type=F32)
    h = h.reshape(mub, paux, -1) * scale_ref[...]
    h = h.reshape(mub * paux, -1).astype(BF16).astype(F32)
    first = pl.multiple_of(step * (mub * paux), 8)
    for t in range(h_ref.shape[0]):
        h_ref[t, pl.ds(first, mub * paux), :] = h[:, t * LANES : (t + 1) * LANES]


def rows_of(h_ref, p, paux):
    rows = h_ref.shape[1] // paux
    return jnp.concatenate(
        [h_ref[t, pl.ds(p, rows, stride=paux), :] for t in range(h_ref.shape[0])], axis=1
    )


def rot_kernel(paux, fan, nz, cuts, me_ref, b_ref, m_ref, scale_ref, ct_ref, w_ref, tie_ref, *rest):
    outs, gamma_ref, h_ref = rest[:fan], rest[fan], rest[fan + 1]
    rows_times(b_ref, m_ref, scale_ref, h_ref)

    @pl.when(pl.program_id(0) == pl.num_programs(0) - 1)
    def _():
        width = ct_ref.shape[0]
        shard = width // cuts
        for d in range(0, fan, cuts):
            wide = []
            for k in range(nz):
                p = (k * fan + jnp.bitwise_xor(me_ref[0], d)) // cuts
                hp = rows_of(h_ref, p, paux)
                gamma_ref[pl.ds(p, 1)] = jnp.sum(hp * w_ref[...], axis=0, keepdims=True)[None]
                wide.append(hp.astype(BF16))
            y = jnp.dot(ct_ref[...], jnp.concatenate(wide, axis=1), preferred_element_type=F32)
            y = y.astype(BF16)
            for k in range(nz):
                for e in range(cuts):
                    outs[d + e][k] = y[e * shard : (e + 1) * shard, k * width : (k + 1) * width]


def occ_kernel(paux, b_ref, m_ref, scale_ref, tie_ref, out_ref, h_ref):
    rows_times(b_ref, m_ref, scale_ref, h_ref)

    @pl.when(pl.program_id(0) == pl.num_programs(0) - 1)
    def _():
        for p in range(paux):
            out_ref[p] = rows_of(h_ref, p, paux).astype(BF16)


def sigma_kernel(batch, gamma_ref, base_ref, h_ref, y_ref, out_ref):
    step = pl.program_id(0)

    @pl.when(step == 0)
    def _():
        out_ref[...] = base_ref[...]

    h = jnp.concatenate([h_ref[b] for b in range(batch)], axis=1)
    y = y_ref[...].reshape(-1, y_ref.shape[2])
    acc = out_ref[...] - jnp.dot(h, y, preferred_element_type=F32)
    for b in range(batch):
        acc = acc + (2.0 * gamma_ref[step * batch + b]) * h_ref[b].astype(F32)
    out_ref[...] = acc


def cost(flops, nbytes):
    return pl.CostEstimate(flops=flops, bytes_accessed=nbytes, transcendentals=0)


def block_specs(rows, nscale, paux, naos, width, chunk):
    mub = rows // nscale
    return [
        pl.BlockSpec((mub, paux, naos), lambda s, *_: (s, chunk, 0)),
        pl.BlockSpec((naos, width), lambda s, *_: (0, 0), pipeline_mode=pl.Buffered(1)),
        pl.BlockSpec((1, paux, 1), lambda s, *_: (s, chunk, 0)),
    ]


def rot_part(me, blocks, matrix, scale, ct, weighted, tie, chunk, paux, fan, nz, cuts):
    rows, _, naos = blocks.shape
    nscale, width = scale.shape[0], matrix.shape[1]
    piece = jax.ShapeDtypeStruct((nz, width // cuts, width), BF16)

    def whole(shape):
        return pl.BlockSpec(shape, lambda s, *_: (0,) * len(shape))

    return pl.pallas_call(
        functools.partial(rot_kernel, paux, fan, nz, cuts),
        grid_spec=pltpu.PrefetchScalarGridSpec(
            num_scalar_prefetch=1,
            grid=(nscale,),
            in_specs=block_specs(rows, nscale, paux, naos, width, chunk)
            + [whole(ct.shape), whole(weighted.shape), pl.BlockSpec(memory_space=pl.ANY)],
            out_specs=[whole(piece.shape)] * fan + [whole((paux, 1, width))],
            scratch_shapes=[pltpu.VMEM((width // LANES, rows * paux, LANES), F32)],
        ),
        out_shape=[piece] * fan + [jax.ShapeDtypeStruct((paux, 1, width), F32)],
        compiler_params=pltpu.CompilerParams(vmem_limit_bytes=VMEM_BYTES),
        cost_estimate=cost(2 * rows * paux * naos * width, 2 * rows * paux * naos),
    )(me, blocks, matrix, scale, ct, weighted, tie)


def occ_part(blocks, matrix, scale, tie, chunk, paux):
    rows, _, naos = blocks.shape
    nscale, width = scale.shape[0], matrix.shape[1]
    return pl.pallas_call(
        functools.partial(occ_kernel, paux),
        grid=(nscale,),
        in_specs=block_specs(rows, nscale, paux, naos, width, chunk)
        + [pl.BlockSpec(memory_space=pl.ANY)],
        out_specs=pl.BlockSpec((paux, rows, width), lambda s: (0, 0, 0)),
        out_shape=jax.ShapeDtypeStruct((paux, rows, width), BF16),
        scratch_shapes=[pltpu.VMEM((width // LANES, rows * paux, LANES), F32)],
        compiler_params=pltpu.CompilerParams(vmem_limit_bytes=VMEM_BYTES),
        cost_estimate=cost(2 * rows * paux * naos * width, 2 * rows * paux * naos),
    )(blocks, matrix, scale, tie)


def sigma_part(gamma, base, h_occ, ymo):
    paux, width, _ = ymo.shape
    rows = h_occ.shape[1]
    batch = 4 if paux % 4 == 0 else 1
    total = pl.BlockSpec((rows, width), lambda s: (0, 0))
    return pl.pallas_call(
        functools.partial(sigma_kernel, batch),
        grid=(paux // batch,),
        in_specs=[
            pl.BlockSpec(memory_space=pltpu.SMEM),
            total,
            pl.BlockSpec((batch, rows, width), lambda s: (s, 0, 0)),
            pl.BlockSpec((batch, width, width), lambda s: (s, 0, 0)),
        ],
        out_specs=total,
        out_shape=jax.ShapeDtypeStruct((rows, width), F32),
        compiler_params=pltpu.CompilerParams(vmem_limit_bytes=VMEM_BYTES),
        cost_estimate=cost(2 * rows * paux * width * width, 2 * paux * width * width),
    )(gamma, base, h_occ, ymo)


def after(value, others):
    return lax.optimization_barrier((value, others))[0]


def body(blocks, block_scale, coeff, rot_coeff, occupation):
    groups, parts = lax.axis_size("ao"), lax.axis_size("aux")
    nz, nx, ncore = layout_of(groups)
    fan = nx * ncore
    naux, rows, naos = blocks.shape
    nint = coeff.shape[1]
    width = up_to(nint, LANES)
    index = lax.axis_index("ao")
    z = index // fan
    me = jnp.reshape(index % fan, (1,)).astype(jnp.int32)

    def swap(value, bit):
        return lax.ppermute(value, "ao", [(i, i ^ bit) for i in range(groups)])

    def turn_z(value, by):
        return lax.ppermute(value, "ao", [(i, (i + by * fan) % groups) for i in range(groups)])

    def pick(value, k):
        return lax.dynamic_index_in_dim(value, k % nz, 0, keepdims=False)

    def gathered(local):
        wide = jnp.pad(local, ((0, 0), (0, width - nint)))
        return lax.all_gather(wide, "ao", axis=0, tiled=True)

    paux = 8 if naux % 8 == 0 else naux
    chunks = naux // paux
    cuts = groups // paux

    by_rows = blocks.transpose(1, 0, 2)
    scale = block_scale.T[:, :, None]
    ct = jnp.pad(coeff.T, ((0, width - nint), (0, 0))).reshape(cuts, width // cuts, rows)
    ct = jnp.concatenate(
        [lax.dynamic_index_in_dim(ct, index % cuts ^ e, 0, keepdims=False) for e in range(cuts)]
    )
    weighted = jnp.pad(coeff.astype(F32) * occupation[None, :], ((0, 0), (0, width - nint)))
    whole_r = gathered(rot_coeff)
    whole_c = gathered(coeff)
    bits = [1 << k for k in range(fan.bit_length() - 1)]

    def reduce_steps(first):
        live = dict(enumerate(first))
        for bit in bits:
            sent = {d: swap(v, bit) for d, v in live.items() if d & bit}
            sent = yield sent, list(live.values())
            live = {d: v + sent[d | bit] for d, v in live.items() if not d & bit}
        mine = live[0]
        got = [turn_z(pick(mine, z + d), d) for d in range(1, nz)]
        got = yield got, mine
        total = pick(mine, z).astype(F32)
        for part in got:
            total = total + part.astype(F32)
        shard_sum = total.astype(BF16)
        whole = lax.all_gather(shard_sum, "ao", axis=0, tiled=True)
        yield whole.reshape(paux, width, width), shard_sum

    flows, waiting, occ, gammas = [], [], [], []
    start = jnp.zeros((8, LANES), F32)

    def in_transit(c):
        return not isinstance(waiting[c], jax.Array)

    def advance(which, done=()):
        which = [c for c in which if in_transit(c)]
        arrived = after([waiting[c] for c in which], done)
        for c, got in zip(which, arrived):
            waiting[c], marks[c] = flows[c].send(got)

    marks = {}
    for c in range(chunks):
        *first, g = rot_part(
            me, by_rows, whole_r, scale, ct, weighted, after(start, marks), c, paux, fan, nz, cuts
        )
        gammas.append(g)
        flows.append(reduce_steps(first))
        got, marks[c] = next(flows[c])
        waiting.append(got)
        advance(range(c + 1), g)
    gamma = jnp.sum(jnp.concatenate(gammas, axis=0), axis=(1, 2))
    bit = 1
    for c in range(chunks):
        got = swap(gamma, bit) if bit < groups else None
        out = occ_part(by_rows, whole_c, scale, after(start, (marks, gamma)), c, paux)
        occ.append(out)
        if got is not None:
            gamma = gamma + after(got, out)
            bit *= 2
        if any(in_transit(e) for e in range(chunks)):
            advance(range(chunks), out)
    while any(in_transit(e) for e in range(chunks)):
        advance(range(chunks))
    while bit < groups:
        gamma = gamma + swap(gamma, bit)
        bit *= 2

    sigma = jnp.zeros((rows, width), F32)
    for c in range(chunks):
        sigma = sigma_part(gamma[c * paux : (c + 1) * paux], sigma, occ[c], waiting[c])
    bit = 1
    while bit < parts:
        sigma = sigma + lax.ppermute(sigma, "aux", [(i, i ^ bit) for i in range(parts)])
        bit *= 2
    return sigma[:, :nint] / math.sqrt(naux * parts * nint)


def solution(mesh):
    in_specs = (P("aux", "ao", None), P("aux", "ao"), P("ao", None), P("ao", None), P())
    out_specs = P("ao", None)
    return jax.shard_map(body, mesh=mesh, in_specs=in_specs, out_specs=out_specs, check_vma=False)
```

time: 381 us -> 374 us (0.982)
  the two profiles are of different devices: /device:TPU:0 before, /device:TPU:28 now
where the time goes in v2:
time: 374 us; the launch traced here: 369 us
  Pallas kernels  137 us (37%)
  waiting for transfers between devices  131 us (35%)
  starting transfers between devices  44.9 us (12%)
  local copies, waits for them, and re-layouts  23.8 us (6%)
  other arithmetic  17.7 us (5%)
  between operations  13.9 us (4%)
    pallas_call x4, Pallas kernels, rot_part(): pl.pallas_call(functools.partial(rot_kernel, paux, fan, nz, cuts), grid_s...  64.5 us
    pallas_call x4, Pallas kernels, occ_part(): pl.pallas_call(functools.partial(occ_kernel, paux), grid=(nscale,), in_sp...  62.1 us
    all_gather x2, waiting for transfers between devices, gathered(): return lax.all_gather(wide, 'ao', axis=0, tiled=True)  41.6 us
    all_gather x4, waiting for transfers between devices, reduce_steps(): whole = lax.all_gather(shard_sum, 'ao', axis=0, tiled=True)  36.9 us
    ppermute x12, starting transfers between devices, turn_z(): lax.ppermute(value, 'ao', [(i, (i + by * fan) % groups) for i in range(gr...  35 us
    ppermute x12, waiting for transfers between devices, turn_z(): lax.ppermute(value, 'ao', [(i, (i + by * fan) % groups) for i in range(gr...  21.6 us
    unnamed x31, local copies, waits for them, and re-layouts  20.8 us
    ppermute x16, waiting for transfers between devices, swap(): return lax.ppermute(value, 'ao', [(i, i ^ bit) for i in range(groups)])  20.4 us
  transfers between devices with their start and end apart: 35, of which 16 were waited for; matrix products, arithmetic and copies ran while one was open for 9% of the time, Pallas kernels for 37%

profile of v2, /device:TPU:28, one launch (start us, length us, event | category | flops | bytes accessed | tf_op | source)
XLA Modules:
  0.0 368.6 jit_solution(18001855537338317630)
XLA Ops:
  6.5 1.6 pad_bitcast_fusion.1
  8.2 1.6 pad_bitcast_fusion
  13.0 41.6 %all-gather.17.cloned.1.call-done = bf16[16,250,384]{2,1,0:T(8,128)(2,1)} async-done(((bf16[1,250,384]{2,1,0:T(8,128)(2,1)}), bf16[16,250,384]{2,1,0:T(8,128)(2,1)}) %all-gather.17.cloned.1.call-update) | async-done | bytes 3072016 | tf_op jit(solution)/shard_map/all_gather | solution.py:193
  54.6 4.5 %reshape.38.m_ref = bf16[4000,384]{1,0:T(8,128)(2,1)} reshape(bf16[16,250,384]{2,1,0:T(8,128)(2,1)} %all-gather.17.cloned.1.call-done) | data formatting | bytes 6144000
  59.1 16.1 %shard_map.55 = (bf16[4,192,384]{2,1,0:T(8,128)(2,1)S(1)}, bf16[4,192,384]{2,1,0:T(8,128)(2,1)S(1)}, bf16[4,192,384]{2,1,0:T(8,128)(2,1)S(1)}, bf16[4,192,384]{2,1,0:T(8,128)(2,1)S(1)}, f32[8,1,384]{2,1,0:T(1,128)S(1)}) custom-call(s32[1]{0:T(128)} %bitcast.me_ref, bf16[250,32,4000]{2,1,0:T(8,128)(2,1)} %bitcast.55, bf16[4000,384]{1,0:T(8,128)(2,1)} %reshape.38.m_ref, ...), custom_call_target="tpu_custom_call" | custom-call | flops 6144000000 | bytes 16000000 | tf_op jit(solution)/shard_map/pallas_call | solution.py:114
  75.9 1.5 collective-permute-done
  78.5 16.2 %shard_map.56 = (bf16[4,192,384]{2,1,0:T(8,128)(2,1)S(1)}, bf16[4,192,384]{2,1,0:T(8,128)(2,1)S(1)}, bf16[4,192,384]{2,1,0:T(8,128)(2,1)S(1)}, bf16[4,192,384]{2,1,0:T(8,128)(2,1)S(1)}, f32[8,1,384]{2,1,0:T(1,128)S(1)}) custom-call(s32[1]{0:T(128)} %bitcast.me_ref, bf16[250,32,4000]{2,1,0:T(8,128)(2,1)} %bitcast.56, bf16[4000,384]{1,0:T(8,128)(2,1)} %reshape.38.m_ref, ...), custom_call_target="tpu_custom_call" | custom-call | flops 6144000000 | bytes 16000000 | tf_op jit(solution)/shard_map/pallas_call | solution.py:114
  97.8 12.9 %collective-permute-done.2 = bf16[4,192,384]{2,1,0:T(8,128)(2,1)S(1)} collective-permute-done((bf16[4,192,384]{2,1,0:T(8,128)(2,1)S(1)}, bf16[4,192,384]{2,1,0:T(8,128)(2,1)S(1)}, u32[]{:S(2)}, u32[]{:S(2)}) %collective-permute-start.2) | collective-permute-done | bytes 589856 | tf_op jit(solution)/shard_map/ppermute | solution.py:183
  113.7 16.1 %shard_map.57 = (bf16[4,192,384]{2,1,0:T(8,128)(2,1)S(1)}, bf16[4,192,384]{2,1,0:T(8,128)(2,1)S(1)}, bf16[4,192,384]{2,1,0:T(8,128)(2,1)S(1)}, bf16[4,192,384]{2,1,0:T(8,128)(2,1)S(1)}, f32[8,1,384]{2,1,0:T(1,128)S(1)}) custom-call(s32[1]{0:T(128)} %bitcast.me_ref, bf16[250,32,4000]{2,1,0:T(8,128)(2,1)} %bitcast.57, bf16[4000,384]{1,0:T(8,128)(2,1)} %reshape.38.m_ref, ...), custom_call_target="tpu_custom_call" | custom-call | flops 6144000000 | bytes 16000000 | tf_op jit(solution)/shard_map/pallas_call | solution.py:114
  131.0 1.8 dynamic-slice_bitcast_fusion.9
  132.8 1.8 collective-permute-start.5
  135.6 3.3 collective-permute-done.5
  138.9 8.3 %collective-permute-start.7 = (bf16[192,384]{1,0:T(8,128)(2,1)}, bf16[192,384]{1,0:T(8,128)(2,1)}, u32[]{:S(2)}, u32[]{:S(2)}) collective-permute-start(bf16[192,384]{1,0:T(8,128)(2,1)} %get-tuple-element.124), channel_id=1, source_target_pairs={{0,12},{1,13},{2,14},{3,15},{4,0},{5,1},{6,2},{7,3},{8,4},{9,5},{1... | collective-permute-start | bytes 442376 | tf_op jit(solution)/shard_map/ppermute | solution.py:186
  147.2 1.4 collective-permute-done.6
  148.6 1.6 collective-permute-done.7
  150.2 1.7 fusion.12
  152.2 1.4 add.201
  153.6 1.2 add.203
  154.8 2.0 add.202
  156.9 16.1 %shard_map.58 = (bf16[4,192,384]{2,1,0:T(8,128)(2,1)S(1)}, bf16[4,192,384]{2,1,0:T(8,128)(2,1)S(1)}, bf16[4,192,384]{2,1,0:T(8,128)(2,1)S(1)}, bf16[4,192,384]{2,1,0:T(8,128)(2,1)S(1)}, f32[8,1,384]{2,1,0:T(1,128)S(1)}) custom-call(s32[1]{0:T(128)} %bitcast.me_ref, bf16[250,32,4000]{2,1,0:T(8,128)(2,1)} %bitcast.58, bf16[4000,384]{1,0:T(8,128)(2,1)} %reshape.38.m_ref, ...), custom_call_target="tpu_custom_call" | custom-call | flops 6144000000 | bytes 16000000 | tf_op jit(solution)/shard_map/pallas_call | solution.py:114
  173.6 1.4 collective-permute-start.15
  175.1 3.9 %collective-permute-start.13 = (bf16[192,384]{1,0:T(8,128)(2,1)S(1)}, bf16[192,384]{1,0:T(8,128)(2,1)S(1)}, u32[]{:S(2)}, u32[]{:S(2)}) collective-permute-start(bf16[192,384]{1,0:T(8,128)(2,1)S(1)} %get-tuple-element.122), channel_id=1, source_target_pairs={{0,8},{1,9},{2,10},{3,11},{4,12},{5,13},{6,14},{7,15},{8,0},{9,1},... | collective-permute-start | bytes 442376 | tf_op jit(solution)/shard_map/ppermute | solution.py:186
  179.0 5.5 %collective-permute-done.12 = bf16[192,384]{1,0:T(8,128)(2,1)S(1)} collective-permute-done((bf16[192,384]{1,0:T(8,128)(2,1)S(1)}, bf16[192,384]{1,0:T(8,128)(2,1)S(1)}, u32[]{:S(2)}, u32[]{:S(2)}) %collective-permute-start.12) | collective-permute-done | bytes 147488 | tf_op jit(solution)/shard_map/ppermute | solution.py:186
  184.5 12.6 %collective-permute-start.14 = (bf16[192,384]{1,0:T(8,128)(2,1)S(1)}, bf16[192,384]{1,0:T(8,128)(2,1)S(1)}, u32[]{:S(2)}, u32[]{:S(2)}) collective-permute-start(bf16[192,384]{1,0:T(8,128)(2,1)S(1)} %get-tuple-element.121), channel_id=1, source_target_pairs={{0,12},{1,13},{2,14},{3,15},{4,0},{5,1},{6,2},{7,3},{8,4},{9,5},{1... | collective-permute-start | bytes 442376 | tf_op jit(solution)/shard_map/ppermute | solution.py:186
  197.1 4.4 %collective-permute-done.13 = bf16[192,384]{1,0:T(8,128)(2,1)S(1)} collective-permute-done((bf16[192,384]{1,0:T(8,128)(2,1)S(1)}, bf16[192,384]{1,0:T(8,128)(2,1)S(1)}, u32[]{:S(2)}, u32[]{:S(2)}) %collective-permute-start.13) | collective-permute-done | bytes 147488 | tf_op jit(solution)/shard_map/ppermute | solution.py:186
  204.0 4.5 %reshape.40.m_ref = bf16[4000,384]{1,0:T(8,128)(2,1)} reshape(bf16[16,250,384]{2,1,0:T(8,128)(2,1)} %all-gather.19.cloned.1.call-done) | data formatting | bytes 6144000
  208.9 1.2 add.207
  210.1 1.2 add.209
  212.5 2.2 collective-permute-start.20
  215.0 15.5 %shard_map.59.h_ref = bf16[8,250,384]{2,1,0:T(8,128)(2,1)S(1)} custom-call(bf16[250,32,4000]{2,1,0:T(8,128)(2,1)} %bitcast.59, bf16[4000,384]{1,0:T(8,128)(2,1)} %reshape.40.m_ref, f32[10,32,1]{2,1,0:T(8,128)S(1)} %copy.18.scale_ref, f32[8,128]{1,0:T(8,128)S(1)} %broadcast_in_dim.11.tie_ref), custom_call_target="tpu_custom_call" | custom-call | flops 6144000000 | bytes 16000000 | tf_op jit(solution)/shard_map/pallas_call | solution.py:133
  231.5 1.1 collective-permute-done.11
  232.6 1.2 add.214
  233.9 3.9 %collective-permute-start.24 = (bf16[192,384]{1,0:T(8,128)(2,1)S(1)}, bf16[192,384]{1,0:T(8,128)(2,1)S(1)}, u32[]{:S(2)}, u32[]{:S(2)}) collective-permute-start(bf16[192,384]{1,0:T(8,128)(2,1)S(1)} %get-tuple-element.117), channel_id=1, source_target_pairs={{0,4},{1,5},{2,6},{3,7},{4,8},{5,9},{6,10},{7,11},{8,12},{9,13},{1... | collective-permute-start | bytes 442376 | tf_op jit(solution)/shard_map/ppermute | solution.py:186
  238.4 15.5 %shard_map.60.h_ref = bf16[8,250,384]{2,1,0:T(8,128)(2,1)S(1)} custom-call(bf16[250,32,4000]{2,1,0:T(8,128)(2,1)} %bitcast.60, bf16[4000,384]{1,0:T(8,128)(2,1)} %reshape.40.m_ref, f32[10,32,1]{2,1,0:T(8,128)S(1)} %copy.18.scale_ref, f32[8,128]{1,0:T(8,128)S(1)} %broadcast_in_dim.11.tie_ref), custom_call_target="tpu_custom_call" | custom-call | flops 6144000000 | bytes 16000000 | tf_op jit(solution)/shard_map/pallas_call | solution.py:133
  253.9 5.4 %collective-permute-done.25 = bf16[192,384]{1,0:T(8,128)(2,1)S(1)} collective-permute-done((bf16[192,384]{1,0:T(8,128)(2,1)S(1)}, bf16[192,384]{1,0:T(8,128)(2,1)S(1)}, u32[]{:S(2)}, u32[]{:S(2)}) %collective-permute-start.25) | collective-permute-done | bytes 147488 | tf_op jit(solution)/shard_map/ppermute | solution.py:186
  260.0 1.5 collective-permute-start.18
  261.6 2.1 collective-permute-done.18
  263.6 15.6 %shard_map.61.h_ref = bf16[8,250,384]{2,1,0:T(8,128)(2,1)S(1)} custom-call(bf16[250,32,4000]{2,1,0:T(8,128)(2,1)} %bitcast.61, bf16[4000,384]{1,0:T(8,128)(2,1)} %reshape.40.m_ref, f32[10,32,1]{2,1,0:T(8,128)S(1)} %copy.18.scale_ref, f32[8,128]{1,0:T(8,128)S(1)} %broadcast_in_dim.11.tie_ref), custom_call_target="tpu_custom_call" | custom-call | flops 6144000000 | bytes 16000000 | tf_op jit(solution)/shard_map/pallas_call | solution.py:133
  279.2 1.2 copy-done
  280.4 1.5 collective-permute-start.27
  281.9 15.5 %shard_map.62.h_ref = bf16[8,250,384]{2,1,0:T(8,128)(2,1)S(1)} custom-call(bf16[250,32,4000]{2,1,0:T(8,128)(2,1)} %bitcast.62, bf16[4000,384]{1,0:T(8,128)(2,1)} %reshape.40.m_ref, f32[10,32,1]{2,1,0:T(8,128)S(1)} %copy.18.scale_ref, f32[8,128]{1,0:T(8,128)S(1)} %broadcast_in_dim.11.tie_ref), custom_call_target="tpu_custom_call" | custom-call | flops 6144000000 | bytes 16000000 | tf_op jit(solution)/shard_map/pallas_call | solution.py:133
  297.4 1.1 copy-done.2
  298.7 2.6 shard_map.63.base_ref
  303.0 2.7 shard_map.64.base_ref
  307.4 2.7 shard_map.65.base_ref
  310.1 36.9 %all-gather.15.cloned.1.call-done = bf16[3072,384]{1,0:T(8,128)(2,1)} async-done(((bf16[192,384]{1,0:T(8,128)(2,1)}), bf16[3072,384]{1,0:T(8,128)(2,1)}) %all-gather.15.cloned.1.call-update) | async-done | bytes 2359312 | tf_op jit(solution)/shard_map/all_gather | solution.py:223
  347.0 2.6 shard_map.66
  350.2 10.7 %collective-permute-done.28 = f32[250,384]{1,0:T(8,128)S(1)} collective-permute-done((f32[250,384]{1,0:T(8,128)S(1)}, f32[250,384]{1,0:T(8,128)S(1)}, u32[]{:S(2)}, u32[]{:S(2)}) %collective-permute-start.28) | collective-permute-done | bytes 384032 | tf_op jit(solution)/shard_map/ppermute | solution.py:270
  (106 shorter events, 25.7 us)
Async XLA Ops:
  6.5 48.1 %all-gather.17.cloned.1.call-start = ((), (), s32[]{:S(2)}) async-start(), calls=%async_computation.4 | async-start | bytes 3342336 | tf_op jit(solution)/shard_map/all_gather | solution.py:193
  8.2 195.8 %all-gather.19.cloned.1.call-start = ((), (), s32[]{:S(2)}) async-start(), calls=%async_computation.5 | async-start | bytes 3342336 | tf_op jit(solution)/shard_map/all_gather | solution.py:193
  9.9 288.7 %all-gather.9.cloned.1.call-start = ((), (), s32[]{:S(2)}) async-start(), calls=%async_computation | async-start | bytes 2506752 | tf_op jit(solution)/shard_map/all_gather | solution.py:223
  75.3 2.1 collective-permute-start
  75.6 2.6 collective-permute-start.1
  94.7 2.1 collective-permute-start.3
  95.0 2.8 collective-permute-start.4
  95.2 15.5 %collective-permute-start.2 = (bf16[4,192,384]{2,1,0:T(8,128)(2,1)S(1)}, bf16[4,192,384]{2,1,0:T(8,128)(2,1)S(1)}, u32[]{:S(2)}, u32[]{:S(2)}) collective-permute-start(bf16[4,192,384]{2,1,0:T(8,128)(2,1)S(1)} %add.183), channel_id=1, source_target_pairs={{0,2},{1,3},{2,0},{3,1},{4,6},{5,7},{6,4},{7,5},{8,10},{9,11},{10,... | collective-permute-start | bytes 1769480 | tf_op jit(solution)/shard_map/ppermute | solution.py:183
  129.8 20.5 %collective-permute-start.10 = (bf16[4,192,384]{2,1,0:T(8,128)(2,1)S(1)}, bf16[4,192,384]{2,1,0:T(8,128)(2,1)}, u32[]{:S(2)}, u32[]{:S(2)}) collective-permute-start(bf16[4,192,384]{2,1,0:T(8,128)(2,1)S(1)} %get-tuple-element.79), channel_id=1, source_target_pairs={{0,1},{1,0},{2,3},{3,2},{4,5},{5,4},{6,7},{7,6},{8,9},{9,8},{10,11... | collective-permute-start | bytes 1769480 | tf_op jit(solution)/shard_map/ppermute | solution.py:183
  129.8 20.4 %collective-permute-start.9 = (bf16[4,192,384]{2,1,0:T(8,128)(2,1)S(1)}, bf16[4,192,384]{2,1,0:T(8,128)(2,1)}, u32[]{:S(2)}, u32[]{:S(2)}) collective-permute-start(bf16[4,192,384]{2,1,0:T(8,128)(2,1)S(1)} %get-tuple-element.78), channel_id=1, source_target_pairs={{0,1},{1,0},{2,3},{3,2},{4,5},{5,4},{6,7},{7,6},{8,9},{9,8},{10,11... | collective-permute-start | bytes 1769480 | tf_op jit(solution)/shard_map/ppermute | solution.py:183
  130.3 19.9 %collective-permute-start.8 = (bf16[4,192,384]{2,1,0:T(8,128)(2,1)}, bf16[4,192,384]{2,1,0:T(8,128)(2,1)}, u32[]{:S(2)}, u32[]{:S(2)}) collective-permute-start(bf16[4,192,384]{2,1,0:T(8,128)(2,1)} %add.186), channel_id=1, source_target_pairs={{0,2},{1,3},{2,0},{3,1},{4,6},{5,7},{6,4},{7,5},{8,10},{9,11},{10,... | collective-permute-start | bytes 1769480 | tf_op jit(solution)/shard_map/ppermute | solution.py:183
  132.8 6.1 %collective-permute-start.5 = (bf16[192,384]{1,0:T(8,128)(2,1)S(1)}, bf16[192,384]{1,0:T(8,128)(2,1)S(1)}, u32[]{:S(2)}, u32[]{:S(2)}) collective-permute-start(bf16[192,384]{1,0:T(8,128)(2,1)S(1)} %get-tuple-element.126), channel_id=1, source_target_pairs={{0,4},{1,5},{2,6},{3,7},{4,8},{5,9},{6,10},{7,11},{8,12},{9,13},{1... | collective-permute-start | bytes 442376 | tf_op jit(solution)/shard_map/ppermute | solution.py:186
  134.6 14.0 %collective-permute-start.6 = (bf16[192,384]{1,0:T(8,128)(2,1)}, bf16[192,384]{1,0:T(8,128)(2,1)S(1)}, u32[]{:S(2)}, u32[]{:S(2)}) collective-permute-start(bf16[192,384]{1,0:T(8,128)(2,1)} %get-tuple-element.125), channel_id=1, source_target_pairs={{0,8},{1,9},{2,10},{3,11},{4,12},{5,13},{6,14},{7,15},{8,0},{9,1},... | collective-permute-start | bytes 442376 | tf_op jit(solution)/shard_map/ppermute | solution.py:186
  138.9 11.3 %collective-permute-start.7 = (bf16[192,384]{1,0:T(8,128)(2,1)}, bf16[192,384]{1,0:T(8,128)(2,1)}, u32[]{:S(2)}, u32[]{:S(2)}) collective-permute-start(bf16[192,384]{1,0:T(8,128)(2,1)} %get-tuple-element.124), channel_id=1, source_target_pairs={{0,12},{1,13},{2,14},{3,15},{4,0},{5,1},{6,2},{7,3},{8,4},{9,5},{1... | collective-permute-start | bytes 442376 | tf_op jit(solution)/shard_map/ppermute | solution.py:186
  152.0 150.0 %all-gather.11.cloned.1.call-start = ((), (), s32[]{:S(2)}) async-start(), calls=%async_computation.1 | async-start | bytes 2506752 | tf_op jit(solution)/shard_map/all_gather | solution.py:223
  173.0 28.5 %collective-permute-start.16 = (bf16[4,192,384]{2,1,0:T(8,128)(2,1)S(1)}, bf16[4,192,384]{2,1,0:T(8,128)(2,1)S(1)}, u32[]{:S(2)}, u32[]{:S(2)}) collective-permute-start(bf16[4,192,384]{2,1,0:T(8,128)(2,1)S(1)} %get-tuple-element.90), channel_id=1, source_target_pairs={{0,1},{1,0},{2,3},{3,2},{4,5},{5,4},{6,7},{7,6},{8,9},{9,8},{10,11... | collective-permute-start | bytes 1769480 | tf_op jit(solution)/shard_map/ppermute | solution.py:183
  173.1 28.4 %collective-permute-start.17 = (bf16[4,192,384]{2,1,0:T(8,128)(2,1)S(1)}, bf16[4,192,384]{2,1,0:T(8,128)(2,1)S(1)}, u32[]{:S(2)}, u32[]{:S(2)}) collective-permute-start(bf16[4,192,384]{2,1,0:T(8,128)(2,1)S(1)} %get-tuple-element.91), channel_id=1, source_target_pairs={{0,1},{1,0},{2,3},{3,2},{4,5},{5,4},{6,7},{7,6},{8,9},{9,8},{10,11... | collective-permute-start | bytes 1769480 | tf_op jit(solution)/shard_map/ppermute | solution.py:183
  173.6 28.8 %collective-permute-start.15 = (bf16[4,192,384]{2,1,0:T(8,128)(2,1)S(1)}, bf16[4,192,384]{2,1,0:T(8,128)(2,1)S(1)}, u32[]{:S(2)}, u32[]{:S(2)}) collective-permute-start(bf16[4,192,384]{2,1,0:T(8,128)(2,1)S(1)} %add.203), channel_id=1, source_target_pairs={{0,2},{1,3},{2,0},{3,1},{4,6},{5,7},{6,4},{7,5},{8,10},{9,11},{10,... | collective-permute-start | bytes 1769480 | tf_op jit(solution)/shard_map/ppermute | solution.py:183
  175.0 9.5 %collective-permute-start.12 = (bf16[192,384]{1,0:T(8,128)(2,1)S(1)}, bf16[192,384]{1,0:T(8,128)(2,1)S(1)}, u32[]{:S(2)}, u32[]{:S(2)}) collective-permute-start(bf16[192,384]{1,0:T(8,128)(2,1)S(1)} %get-tuple-element.123), channel_id=1, source_target_pairs={{0,4},{1,5},{2,6},{3,7},{4,8},{5,9},{6,10},{7,11},{8,12},{9,13},{1... | collective-permute-start | bytes 442376 | tf_op jit(solution)/shard_map/ppermute | solution.py:186
  175.1 26.4 %collective-permute-start.13 = (bf16[192,384]{1,0:T(8,128)(2,1)S(1)}, bf16[192,384]{1,0:T(8,128)(2,1)S(1)}, u32[]{:S(2)}, u32[]{:S(2)}) collective-permute-start(bf16[192,384]{1,0:T(8,128)(2,1)S(1)} %get-tuple-element.122), channel_id=1, source_target_pairs={{0,8},{1,9},{2,10},{3,11},{4,12},{5,13},{6,14},{7,15},{8,0},{9,1},... | collective-permute-start | bytes 442376 | tf_op jit(solution)/shard_map/ppermute | solution.py:186
  184.5 17.0 %collective-permute-start.14 = (bf16[192,384]{1,0:T(8,128)(2,1)S(1)}, bf16[192,384]{1,0:T(8,128)(2,1)S(1)}, u32[]{:S(2)}, u32[]{:S(2)}) collective-permute-start(bf16[192,384]{1,0:T(8,128)(2,1)S(1)} %get-tuple-element.121), channel_id=1, source_target_pairs={{0,12},{1,13},{2,14},{3,15},{4,0},{5,1},{6,2},{7,3},{8,4},{9,5},{1... | collective-permute-start | bytes 442376 | tf_op jit(solution)/shard_map/ppermute | solution.py:186
  201.5 2.4 copy-start.9
  201.5 0.8 copy-start.11
  202.3 0.8 copy-start.12
  203.9 4.9 %copy-start.8 = (bf16[4,192,384]{2,1,0:T(8,128)(2,1)S(1)}, bf16[4,192,384]{2,1,0:T(8,128)(2,1)}, u32[]{:S(2)}) copy-start(bf16[4,192,384]{2,1,0:T(8,128)(2,1)} %add.202) | copy-start | bytes 1769476
  203.9 102.5 %all-gather.13.cloned.1.call-start = ((), (), s32[]{:S(2)}) async-start(), calls=%async_computation.2 | async-start | bytes 2506752 | tf_op jit(solution)/shard_map/all_gather | solution.py:223
  208.5 6.4 %copy-start.10 = (bf16[4,192,384]{2,1,0:T(8,128)(2,1)S(1)}, bf16[4,192,384]{2,1,0:T(8,128)(2,1)}, u32[]{:S(2)}) copy-start(bf16[4,192,384]{2,1,0:T(8,128)(2,1)} %copy-done.9) | copy-start | bytes 1769476
  211.3 19.3 %collective-permute-start.22 = (bf16[4,192,384]{2,1,0:T(8,128)(2,1)S(1)}, bf16[4,192,384]{2,1,0:T(8,128)(2,1)}, u32[]{:S(2)}, u32[]{:S(2)}) collective-permute-start(bf16[4,192,384]{2,1,0:T(8,128)(2,1)S(1)} %add.209), channel_id=1, source_target_pairs={{0,2},{1,3},{2,0},{3,1},{4,6},{5,7},{6,4},{7,5},{8,10},{9,11},{10,... | collective-permute-start | bytes 1769480 | tf_op jit(solution)/shard_map/ppermute | solution.py:183
  212.0 18.6 %collective-permute-start.19 = (bf16[192,384]{1,0:T(8,128)(2,1)S(1)}, bf16[192,384]{1,0:T(8,128)(2,1)S(1)}, u32[]{:S(2)}, u32[]{:S(2)}) collective-permute-start(bf16[192,384]{1,0:T(8,128)(2,1)S(1)} %get-tuple-element.120), channel_id=1, source_target_pairs={{0,4},{1,5},{2,6},{3,7},{4,8},{5,9},{6,10},{7,11},{8,12},{9,13},{1... | collective-permute-start | bytes 442376 | tf_op jit(solution)/shard_map/ppermute | solution.py:186
  212.5 18.1 %collective-permute-start.20 = (bf16[192,384]{1,0:T(8,128)(2,1)S(1)}, bf16[192,384]{1,0:T(8,128)(2,1)S(1)}, u32[]{:S(2)}, u32[]{:S(2)}) collective-permute-start(bf16[192,384]{1,0:T(8,128)(2,1)S(1)} %get-tuple-element.119), channel_id=1, source_target_pairs={{0,8},{1,9},{2,10},{3,11},{4,12},{5,13},{6,14},{7,15},{8,0},{9,1},... | collective-permute-start | bytes 442376 | tf_op jit(solution)/shard_map/ppermute | solution.py:186
  214.7 15.9 %collective-permute-start.21 = (bf16[192,384]{1,0:T(8,128)(2,1)S(1)}, bf16[192,384]{1,0:T(8,128)(2,1)S(1)}, u32[]{:S(2)}, u32[]{:S(2)}) collective-permute-start(bf16[192,384]{1,0:T(8,128)(2,1)S(1)} %get-tuple-element.118), channel_id=1, source_target_pairs={{0,12},{1,13},{2,14},{3,15},{4,0},{5,1},{6,2},{7,3},{8,4},{9,5},{1... | collective-permute-start | bytes 442376 | tf_op jit(solution)/shard_map/ppermute | solution.py:186
  231.3 115.7 %all-gather.15.cloned.1.call-start = ((), (), s32[]{:S(2)}) async-start(), calls=%async_computation.3 | async-start | bytes 2506752 | tf_op jit(solution)/shard_map/all_gather | solution.py:223
  231.4 1.2 collective-permute-start.11
  233.9 20.1 %collective-permute-start.24 = (bf16[192,384]{1,0:T(8,128)(2,1)S(1)}, bf16[192,384]{1,0:T(8,128)(2,1)S(1)}, u32[]{:S(2)}, u32[]{:S(2)}) collective-permute-start(bf16[192,384]{1,0:T(8,128)(2,1)S(1)} %get-tuple-element.117), channel_id=1, source_target_pairs={{0,4},{1,5},{2,6},{3,7},{4,8},{5,9},{6,10},{7,11},{8,12},{9,13},{1... | collective-permute-start | bytes 442376 | tf_op jit(solution)/shard_map/ppermute | solution.py:186
  237.7 21.5 %collective-permute-start.25 = (bf16[192,384]{1,0:T(8,128)(2,1)S(1)}, bf16[192,384]{1,0:T(8,128)(2,1)S(1)}, u32[]{:S(2)}, u32[]{:S(2)}) collective-permute-start(bf16[192,384]{1,0:T(8,128)(2,1)S(1)} %get-tuple-element.116), channel_id=1, source_target_pairs={{0,8},{1,9},{2,10},{3,11},{4,12},{5,13},{6,14},{7,15},{8,0},{9,1},... | collective-permute-start | bytes 442376 | tf_op jit(solution)/shard_map/ppermute | solution.py:186
  237.7 21.5 %collective-permute-start.26 = (bf16[192,384]{1,0:T(8,128)(2,1)S(1)}, bf16[192,384]{1,0:T(8,128)(2,1)S(1)}, u32[]{:S(2)}, u32[]{:S(2)}) collective-permute-start(bf16[192,384]{1,0:T(8,128)(2,1)S(1)} %get-tuple-element.115), channel_id=1, source_target_pairs={{0,12},{1,13},{2,14},{3,15},{4,0},{5,1},{6,2},{7,3},{8,4},{9,5},{1... | collective-permute-start | bytes 442376 | tf_op jit(solution)/shard_map/ppermute | solution.py:186
  260.0 3.6 collective-permute-start.18
  263.6 16.7 %collective-permute-start.23 = (f32[32]{0:T(128)S(1)}, f32[32]{0:T(128)S(1)}, u32[]{:S(2)}, u32[]{:S(2)}) collective-permute-start(f32[32]{0:T(128)S(1)} %add.215), channel_id=1, source_target_pairs={{0,4},{1,5},{2,6},{3,7},{4,0},{5,1},{6,2},{7,3},{8,12},{9,13},{10,... | collective-permute-start | bytes 392 | tf_op jit(solution)/shard_map/ppermute | solution.py:183
  279.2 1.2 copy-start
  280.4 18.2 %collective-permute-start.27 = (f32[32]{0:T(128)S(1)}, f32[32]{0:T(128)S(1)}, u32[]{:S(2)}, u32[]{:S(2)}) collective-permute-start(f32[32]{0:T(128)S(1)} %add.219), channel_id=1, source_target_pairs={{0,8},{1,9},{2,10},{3,11},{4,12},{5,13},{6,14},{7,15},{8,0},{9,1},... | collective-permute-start | bytes 392 | tf_op jit(solution)/shard_map/ppermute | solution.py:183
  297.4 1.2 copy-start.2
  301.2 0.7 copy-start.4
  302.0 1.0 copy-start.5
  303.0 3.4 copy-start.1
  305.7 0.7 copy-start.6
  306.4 1.0 copy-start.7
  307.4 39.6 %copy-start.3 = (bf16[8,250,384]{2,1,0:T(8,128)(2,1)S(1)}, bf16[8,250,384]{2,1,0:T(8,128)(2,1)}, u32[]{:S(2)}) copy-start(bf16[8,250,384]{2,1,0:T(8,128)(2,1)} %copy-done.2) | copy-start | bytes 4608004
  349.6 11.3 %collective-permute-start.28 = (f32[250,384]{1,0:T(8,128)S(1)}, f32[250,384]{1,0:T(8,128)S(1)}, u32[]{:S(2)}, u32[]{:S(2)}) collective-permute-start(f32[250,384]{1,0:T(8,128)S(1)} %shard_map.66), channel_id=1, source_target_pairs={{0,16},{16,0},{1,17},{17,1},{2,18},{18,2},{3,19},{19,3},{4,20},{20... | collective-permute-start | bytes 1152008 | tf_op jit(solution)/shard_map/ppermute | solution.py:270
Sparse Core Ops, SparseCore 0:
  9.6 44.9 all-gather.16
  56.9 43.9 all-gather.18
  152.1 50.2 all-gather.8
  204.5 54.8 all-gather.10
  261.5 42.1 all-gather.12
  305.9 41.0 all-gather.14

commit v3 on v2

--- a/solution.py
+++ b/solution.py
@@ -87,6 +87,20 @@
     acc = out_ref[...] - jnp.dot(h, y, preferred_element_type=F32)
     for b in range(batch):
         acc = acc + (2.0 * gamma_ref[step * batch + b]) * h_ref[b].astype(F32)
+    out_ref[...] = acc
+
+
+def shards_kernel(count, owners_ref, gamma_ref, base_ref, h_ref, *rest):
+    y_refs, out_ref = rest[:count], rest[count]
+    batch = 4 if count % 4 == 0 else 1
+    acc = base_ref[...]
+    for first in range(0, count, batch):
+        some = range(first, first + batch)
+        h = [h_ref[owners_ref[i]] for i in some]
+        y = jnp.concatenate([y_refs[i][...] for i in some], axis=0)
+        acc = acc - jnp.dot(jnp.concatenate(h, axis=1), y, preferred_element_type=F32)
+        for i, one in zip(some, h):
+            acc = acc + (2.0 * gamma_ref[owners_ref[i]]) * one.astype(F32)
     out_ref[...] = acc
 
 
@@ -164,6 +178,19 @@
     )(gamma, base, h_occ, ymo)
 
 
+def sigma_shards(owners, gamma, base, h_occ, shards):
+    paux, rows, width = h_occ.shape
+    return pl.pallas_call(
+        functools.partial(shards_kernel, len(shards)),
+        in_specs=[pl.BlockSpec(memory_space=pltpu.SMEM)] * 2
+        + [pl.BlockSpec(memory_space=pltpu.VMEM)] * (2 + len(shards)),
+        out_specs=pl.BlockSpec(memory_space=pltpu.VMEM),
+        out_shape=jax.ShapeDtypeStruct((rows, width), F32),
+        compiler_params=pltpu.CompilerParams(vmem_limit_bytes=VMEM_BYTES),
+        cost_estimate=cost(2 * rows * len(shards) * width * width, 2 * len(shards) * width * width),
+    )(owners, gamma, base, h_occ, *shards)
+
+
 def after(value, others):
     return lax.optimization_barrier((value, others))[0]
 
@@ -192,7 +219,7 @@
         wide = jnp.pad(local, ((0, 0), (0, width - nint)))
         return lax.all_gather(wide, "ao", axis=0, tiled=True)
 
-    paux = 8 if naux % 8 == 0 else naux
+    paux = 16 if naux % 16 == 0 else naux
     chunks = naux // paux
     cuts = groups // paux
 
@@ -207,33 +234,42 @@
     whole_c = gathered(coeff)
     bits = [1 << k for k in range(fan.bit_length() - 1)]
 
-    def reduce_steps(first):
+    def reduce_steps(first, by_permutes):
         live = dict(enumerate(first))
         for bit in bits:
             sent = {d: swap(v, bit) for d, v in live.items() if d & bit}
             sent = yield sent, list(live.values())
             live = {d: v + sent[d | bit] for d, v in live.items() if not d & bit}
         mine = live[0]
-        got = [turn_z(pick(mine, z + d), d) for d in range(1, nz)]
-        got = yield got, mine
+        sent = [pick(mine, z + d) for d in range(1, nz)]
+        got = yield [turn_z(v, d + 1) for d, v in enumerate(sent)], sent
         total = pick(mine, z).astype(F32)
         for part in got:
             total = total + part.astype(F32)
-        shard_sum = total.astype(BF16)
-        whole = lax.all_gather(shard_sum, "ao", axis=0, tiled=True)
-        yield whole.reshape(paux, width, width), shard_sum
+        total = total.astype(BF16)
+        if not by_permutes:
+            whole = lax.all_gather(total, "ao", axis=0, tiled=True)
+            yield whole.reshape(paux, width, width), total
+            return
+        shards = [[total] + [turn_z(total, d) for d in range(1, nz)]]
+        for bit in reversed(bits):
+            shards = shards + [[swap(v, bit) for v in column] for column in shards]
+        yield shards, total
 
     flows, waiting, occ, gammas = [], [], [], []
     start = jnp.zeros((8, LANES), F32)
 
+    left = [len(bits) + 1] * chunks
+
     def in_transit(c):
-        return not isinstance(waiting[c], jax.Array)
+        return left[c] > 0
 
     def advance(which, done=()):
         which = [c for c in which if in_transit(c)]
         arrived = after([waiting[c] for c in which], done)
         for c, got in zip(which, arrived):
             waiting[c], marks[c] = flows[c].send(got)
+            left[c] -= 1
 
     marks = {}
     for c in range(chunks):
@@ -241,7 +277,7 @@
             me, by_rows, whole_r, scale, ct, weighted, after(start, marks), c, paux, fan, nz, cuts
         )
         gammas.append(g)
-        flows.append(reduce_steps(first))
+        flows.append(reduce_steps(first, cuts == 1 and c == chunks - 1 > 0))
         got, marks[c] = next(flows[c])
         waiting.append(got)
         advance(range(c + 1), g)
@@ -254,9 +290,9 @@
         if got is not None:
             gamma = gamma + after(got, out)
             bit *= 2
-        if any(in_transit(e) for e in range(chunks)):
+        if any(left):
             advance(range(chunks), out)
-    while any(in_transit(e) for e in range(chunks)):
+    while any(left):
         advance(range(chunks))
     while bit < groups:
         gamma = gamma + swap(gamma, bit)
@@ -264,7 +300,20 @@
 
     sigma = jnp.zeros((rows, width), F32)
     for c in range(chunks):
-        sigma = sigma_part(gamma[c * paux : (c + 1) * paux], sigma, occ[c], waiting[c])
+        g = gamma[c * paux : (c + 1) * paux]
+        if isinstance(waiting[c], jax.Array):
+            sigma = sigma_part(g, sigma, occ[c], waiting[c])
+            continue
+        shards = waiting[c]
+        order = [0]
+        for bit in reversed(bits):
+            order = order + [d ^ bit for d in order]
+        for lo in range(0, fan, fan // ncore):
+            some = range(lo, lo + fan // ncore)
+            owners = [(z - k) % nz * fan + (index % fan ^ order[d]) for d in some for k in range(nz)]
+            sigma = sigma_shards(
+                jnp.stack(owners).astype(jnp.int32), g, sigma, occ[c], [v for d in some for v in shards[d]]
+            )
     bit = 1
     while bit < parts:
         sigma = sigma + lax.ppermute(sigma, "aux", [(i, i ^ bit) for i in range(parts)])

time: 374 us -> 314 us (0.84)
  Pallas kernels: 137 us -> 116 us
  starting transfers between devices: 44.9 us -> 25.5 us
  local copies, waits for them, and re-layouts: 23.8 us -> 14.6 us
  waiting for transfers between devices: 131 us -> 126 us
    ppermute x16 -> x22, waiting for transfers between devices: 20.4 us -> 64.7 us  [swap(): return lax.ppermute(value, 'ao', [(i, i ^ bit) for i in range(groups)])]
    all_gather x4 -> x1, waiting for transfers between devices: 36.9 us -> 0.01 us  [reduce_steps(): whole = lax.all_gather(total, 'ao', axis=0, tiled=True)]
    ppermute x12 -> x9, starting transfers between devices: 35 us -> 11.7 us  [turn_z(): lax.ppermute(value, 'ao', [(i, (i + by * fan) % groups) for i in range(gr...]
    ppermute x12 -> x9, waiting for transfers between devices: 21.6 us -> 6.04 us  [turn_z(): lax.ppermute(value, 'ao', [(i, (i + by * fan) % groups) for i in range(gr...]
    pallas_call x4 -> x2, Pallas kernels: 64.5 us -> 53.7 us  [rot_part(): pl.pallas_call(functools.partial(rot_kernel, paux, fan, nz, cuts), grid_s...]
    pallas_call x4 -> x2, Pallas kernels: 62.1 us -> 51.6 us  [occ_part(): pl.pallas_call(functools.partial(occ_kernel, paux), grid=(nscale,), in_sp...]
    unnamed x31 -> x19, local copies, waits for them, and re-layouts: 20.8 us -> 13.9 us
    pallas_call x0 -> x2, Pallas kernels: none -> 6.18 us  [sigma_shards(): pl.pallas_call(functools.partial(shards_kernel, len(shards)), in_specs=[p...]
  transfers between devices with their start and end apart: 35 -> 35, of which waited for: 16 -> 11; matrix products, arithmetic and copies ran while one was open for 9% -> 6% of each run, Pallas kernels for 37% -> 36%
where the time goes in v3:
time: 314 us; the launch traced here: 309 us
  waiting for transfers between devices  126 us (40%)
  Pallas kernels  116 us (37%)
  starting transfers between devices  25.5 us (8%)
  local copies, waits for them, and re-layouts  14.6 us (5%)
  other arithmetic  14.1 us (4%)
  between operations  13.4 us (4%)
    ppermute x22, waiting for transfers between devices, swap(): return lax.ppermute(value, 'ao', [(i, i ^ bit) for i in range(groups)])  64.7 us
    pallas_call x2, Pallas kernels, rot_part(): pl.pallas_call(functools.partial(rot_kernel, paux, fan, nz, cuts), grid_s...  53.7 us
    pallas_call x2, Pallas kernels, occ_part(): pl.pallas_call(functools.partial(occ_kernel, paux), grid=(nscale,), in_sp...  51.6 us
    all_gather x2, waiting for transfers between devices, gathered(): return lax.all_gather(wide, 'ao', axis=0, tiled=True)  44.2 us
    unnamed x19, local copies, waits for them, and re-layouts  13.9 us
    ppermute x22, starting transfers between devices, swap(): return lax.ppermute(value, 'ao', [(i, i ^ bit) for i in range(groups)])  13.1 us
    add x6, other arithmetic, reduce_steps(): live = {d: v + sent[d | bit] for d, v in live.items() if not d & bit}  11.9 us
    ppermute x9, starting transfers between devices, turn_z(): lax.ppermute(value, 'ao', [(i, (i + by * fan) % groups) for i in range(gr...  11.7 us
  transfers between devices with their start and end apart: 35, of which 11 were waited for; matrix products, arithmetic and copies ran while one was open for 6% of the time, Pallas kernels for 36%

profile of v3, /device:TPU:28, one launch (start us, length us, event | category | flops | bytes accessed | tf_op | source)
XLA Modules:
  0.0 309.2 jit_solution(18134057794511294753)
XLA Ops:
  6.5 1.7 pad_bitcast_fusion.1
  8.3 1.7 pad_bitcast_fusion
  10.5 44.2 %all-gather.8.cloned.1.call-done = bf16[16,250,384]{2,1,0:T(8,128)(2,1)} async-done(((bf16[1,250,384]{2,1,0:T(8,128)(2,1)}), bf16[16,250,384]{2,1,0:T(8,128)(2,1)}) %all-gather.8.cloned.1.call-update) | async-done | bytes 3072016 | tf_op jit(solution)/shard_map/all_gather | solution.py:220
  54.6 4.5 %reshape.19.m_ref = bf16[4000,384]{1,0:T(8,128)(2,1)} reshape(bf16[16,250,384]{2,1,0:T(8,128)(2,1)} %all-gather.8.cloned.1.call-done) | data formatting | bytes 6144000
  59.1 26.6 %shard_map.55 = (bf16[4,384,384]{2,1,0:T(8,128)(2,1)S(1)}, bf16[4,384,384]{2,1,0:T(8,128)(2,1)S(1)}, bf16[4,384,384]{2,1,0:T(8,128)(2,1)}, bf16[4,384,384]{2,1,0:T(8,128)(2,1)}, f32[16,1,384]{2,1,0:T(1,128)S(1)}) custom-call(s32[1]{0:T(128)} %bitcast.8.me_ref, bf16[250,32,4000]{2,1,0:T(8,128)(2,1)} %bitcast.45, bf16[4000,384]{1,0:T(8,128)(2,1)} %reshape.19.m_ref, ...), custom_call_target="tpu_custom_call" | custom-call | flops 12288000000 | bytes 32000000 | tf_op jit(solution)/shard_map/pallas_call | solution.py:128
  86.2 2.3 collective-permute-done
  88.6 2.0 collective-permute-done.1
  90.5 2.6 add.215
  93.1 0.6 collective-permute-start.3
  93.7 1.3 add.214
  95.0 27.0 %shard_map.56 = (bf16[4,384,384]{2,1,0:T(8,128)(2,1)S(1)}, bf16[4,384,384]{2,1,0:T(8,128)(2,1)}, bf16[4,384,384]{2,1,0:T(8,128)(2,1)}, bf16[4,384,384]{2,1,0:T(8,128)(2,1)}, f32[16,1,384]{2,1,0:T(1,128)S(1)}) custom-call(s32[1]{0:T(128)} %bitcast.8.me_ref, bf16[250,32,4000]{2,1,0:T(8,128)(2,1)} %bitcast.46, bf16[4000,384]{1,0:T(8,128)(2,1)} %reshape.19.m_ref, ...), custom_call_target="tpu_custom_call" | custom-call | flops 12288000000 | bytes 32000000 | tf_op jit(solution)/shard_map/pallas_call | solution.py:128
  122.1 1.1 copy-done.1
  123.7 3.0 reshape.21.m_ref
  127.0 1.0 collective-permute-done.5
  128.0 1.9 add.216
  129.9 1.6 add.227
  131.5 1.5 collective-permute-start.10
  133.1 1.7 collective-permute-start.7
  134.8 1.3 collective-permute-start.8
  136.1 1.3 collective-permute-start.9
  137.3 2.6 add.226
  139.9 25.7 %shard_map.57.h_ref = bf16[16,250,384]{2,1,0:T(8,128)(2,1)} custom-call(bf16[250,32,4000]{2,1,0:T(8,128)(2,1)} %bitcast.47, bf16[4000,384]{1,0:T(8,128)(2,1)S(1)} %reshape.21.m_ref, f32[10,32,1]{2,1,0:T(8,128)S(1)} %copy.13.scale_ref, f32[8,128]{1,0:T(8,128)S(1)} %broadcast_in_dim.11.tie_ref), custom_call_target="tpu_custom_call" | custom-call | flops 12288000000 | bytes 32000000 | tf_op jit(solution)/shard_map/pallas_call | solution.py:147
  165.6 0.9 fusion.5
  166.6 1.1 collective-permute-done.2
  168.3 1.9 add.233
  170.3 2.6 collective-permute-start.13
  173.0 0.6 collective-permute-start.15
  173.6 25.9 %shard_map.58.h_ref = bf16[16,250,384]{2,1,0:T(8,128)(2,1)} custom-call(bf16[250,32,4000]{2,1,0:T(8,128)(2,1)} %bitcast.48, bf16[4000,384]{1,0:T(8,128)(2,1)S(1)} %reshape.21.m_ref, f32[10,32,1]{2,1,0:T(8,128)S(1)} %copy.13.scale_ref, f32[8,128]{1,0:T(8,128)S(1)} %broadcast_in_dim.11.tie_ref), custom_call_target="tpu_custom_call" | custom-call | flops 12288000000 | bytes 32000000 | tf_op jit(solution)/shard_map/pallas_call | solution.py:147
  199.5 2.7 collective-permute-start.11
  202.2 6.0 %collective-permute-done.14 = bf16[384,384]{1,0:T(8,128)(2,1)S(1)} collective-permute-done((bf16[384,384]{1,0:T(8,128)(2,1)S(1)}, bf16[384,384]{1,0:T(8,128)(2,1)S(1)}, u32[]{:S(2)}, u32[]{:S(2)}) %collective-permute-start.14) | collective-permute-done | bytes 294944 | tf_op jit(solution)/shard_map/ppermute | solution.py:213
  208.5 2.2 collective-permute-start.17
  210.7 1.9 collective-permute-start.18
  212.6 0.8 collective-permute-start.12
  213.4 1.3 collective-permute-start.19
  214.7 40.3 %collective-permute-done.12 = f32[32]{0:T(128)S(1)} collective-permute-done((f32[32]{0:T(128)S(1)}, f32[32]{0:T(128)S(1)}, u32[]{:S(2)}, u32[]{:S(2)}) %collective-permute-start.12) | collective-permute-done | bytes 160 | tf_op jit(solution)/shard_map/ppermute | solution.py:210
  254.9 1.4 collective-permute-start.20
  256.4 0.6 collective-permute-start.21
  257.0 1.4 collective-permute-start.22
  259.1 5.6 %collective-permute-done.20.rest_5_ = bf16[384,384]{1,0:T(8,128)(2,1)S(1)} collective-permute-done((bf16[384,384]{1,0:T(8,128)(2,1)S(1)}, bf16[384,384]{1,0:T(8,128)(2,1)S(1)}, u32[]{:S(2)}, u32[]{:S(2)}) %collective-permute-start.20) | collective-permute-done | bytes 294944 | tf_op jit(solution)/shard_map/ppermute | solution.py:210
  264.7 6.3 %collective-permute-done.21.rest_6_ = bf16[384,384]{1,0:T(8,128)(2,1)S(1)} collective-permute-done((bf16[384,384]{1,0:T(8,128)(2,1)S(1)}, bf16[384,384]{1,0:T(8,128)(2,1)S(1)}, u32[]{:S(2)}, u32[]{:S(2)}) %collective-permute-start.21) | collective-permute-done | bytes 294944 | tf_op jit(solution)/shard_map/ppermute | solution.py:210
  271.1 5.9 %collective-permute-done.22.rest_7_ = bf16[384,384]{1,0:T(8,128)(2,1)S(1)} collective-permute-done((bf16[384,384]{1,0:T(8,128)(2,1)S(1)}, bf16[384,384]{1,0:T(8,128)(2,1)S(1)}, u32[]{:S(2)}, u32[]{:S(2)}) %collective-permute-start.22) | collective-permute-done | bytes 294944 | tf_op jit(solution)/shard_map/ppermute | solution.py:210
  277.7 1.9 copy-done
  279.6 4.6 %shard_map.59.base_ref = f32[250,384]{1,0:T(8,128)S(1)} custom-call(f32[16]{0:T(128)S(1)} %get-tuple-element.65.gamma_ref, f32[250,384]{1,0:T(8,128)S(1)} %broadcast_in_dim.12.base_ref, bf16[16,250,384]{2,1,0:T(8,128)(2,1)S(1)} %copy-done, bf16[16,384,384]{2,1,0:T(8,128)(2,1)} %bitcast.49), custom_call_target="tpu_custom_call" | custom-call | flops 1179648000 | bytes 4718592 | tf_op jit(solution)/shard_map/pallas_call | solution.py:165
  284.1 2.9 shard_map.60.base_ref
  287.1 3.2 %shard_map.61 = f32[250,384]{1,0:T(8,128)S(1)} custom-call(s32[8]{0:T(128)S(1)} %stack.62.owners_ref, f32[16]{0:T(128)S(1)} %get-tuple-element.66.gamma_ref, f32[250,384]{1,0:T(8,128)S(1)} %shard_map.60.base_ref, bf16[16,250,384]{2,1,0:T(8,128)(2,1)} %shard_map.58.h_ref, bf16[384,384]{1,0:T(8,128)(2,1)S(1)} %collective-permute-done.23.rest_0_, ...), custom_call_target="tpu_custom_call" | custom-call | flops 589824000 | bytes 2359296 | tf_op jit(solution)/shard_map/pallas_call | solution.py:183
  290.4 0.6 collective-permute-start.31
  291.0 10.9 %collective-permute-done.31 = f32[250,384]{1,0:T(8,128)S(1)} collective-permute-done((f32[250,384]{1,0:T(8,128)S(1)}, f32[250,384]{1,0:T(8,128)S(1)}, u32[]{:S(2)}, u32[]{:S(2)}) %collective-permute-start.31) | collective-permute-done | bytes 384032 | tf_op jit(solution)/shard_map/ppermute | solution.py:319
  301.9 0.8 fusion.6
  (76 shorter events, 4.4 us)
Async XLA Ops:
  6.5 3.5 %copy-start.3 = (bf16[250,380]{1,0:T(8,128)(2,1)S(1)}, bf16[250,380]{1,0:T(8,128)(2,1)}, u32[]{:S(2)}) copy-start(bf16[250,380]{1,0:T(8,128)(2,1)} %param.7) | copy-start | bytes 570004
  6.5 3.6 %copy-start.5 = (f32[32,10]{0,1:T(8,128)S(1)}, f32[32,10]{0,1:T(8,128)}, u32[]{:S(2)}) copy-start(f32[32,10]{0,1:T(8,128)} %param.6) | copy-start | bytes 3844
  6.5 3.8 %copy-start.6 = (f32[380]{0:T(512)S(1)}, f32[380]{0:T(512)}, u32[]{:S(2)}) copy-start(f32[380]{0:T(512)} %param.9) | copy-start | bytes 4564
  6.5 48.1 %all-gather.8.cloned.1.call-start = ((), (), s32[]{:S(2)}) async-start(), calls=%async_computation.1 | async-start | bytes 3342336 | tf_op jit(solution)/shard_map/all_gather | solution.py:220
  8.2 115.4 %all-gather.10.cloned.1.call-start = ((), (), s32[]{:S(2)}) async-start(), calls=%async_computation.2 | async-start | bytes 3342336 | tf_op jit(solution)/shard_map/all_gather | solution.py:220
  10.0 267.7 %all-gather.6.cloned.1.call-start = ((), (), s32[]{:S(2)}) async-start(), calls=%async_computation | async-start | bytes 5013504 | tf_op jit(solution)/shard_map/all_gather | solution.py:251
  85.7 2.8 collective-permute-start
  86.0 4.5 %collective-permute-start.1 = (bf16[4,384,384]{2,1,0:T(8,128)(2,1)}, bf16[4,384,384]{2,1,0:T(8,128)(2,1)S(1)}, u32[]{:S(2)}, u32[]{:S(2)}) collective-permute-start(bf16[4,384,384]{2,1,0:T(8,128)(2,1)} %get-tuple-element.35), channel_id=1, source_target_pairs={{0,1},{1,0},{2,3},{3,2},{4,5},{5,4},{6,7},{7,6},{8,9},{9,8},{10,11... | collective-permute-start | bytes 3538952 | tf_op jit(solution)/shard_map/ppermute | solution.py:210
  93.1 33.9 %collective-permute-start.3 = (bf16[4,384,384]{2,1,0:T(8,128)(2,1)}, bf16[4,384,384]{2,1,0:T(8,128)(2,1)}, u32[]{:S(2)}, u32[]{:S(2)}) collective-permute-start(bf16[4,384,384]{2,1,0:T(8,128)(2,1)} %add.215), channel_id=1, source_target_pairs={{0,2},{1,3},{2,0},{3,1},{4,6},{5,7},{6,4},{7,5},{8,10},{9,11},{10,... | collective-permute-start | bytes 3538952 | tf_op jit(solution)/shard_map/ppermute | solution.py:210
  122.1 1.1 copy-start.1
  123.1 3.8 %collective-permute-start.4 = (bf16[4,384,384]{2,1,0:T(8,128)(2,1)}, bf16[4,384,384]{2,1,0:T(8,128)(2,1)}, u32[]{:S(2)}, u32[]{:S(2)}) collective-permute-start(bf16[4,384,384]{2,1,0:T(8,128)(2,1)} %get-tuple-element.41), channel_id=1, source_target_pairs={{0,1},{1,0},{2,3},{3,2},{4,5},{5,4},{6,7},{7,6},{8,9},{9,8},{10,11... | collective-permute-start | bytes 3538952 | tf_op jit(solution)/shard_map/ppermute | solution.py:210
  123.1 4.9 %collective-permute-start.5 = (bf16[4,384,384]{2,1,0:T(8,128)(2,1)}, bf16[4,384,384]{2,1,0:T(8,128)(2,1)}, u32[]{:S(2)}, u32[]{:S(2)}) collective-permute-start(bf16[4,384,384]{2,1,0:T(8,128)(2,1)} %get-tuple-element.42), channel_id=1, source_target_pairs={{0,1},{1,0},{2,3},{3,2},{4,5},{5,4},{6,7},{7,6},{8,9},{9,8},{10,11... | collective-permute-start | bytes 3538952 | tf_op jit(solution)/shard_map/ppermute | solution.py:210
  127.0 3.0 copy-start.4
  131.5 5.8 %copy-start.2 = (bf16[4,384,384]{2,1,0:T(8,128)(2,1)S(1)}, bf16[4,384,384]{2,1,0:T(8,128)(2,1)}, u32[]{:S(2)}) copy-start(bf16[4,384,384]{2,1,0:T(8,128)(2,1)} %copy-done.1) | copy-start | bytes 3538948
  131.5 34.1 %collective-permute-start.10 = (bf16[4,384,384]{2,1,0:T(8,128)(2,1)S(1)}, bf16[4,384,384]{2,1,0:T(8,128)(2,1)}, u32[]{:S(2)}, u32[]{:S(2)}) collective-permute-start(bf16[4,384,384]{2,1,0:T(8,128)(2,1)S(1)} %add.227), channel_id=1, source_target_pairs={{0,2},{1,3},{2,0},{3,1},{4,6},{5,7},{6,4},{7,5},{8,10},{9,11},{10,... | collective-permute-start | bytes 3538952 | tf_op jit(solution)/shard_map/ppermute | solution.py:210
  133.1 32.5 %collective-permute-start.7 = (bf16[384,384]{1,0:T(8,128)(2,1)S(1)}, bf16[384,384]{1,0:T(8,128)(2,1)S(1)}, u32[]{:S(2)}, u32[]{:S(2)}) collective-permute-start(bf16[384,384]{1,0:T(8,128)(2,1)S(1)} %get-tuple-element.64), channel_id=1, source_target_pairs={{0,4},{1,5},{2,6},{3,7},{4,8},{5,9},{6,10},{7,11},{8,12},{9,13},{1... | collective-permute-start | bytes 884744 | tf_op jit(solution)/shard_map/ppermute | solution.py:213
  134.8 30.8 %collective-permute-start.8 = (bf16[384,384]{1,0:T(8,128)(2,1)S(1)}, bf16[384,384]{1,0:T(8,128)(2,1)S(1)}, u32[]{:S(2)}, u32[]{:S(2)}) collective-permute-start(bf16[384,384]{1,0:T(8,128)(2,1)S(1)} %get-tuple-element.63), channel_id=1, source_target_pairs={{0,8},{1,9},{2,10},{3,11},{4,12},{5,13},{6,14},{7,15},{8,0},{9,1},... | collective-permute-start | bytes 884744 | tf_op jit(solution)/shard_map/ppermute | solution.py:213
  136.1 29.6 %collective-permute-start.9 = (bf16[384,384]{1,0:T(8,128)(2,1)S(1)}, bf16[384,384]{1,0:T(8,128)(2,1)S(1)}, u32[]{:S(2)}, u32[]{:S(2)}) collective-permute-start(bf16[384,384]{1,0:T(8,128)(2,1)S(1)} %get-tuple-element.62), channel_id=1, source_target_pairs={{0,12},{1,13},{2,14},{3,15},{4,0},{5,1},{6,2},{7,3},{8,4},{9,5},{1... | collective-permute-start | bytes 884744 | tf_op jit(solution)/shard_map/ppermute | solution.py:213
  166.5 1.2 collective-permute-start.2
  167.7 31.8 %collective-permute-start.6 = (f32[32]{0:T(128)S(1)}, f32[32]{0:T(128)S(1)}, u32[]{:S(2)}, u32[]{:S(2)}) collective-permute-start(f32[32]{0:T(128)S(1)} %add.228), channel_id=1, source_target_pairs={{0,2},{1,3},{2,0},{3,1},{4,6},{5,7},{6,4},{7,5},{8,10},{9,11},{10,... | collective-permute-start | bytes 392 | tf_op jit(solution)/shard_map/ppermute | solution.py:210
  170.3 31.9 %collective-permute-start.13 = (bf16[384,384]{1,0:T(8,128)(2,1)S(1)}, bf16[384,384]{1,0:T(8,128)(2,1)S(1)}, u32[]{:S(2)}, u32[]{:S(2)}) collective-permute-start(bf16[384,384]{1,0:T(8,128)(2,1)S(1)} %get-tuple-element.61), channel_id=1, source_target_pairs={{0,4},{1,5},{2,6},{3,7},{4,8},{5,9},{6,10},{7,11},{8,12},{9,13},{1... | collective-permute-start | bytes 884744 | tf_op jit(solution)/shard_map/ppermute | solution.py:213
  173.0 35.3 %collective-permute-start.14 = (bf16[384,384]{1,0:T(8,128)(2,1)S(1)}, bf16[384,384]{1,0:T(8,128)(2,1)S(1)}, u32[]{:S(2)}, u32[]{:S(2)}) collective-permute-start(bf16[384,384]{1,0:T(8,128)(2,1)S(1)} %get-tuple-element.60), channel_id=1, source_target_pairs={{0,8},{1,9},{2,10},{3,11},{4,12},{5,13},{6,14},{7,15},{8,0},{9,1},... | collective-permute-start | bytes 884744 | tf_op jit(solution)/shard_map/ppermute | solution.py:213
  173.0 35.3 %collective-permute-start.15 = (bf16[384,384]{1,0:T(8,128)(2,1)S(1)}, bf16[384,384]{1,0:T(8,128)(2,1)S(1)}, u32[]{:S(2)}, u32[]{:S(2)}) collective-permute-start(bf16[384,384]{1,0:T(8,128)(2,1)S(1)} %get-tuple-element.59), channel_id=1, source_target_pairs={{0,12},{1,13},{2,14},{3,15},{4,0},{5,1},{6,2},{7,3},{8,4},{9,5},{1... | collective-permute-start | bytes 884744 | tf_op jit(solution)/shard_map/ppermute | solution.py:213
  199.5 11.2 %collective-permute-start.11 = (f32[32]{0:T(128)S(1)}, f32[32]{0:T(128)S(1)}, u32[]{:S(2)}, u32[]{:S(2)}) collective-permute-start(f32[32]{0:T(128)S(1)} %add.234), channel_id=1, source_target_pairs={{0,4},{1,5},{2,6},{3,7},{4,0},{5,1},{6,2},{7,3},{8,12},{9,13},{10,... | collective-permute-start | bytes 392 | tf_op jit(solution)/shard_map/ppermute | solution.py:210
  208.4 46.5 %collective-permute-start.16 = (bf16[384,384]{1,0:T(8,128)(2,1)S(1)}, bf16[384,384]{1,0:T(8,128)(2,1)S(1)}, u32[]{:S(2)}, u32[]{:S(2)}) collective-permute-start(bf16[384,384]{1,0:T(8,128)(2,1)S(1)} %fusion.2.rest_0_), channel_id=1, source_target_pairs={{0,4},{1,5},{2,6},{3,7},{4,8},{5,9},{6,10},{7,11},{8,12},{9,13},{1... | collective-permute-start | bytes 884744 | tf_op jit(solution)/shard_map/ppermute | solution.py:213
  208.5 47.9 %collective-permute-start.17 = (bf16[384,384]{1,0:T(8,128)(2,1)S(1)}, bf16[384,384]{1,0:T(8,128)(2,1)S(1)}, u32[]{:S(2)}, u32[]{:S(2)}) collective-permute-start(bf16[384,384]{1,0:T(8,128)(2,1)S(1)} %fusion.2.rest_0_), channel_id=1, source_target_pairs={{0,8},{1,9},{2,10},{3,11},{4,12},{5,13},{6,14},{7,15},{8,0},{9,1},... | collective-permute-start | bytes 884744 | tf_op jit(solution)/shard_map/ppermute | solution.py:213
  210.7 46.3 %collective-permute-start.18 = (bf16[384,384]{1,0:T(8,128)(2,1)S(1)}, bf16[384,384]{1,0:T(8,128)(2,1)S(1)}, u32[]{:S(2)}, u32[]{:S(2)}) collective-permute-start(bf16[384,384]{1,0:T(8,128)(2,1)S(1)} %fusion.2.rest_0_), channel_id=1, source_target_pairs={{0,12},{1,13},{2,14},{3,15},{4,0},{5,1},{6,2},{7,3},{8,4},{9,5},{1... | collective-permute-start | bytes 884744 | tf_op jit(solution)/shard_map/ppermute | solution.py:213
  212.6 42.3 %collective-permute-start.12 = (f32[32]{0:T(128)S(1)}, f32[32]{0:T(128)S(1)}, u32[]{:S(2)}, u32[]{:S(2)}) collective-permute-start(f32[32]{0:T(128)S(1)} %add.235), channel_id=1, source_target_pairs={{0,8},{1,9},{2,10},{3,11},{4,12},{5,13},{6,14},{7,15},{8,0},{9,1},... | collective-permute-start | bytes 392 | tf_op jit(solution)/shard_map/ppermute | solution.py:210
  213.4 45.0 %collective-permute-start.19 = (bf16[384,384]{1,0:T(8,128)(2,1)S(1)}, bf16[384,384]{1,0:T(8,128)(2,1)S(1)}, u32[]{:S(2)}, u32[]{:S(2)}) collective-permute-start(bf16[384,384]{1,0:T(8,128)(2,1)S(1)} %fusion.2.rest_0_), channel_id=1, source_target_pairs={{0,2},{1,3},{2,0},{3,1},{4,6},{5,7},{6,4},{7,5},{8,10},{9,11},{10,... | collective-permute-start | bytes 884744 | tf_op jit(solution)/shard_map/ppermute | solution.py:210
  254.9 3.5 %collective-permute-start.23 = (bf16[384,384]{1,0:T(8,128)(2,1)S(1)}, bf16[384,384]{1,0:T(8,128)(2,1)S(1)}, u32[]{:S(2)}, u32[]{:S(2)}) collective-permute-start(bf16[384,384]{1,0:T(8,128)(2,1)S(1)} %fusion.2.rest_0_), channel_id=1, source_target_pairs={{0,1},{1,0},{2,3},{3,2},{4,5},{5,4},{6,7},{7,6},{8,9},{9,8},{10,11... | collective-permute-start | bytes 884744 | tf_op jit(solution)/shard_map/ppermute | solution.py:210
  254.9 9.8 %collective-permute-start.20 = (bf16[384,384]{1,0:T(8,128)(2,1)S(1)}, bf16[384,384]{1,0:T(8,128)(2,1)S(1)}, u32[]{:S(2)}, u32[]{:S(2)}) collective-permute-start(bf16[384,384]{1,0:T(8,128)(2,1)S(1)} %collective-permute-done.16.rest_1_), channel_id=1, source_target_pairs={{0,2},{1,3},{2,0},{3,1},{4,6},{5,7},{6,4},{7,5},{8,10},{9,11},{10,... | collective-permute-start | bytes 884744 | tf_op jit(solution)/shard_map/ppermute | solution.py:210
  256.4 14.7 %collective-permute-start.21 = (bf16[384,384]{1,0:T(8,128)(2,1)S(1)}, bf16[384,384]{1,0:T(8,128)(2,1)S(1)}, u32[]{:S(2)}, u32[]{:S(2)}) collective-permute-start(bf16[384,384]{1,0:T(8,128)(2,1)S(1)} %collective-permute-done.17.rest_2_), channel_id=1, source_target_pairs={{0,2},{1,3},{2,0},{3,1},{4,6},{5,7},{6,4},{7,5},{8,10},{9,11},{10,... | collective-permute-start | bytes 884744 | tf_op jit(solution)/shard_map/ppermute | solution.py:210
  257.0 20.0 %collective-permute-start.22 = (bf16[384,384]{1,0:T(8,128)(2,1)S(1)}, bf16[384,384]{1,0:T(8,128)(2,1)S(1)}, u32[]{:S(2)}, u32[]{:S(2)}) collective-permute-start(bf16[384,384]{1,0:T(8,128)(2,1)S(1)} %collective-permute-done.18.rest_3_), channel_id=1, source_target_pairs={{0,2},{1,3},{2,0},{3,1},{4,6},{5,7},{6,4},{7,5},{8,10},{9,11},{10,... | collective-permute-start | bytes 884744 | tf_op jit(solution)/shard_map/ppermute | solution.py:210
  258.4 18.6 %collective-permute-start.24 = (bf16[384,384]{1,0:T(8,128)(2,1)S(1)}, bf16[384,384]{1,0:T(8,128)(2,1)S(1)}, u32[]{:S(2)}, u32[]{:S(2)}) collective-permute-start(bf16[384,384]{1,0:T(8,128)(2,1)S(1)} %collective-permute-done.16.rest_1_), channel_id=1, source_target_pairs={{0,1},{1,0},{2,3},{3,2},{4,5},{5,4},{6,7},{7,6},{8,9},{9,8},{10,11... | collective-permute-start | bytes 884744 | tf_op jit(solution)/shard_map/ppermute | solution.py:210
  258.4 19.1 %collective-permute-start.25 = (bf16[384,384]{1,0:T(8,128)(2,1)S(1)}, bf16[384,384]{1,0:T(8,128)(2,1)S(1)}, u32[]{:S(2)}, u32[]{:S(2)}) collective-permute-start(bf16[384,384]{1,0:T(8,128)(2,1)S(1)} %collective-permute-done.17.rest_2_), channel_id=1, source_target_pairs={{0,1},{1,0},{2,3},{3,2},{4,5},{5,4},{6,7},{7,6},{8,9},{9,8},{10,11... | collective-permute-start | bytes 884744 | tf_op jit(solution)/shard_map/ppermute | solution.py:210
  264.7 22.4 %collective-permute-start.26 = (bf16[384,384]{1,0:T(8,128)(2,1)S(1)}, bf16[384,384]{1,0:T(8,128)(2,1)S(1)}, u32[]{:S(2)}, u32[]{:S(2)}) collective-permute-start(bf16[384,384]{1,0:T(8,128)(2,1)S(1)} %collective-permute-done.18.rest_3_), channel_id=1, source_target_pairs={{0,1},{1,0},{2,3},{3,2},{4,5},{5,4},{6,7},{7,6},{8,9},{9,8},{10,11... | collective-permute-start | bytes 884744 | tf_op jit(solution)/shard_map/ppermute | solution.py:210
  271.1 16.0 %collective-permute-start.27 = (bf16[384,384]{1,0:T(8,128)(2,1)S(1)}, bf16[384,384]{1,0:T(8,128)(2,1)}, u32[]{:S(2)}, u32[]{:S(2)}) collective-permute-start(bf16[384,384]{1,0:T(8,128)(2,1)S(1)} %collective-permute-done.19.rest_4_), channel_id=1, source_target_pairs={{0,1},{1,0},{2,3},{3,2},{4,5},{5,4},{6,7},{7,6},{8,9},{9,8},{10,11... | collective-permute-start | bytes 884744 | tf_op jit(solution)/shard_map/ppermute | solution.py:210
  277.0 10.1 %collective-permute-start.28 = (bf16[384,384]{1,0:T(8,128)(2,1)S(1)}, bf16[384,384]{1,0:T(8,128)(2,1)}, u32[]{:S(2)}, u32[]{:S(2)}) collective-permute-start(bf16[384,384]{1,0:T(8,128)(2,1)S(1)} %collective-permute-done.20.rest_5_), channel_id=1, source_target_pairs={{0,1},{1,0},{2,3},{3,2},{4,5},{5,4},{6,7},{7,6},{8,9},{9,8},{10,11... | collective-permute-start | bytes 884744 | tf_op jit(solution)/shard_map/ppermute | solution.py:210
  277.0 10.1 %collective-permute-start.29 = (bf16[384,384]{1,0:T(8,128)(2,1)S(1)}, bf16[384,384]{1,0:T(8,128)(2,1)}, u32[]{:S(2)}, u32[]{:S(2)}) collective-permute-start(bf16[384,384]{1,0:T(8,128)(2,1)S(1)} %collective-permute-done.21.rest_6_), channel_id=1, source_target_pairs={{0,1},{1,0},{2,3},{3,2},{4,5},{5,4},{6,7},{7,6},{8,9},{9,8},{10,11... | collective-permute-start | bytes 884744 | tf_op jit(solution)/shard_map/ppermute | solution.py:210
  277.5 9.6 %collective-permute-start.30 = (bf16[384,384]{1,0:T(8,128)(2,1)S(1)}, bf16[384,384]{1,0:T(8,128)(2,1)}, u32[]{:S(2)}, u32[]{:S(2)}) collective-permute-start(bf16[384,384]{1,0:T(8,128)(2,1)S(1)} %collective-permute-done.22.rest_7_), channel_id=1, source_target_pairs={{0,1},{1,0},{2,3},{3,2},{4,5},{5,4},{6,7},{7,6},{8,9},{9,8},{10,11... | collective-permute-start | bytes 884744 | tf_op jit(solution)/shard_map/ppermute | solution.py:210
  277.7 1.9 copy-start
  290.4 11.5 %collective-permute-start.31 = (f32[250,384]{1,0:T(8,128)S(1)}, f32[250,384]{1,0:T(8,128)S(1)}, u32[]{:S(2)}, u32[]{:S(2)}) collective-permute-start(f32[250,384]{1,0:T(8,128)S(1)} %shard_map.61), channel_id=1, source_target_pairs={{0,16},{16,0},{1,17},{17,1},{2,18},{18,2},{3,19},{19,3},{4,20},{20... | collective-permute-start | bytes 1152008 | tf_op jit(solution)/shard_map/ppermute | solution.py:319
Sparse Core Ops, SparseCore 0:
  9.6 44.9 all-gather.7
  56.9 44.2 all-gather.9
  166.7 88.0 all-gather.5

commit v4 on v3

--- a/solution.py
+++ b/solution.py
@@ -24,6 +24,14 @@
     while 4 * x * x <= chips and chips % (2 * x) == 0:
         x *= 2
     return chips // x, x, core
+
+
+def joined(parts_ref, m_ref):
+    count, rows, cols = parts_ref.shape
+    if cols < m_ref.shape[1]:
+        m_ref[:, cols - cols % LANES :] = jnp.zeros((m_ref.shape[0], LANES), BF16)
+    for k in range(count):
+        m_ref[k * rows : (k + 1) * rows, :cols] = parts_ref[k]
 
 
 def rows_times(b_ref, m_ref, scale_ref, h_ref):
@@ -45,7 +53,10 @@
 
 
 def rot_kernel(paux, fan, nz, cuts, me_ref, b_ref, m_ref, scale_ref, ct_ref, w_ref, tie_ref, *rest):
-    outs, gamma_ref, h_ref = rest[:fan], rest[fan], rest[fan + 1]
+    outs, gamma_ref, h_ref = rest[:fan], rest[fan], rest[-1]
+    if len(m_ref.shape) == 3:
+        parts_ref, m_ref = m_ref, rest[fan + 1]
+        pl.when(pl.program_id(0) == 0)(lambda: joined(parts_ref, m_ref))
     rows_times(b_ref, m_ref, scale_ref, h_ref)
 
     @pl.when(pl.program_id(0) == pl.num_programs(0) - 1)
@@ -66,7 +77,11 @@
                     outs[d + e][k] = y[e * shard : (e + 1) * shard, k * width : (k + 1) * width]
 
 
-def occ_kernel(paux, b_ref, m_ref, scale_ref, tie_ref, out_ref, h_ref):
+def occ_kernel(paux, b_ref, m_ref, scale_ref, tie_ref, out_ref, *rest):
+    h_ref = rest[-1]
+    if len(m_ref.shape) == 3:
+        parts_ref, m_ref = m_ref, rest[0]
+        pl.when(pl.program_id(0) == 0)(lambda: joined(parts_ref, m_ref))
     rows_times(b_ref, m_ref, scale_ref, h_ref)
 
     @pl.when(pl.program_id(0) == pl.num_programs(0) - 1)
@@ -108,18 +123,19 @@
     return pl.CostEstimate(flops=flops, bytes_accessed=nbytes, transcendentals=0)
 
 
-def block_specs(rows, nscale, paux, naos, width, chunk):
+def block_specs(rows, nscale, paux, naos, shape, chunk):
     mub = rows // nscale
     return [
         pl.BlockSpec((mub, paux, naos), lambda s, *_: (s, chunk, 0)),
-        pl.BlockSpec((naos, width), lambda s, *_: (0, 0), pipeline_mode=pl.Buffered(1)),
+        pl.BlockSpec(shape, lambda s, *_: (0,) * len(shape), pipeline_mode=pl.Buffered(1)),
         pl.BlockSpec((1, paux, 1), lambda s, *_: (s, chunk, 0)),
     ]
 
 
 def rot_part(me, blocks, matrix, scale, ct, weighted, tie, chunk, paux, fan, nz, cuts):
     rows, _, naos = blocks.shape
-    nscale, width = scale.shape[0], matrix.shape[1]
+    nscale, width = scale.shape[0], up_to(matrix.shape[-1], LANES)
+    extra = [(naos, width)] if matrix.ndim == 3 else []
     piece = jax.ShapeDtypeStruct((nz, width // cuts, width), BF16)
 
     def whole(shape):
@@ -130,12 +146,16 @@
         grid_spec=pltpu.PrefetchScalarGridSpec(
             num_scalar_prefetch=1,
             grid=(nscale,),
-            in_specs=block_specs(rows, nscale, paux, naos, width, chunk)
+            in_specs=block_specs(rows, nscale, paux, naos, matrix.shape, chunk)
             + [whole(ct.shape), whole(weighted.shape), pl.BlockSpec(memory_space=pl.ANY)],
-            out_specs=[whole(piece.shape)] * fan + [whole((paux, 1, width))],
+            out_specs=[whole(piece.shape)] * fan
+            + [whole((paux, 1, width))]
+            + [pl.BlockSpec(e, lambda s, *_: (0, 0)) for e in extra],
             scratch_shapes=[pltpu.VMEM((width // LANES, rows * paux, LANES), F32)],
         ),
-        out_shape=[piece] * fan + [jax.ShapeDtypeStruct((paux, 1, width), F32)],
+        out_shape=[piece] * fan
+        + [jax.ShapeDtypeStruct((paux, 1, width), F32)]
+        + [jax.ShapeDtypeStruct(e, BF16) for e in extra],
         compiler_params=pltpu.CompilerParams(vmem_limit_bytes=VMEM_BYTES),
         cost_estimate=cost(2 * rows * paux * naos * width, 2 * rows * paux * naos),
     )(me, blocks, matrix, scale, ct, weighted, tie)
@@ -143,14 +163,17 @@
 
 def occ_part(blocks, matrix, scale, tie, chunk, paux):
     rows, _, naos = blocks.shape
-    nscale, width = scale.shape[0], matrix.shape[1]
+    nscale, width = scale.shape[0], up_to(matrix.shape[-1], LANES)
+    extra = [(naos, width)] if matrix.ndim == 3 else []
+    out = jax.ShapeDtypeStruct((paux, rows, width), BF16)
     return pl.pallas_call(
         functools.partial(occ_kernel, paux),
         grid=(nscale,),
-        in_specs=block_specs(rows, nscale, paux, naos, width, chunk)
+        in_specs=block_specs(rows, nscale, paux, naos, matrix.shape, chunk)
         + [pl.BlockSpec(memory_space=pl.ANY)],
-        out_specs=pl.BlockSpec((paux, rows, width), lambda s: (0, 0, 0)),
-        out_shape=jax.ShapeDtypeStruct((paux, rows, width), BF16),
+        out_specs=[pl.BlockSpec(out.shape, lambda s: (0, 0, 0))]
+        + [pl.BlockSpec(e, lambda s: (0, 0)) for e in extra],
+        out_shape=[out] + [jax.ShapeDtypeStruct(e, BF16) for e in extra],
         scratch_shapes=[pltpu.VMEM((width // LANES, rows * paux, LANES), F32)],
         compiler_params=pltpu.CompilerParams(vmem_limit_bytes=VMEM_BYTES),
         cost_estimate=cost(2 * rows * paux * naos * width, 2 * rows * paux * naos),
@@ -215,10 +238,6 @@
     def pick(value, k):
         return lax.dynamic_index_in_dim(value, k % nz, 0, keepdims=False)
 
-    def gathered(local):
-        wide = jnp.pad(local, ((0, 0), (0, width - nint)))
-        return lax.all_gather(wide, "ao", axis=0, tiled=True)
-
     paux = 16 if naux % 16 == 0 else naux
     chunks = naux // paux
     cuts = groups // paux
@@ -230,8 +249,8 @@
         [lax.dynamic_index_in_dim(ct, index % cuts ^ e, 0, keepdims=False) for e in range(cuts)]
     )
     weighted = jnp.pad(coeff.astype(F32) * occupation[None, :], ((0, 0), (0, width - nint)))
-    whole_r = gathered(rot_coeff)
-    whole_c = gathered(coeff)
+    whole_r = lax.all_gather(rot_coeff, "ao", axis=0)
+    whole_c = lax.all_gather(coeff, "ao", axis=0)
     bits = [1 << k for k in range(fan.bit_length() - 1)]
 
     def reduce_steps(first, by_permutes):
@@ -273,30 +292,37 @@
 
     marks = {}
     for c in range(chunks):
-        *first, g = rot_part(
+        out = rot_part(
             me, by_rows, whole_r, scale, ct, weighted, after(start, marks), c, paux, fan, nz, cuts
         )
+        first, g = out[:fan], out[fan]
+        if c == 0:
+            whole_r = out[fan + 1]
         gammas.append(g)
         flows.append(reduce_steps(first, cuts == 1 and c == chunks - 1 > 0))
         got, marks[c] = next(flows[c])
         waiting.append(got)
         advance(range(c + 1), g)
     gamma = jnp.sum(jnp.concatenate(gammas, axis=0), axis=(1, 2))
-    bit = 1
+    hops = [
+        [functools.partial(swap, bit=d) for d in range(1, fan)],
+        [functools.partial(turn_z, by=d) for d in range(1, nz)],
+    ]
     for c in range(chunks):
-        got = swap(gamma, bit) if bit < groups else None
-        out = occ_part(by_rows, whole_c, scale, after(start, (marks, gamma)), c, paux)
+        hop = hops.pop(0) if hops else []
+        got = [move(gamma) for move in hop]
+        out, *extra = occ_part(by_rows, whole_c, scale, after(start, (marks, gamma)), c, paux)
+        if extra:
+            whole_c = extra[0]
         occ.append(out)
-        if got is not None:
-            gamma = gamma + after(got, out)
-            bit *= 2
+        for part in after(got, out):
+            gamma = gamma + part
         if any(left):
-            advance(range(chunks), out)
+            advance(range(chunks), (out, gamma))
+    for hop in hops:
+        gamma = functools.reduce(jnp.add, [move(gamma) for move in hop], gamma)
     while any(left):
         advance(range(chunks))
-    while bit < groups:
-        gamma = gamma + swap(gamma, bit)
-        bit *= 2
 
     sigma = jnp.zeros((rows, width), F32)
     for c in range(chunks):

time: 314 us -> 301 us (0.959); the launches traced: 309 us -> 300 us
  waiting for transfers between devices: 126 us -> 113 us
  local copies, waits for them, and re-layouts: 14.6 us -> 6.26 us
  starting transfers between devices: 25.5 us -> 32.9 us
    ppermute x22 -> x21, waiting for transfers between devices: 64.7 us -> 15.7 us  [swap(): return lax.ppermute(value, 'ao', [(i, i ^ bit) for i in range(groups)])]
    ppermute x9 -> x12, waiting for transfers between devices: 6.04 us -> 40.9 us  [turn_z(): lax.ppermute(value, 'ao', [(i, (i + by * fan) % groups) for i in range(gr...]
    unnamed x19 -> x23, local copies, waits for them, and re-layouts: 13.9 us -> 4.9 us
    ppermute x9 -> x12, starting transfers between devices: 11.7 us -> 20.6 us  [turn_z(): lax.ppermute(value, 'ao', [(i, (i + by * fan) % groups) for i in range(gr...]
    ppermute x22 -> x21, starting transfers between devices: 13.1 us -> 11.7 us  [swap(): return lax.ppermute(value, 'ao', [(i, i ^ bit) for i in range(groups)])]
  transfers between devices with their start and end apart: 35 -> 37, of which waited for: 11 -> 11; matrix products, arithmetic and copies ran while one was open for 6% -> 5% of each run, Pallas kernels for 36% -> 39%
where the time goes in v4:
time: 301 us; the launch traced here: 300 us
  Pallas kernels  119 us (40%)
  waiting for transfers between devices  113 us (38%)
  starting transfers between devices  32.9 us (11%)
  other arithmetic  14.8 us (5%)
  between operations  13.4 us (4%)
  local copies, waits for them, and re-layouts  6.26 us (2%)
    pallas_call x2, Pallas kernels, rot_part(): pl.pallas_call(functools.partial(rot_kernel, paux, fan, nz, cuts), grid_s...  54.9 us
    pallas_call x2, Pallas kernels, occ_part(): pl.pallas_call(functools.partial(occ_kernel, paux), grid=(nscale,), in_sp...  53 us
    all_gather x1, waiting for transfers between devices, body(): whole_r = lax.all_gather(rot_coeff, 'ao', axis=0)  43.6 us
    ppermute x12, waiting for transfers between devices, turn_z(): lax.ppermute(value, 'ao', [(i, (i + by * fan) % groups) for i in range(gr...  40.9 us
    ppermute x12, starting transfers between devices, turn_z(): lax.ppermute(value, 'ao', [(i, (i + by * fan) % groups) for i in range(gr...  20.6 us
    ppermute x21, waiting for transfers between devices, swap(): return lax.ppermute(value, 'ao', [(i, i ^ bit) for i in range(groups)])  15.7 us
    ppermute x21, starting transfers between devices, swap(): return lax.ppermute(value, 'ao', [(i, i ^ bit) for i in range(groups)])  11.7 us
    ppermute x1, waiting for transfers between devices, body(): lax.ppermute(sigma, 'aux', [(i, i ^ bit) for i in range(parts)])  11 us
  transfers between devices with their start and end apart: 37, of which 11 were waited for; matrix products, arithmetic and copies ran while one was open for 5% of the time, Pallas kernels for 39%

profile of v4, /device:TPU:28, one launch (start us, length us, event | category | flops | bytes accessed | tf_op | source)
XLA Modules:
  0.0 299.5 jit_solution(16219365947448832775)
XLA Ops:
  6.5 0.7 all-gather.10.cloned.1.call-update
  7.3 0.7 all-gather.12.cloned.1.call-update
  8.1 1.1 copy.12
  9.1 0.8 copy.13.scale_ref
  10.0 1.0 convert_multiply_fusion
  11.0 43.6 %all-gather.10.cloned.1.call-done.m_ref = bf16[16,250,380]{2,1,0:T(8,128)(2,1)} async-done(((bf16[1,250,380]{2,1,0:T(8,128)(2,1)}), bf16[16,250,380]{2,1,0:T(8,128)(2,1)}) %all-gather.10.cloned.1.call-update) | async-done | bytes 3040016 | tf_op jit(solution)/shard_map/all_gather | solution.py:252
  54.6 28.2 %shard_map.55 = (bf16[4,384,384]{2,1,0:T(8,128)(2,1)S(1)}, bf16[4,384,384]{2,1,0:T(8,128)(2,1)S(1)}, bf16[4,384,384]{2,1,0:T(8,128)(2,1)}, bf16[4,384,384]{2,1,0...) custom-call(s32[1]{0:T(128)} %bitcast.8.me_ref, bf16[250,32,4000]{2,1,0:T(8,128)(2,1)} %bitcast.43, ...), custom_call_target="tpu_custom_call" | custom-call | flops 12288000000 | bytes 32000000 | tf_op jit(solution)/shard_map/pallas_call | solution.py:144
  83.3 2.4 collective-permute-done
  85.7 1.9 collective-permute-done.1
  87.6 2.7 add.217
  90.3 1.4 collective-permute-start.5
  91.7 1.3 add.216
  93.0 26.7 %shard_map.56 = (bf16[4,384,384]{2,1,0:T(8,128)(2,1)S(1)}, bf16[4,384,384]{2,1,0:T(8,128)(2,1)S(1)}, bf16[4,384,384]{2,1,0:T(8,128)(2,1)}, bf16[4,384,384]{2,1,0:T(8,128)(2,1)}, f32[16,1,384]{2,1,0:T(1,128)S(1)}) custom-call(s32[1]{0:T(128)} %bitcast.8.me_ref, bf16[250,32,4000]{2,1,0:T(8,128)(2,1)} %bitcast.44, bf16[4000,384]{1,0:T(8,128)(2,1)} %get-tuple-element.40.m_ref, ...), custom_call_target="tpu_custom_call" | custom-call | flops 12288000000 | bytes 32000000 | tf_op jit(solution)/shard_map/pallas_call | solution.py:144
  120.6 0.7 collective-permute-start.3
  121.3 1.2 collective-permute-start.4
  122.5 1.9 collective-permute-done.6
  124.6 1.9 add.218
  126.6 1.1 collective-permute-start.11
  127.7 1.2 collective-permute-start.12
  128.9 1.7 add.228
  130.7 2.6 add.229
  133.2 1.2 collective-permute-start.13
  134.5 1.4 collective-permute-start.14
  135.9 27.1 %shard_map.57 = (bf16[16,250,384]{2,1,0:T(8,128)(2,1)}, bf16[4000,384]{1,0:T(8,128)(2,1)S(1)}) custom-call(bf16[250,32,4000]{2,1,0:T(8,128)(2,1)} %bitcast.45, bf16[16,250,380]{2,1,0:T(8,128)(2,1)} %all-gather.12.cloned.1.call-done.m_ref, f32[10,32,1]{2,1,0:T(8,128)S(1)} %copy.13.scale_ref, f32[8,128]{1,0:T(8,128)S(1)} %broadcast_in_dim.11.tie_ref), custom_call_target="tpu_custom_call" | custom-call | flops 12288000000 | bytes 32000000 | tf_op jit(solution)/shard_map/pallas_call | solution.py:169
  163.0 1.7 copy-done.1
  164.7 2.1 fusion.5
  166.8 2.7 collective-permute-start.8
  170.6 3.2 %collective-permute-start.15 = (bf16[384,384]{1,0:T(8,128)(2,1)S(1)}, bf16[384,384]{1,0:T(8,128)(2,1)S(1)}, u32[]{:S(2)}, u32[]{:S(2)}) collective-permute-start(bf16[384,384]{1,0:T(8,128)(2,1)S(1)} %get-tuple-element.75), channel_id=1, source_target_pairs={{0,4},{1,5},{2,6},{3,7},{4,8},{5,9},{6,10},{7,11},{8,12},{9,13},{1... | collective-permute-start | bytes 884744 | tf_op jit(solution)/shard_map/ppermute | solution.py:236
  173.9 1.1 collective-permute-start.16
  175.0 25.8 %shard_map.58.h_ref = bf16[16,250,384]{2,1,0:T(8,128)(2,1)} custom-call(bf16[250,32,4000]{2,1,0:T(8,128)(2,1)} %bitcast.46, bf16[4000,384]{1,0:T(8,128)(2,1)S(1)} %copy-done.2, f32[10,32,1]{2,1,0:T(8,128)S(1)} %copy.13.scale_ref, f32[8,128]{1,0:T(8,128)S(1)} %broadcast_in_dim.11.tie_ref), custom_call_target="tpu_custom_call" | custom-call | flops 12288000000 | bytes 32000000 | tf_op jit(solution)/shard_map/pallas_call | solution.py:169
  200.9 7.6 %collective-permute-done.16 = bf16[384,384]{1,0:T(8,128)(2,1)S(1)} collective-permute-done((bf16[384,384]{1,0:T(8,128)(2,1)S(1)}, bf16[384,384]{1,0:T(8,128)(2,1)S(1)}, u32[]{:S(2)}, u32[]{:S(2)}) %collective-permute-start.16) | collective-permute-done | bytes 294944 | tf_op jit(solution)/shard_map/ppermute | solution.py:236
  208.7 7.3 %collective-permute-start.19 = (bf16[384,384]{1,0:T(8,128)(2,1)S(1)}, bf16[384,384]{1,0:T(8,128)(2,1)}, u32[]{:S(2)}, u32[]{:S(2)}) collective-permute-start(bf16[384,384]{1,0:T(8,128)(2,1)S(1)} %fusion.2.rest_0_), channel_id=1, source_target_pairs={{0,8},{1,9},{2,10},{3,11},{4,12},{5,13},{6,14},{7,15},{8,0},{9,1},... | collective-permute-start | bytes 884744 | tf_op jit(solution)/shard_map/ppermute | solution.py:236
  216.0 1.9 collective-permute-start.20
  218.0 1.3 collective-permute-start.21
  219.3 0.7 copy-done.3
  220.0 5.8 %collective-permute-done.18.rest_1_ = bf16[384,384]{1,0:T(8,128)(2,1)} collective-permute-done((bf16[384,384]{1,0:T(8,128)(2,1)S(1)}, bf16[384,384]{1,0:T(8,128)(2,1)}, u32[]{:S(2)}, u32[]{:S(2)}) %collective-permute-start.18) | collective-permute-done | bytes 294944 | tf_op jit(solution)/shard_map/ppermute | solution.py:236
  225.8 1.6 collective-permute-start.22
  227.4 27.4 %collective-permute-done.19.rest_2_ = bf16[384,384]{1,0:T(8,128)(2,1)} collective-permute-done((bf16[384,384]{1,0:T(8,128)(2,1)S(1)}, bf16[384,384]{1,0:T(8,128)(2,1)}, u32[]{:S(2)}, u32[]{:S(2)}) %collective-permute-start.19) | collective-permute-done | bytes 294944 | tf_op jit(solution)/shard_map/ppermute | solution.py:236
  255.3 1.5 collective-permute-start.24
  256.8 0.7 copy-done.7
  257.5 0.7 copy-done.5
  259.0 6.0 %collective-permute-done.23.rest_6_ = bf16[384,384]{1,0:T(8,128)(2,1)} collective-permute-done((bf16[384,384]{1,0:T(8,128)(2,1)}, bf16[384,384]{1,0:T(8,128)(2,1)}, u32[]{:S(2)}, u32[]{:S(2)}) %collective-permute-start.23) | collective-permute-done | bytes 294944 | tf_op jit(solution)/shard_map/ppermute | solution.py:233
  265.0 3.2 %collective-permute-done.24.rest_7_ = bf16[384,384]{1,0:T(8,128)(2,1)} collective-permute-done((bf16[384,384]{1,0:T(8,128)(2,1)}, bf16[384,384]{1,0:T(8,128)(2,1)}, u32[]{:S(2)}, u32[]{:S(2)}) %collective-permute-start.24) | collective-permute-done | bytes 294944 | tf_op jit(solution)/shard_map/ppermute | solution.py:233
  268.9 4.7 %shard_map.59.base_ref = f32[250,384]{1,0:T(8,128)S(1)} custom-call(f32[16]{0:T(128)S(1)} %get-tuple-element.79.gamma_ref, f32[250,384]{1,0:T(8,128)S(1)} %broadcast_in_dim.12.base_ref, bf16[16,250,384]{2,1,0:T(8,128)(2,1)S(1)} %copy-done, bf16[16,384,384]{2,1,0:T(8,128)(2,1)} %bitcast.47), custom_call_target="tpu_custom_call" | custom-call | flops 1179648000 | bytes 4718592 | tf_op jit(solution)/shard_map/pallas_call | solution.py:188
  273.6 3.5 %shard_map.60.base_ref = f32[250,384]{1,0:T(8,128)S(1)} custom-call(s32[8]{0:T(128)S(1)} %stack.71.owners_ref, f32[16]{0:T(128)S(1)} %get-tuple-element.80.gamma_ref, f32[250,384]{1,0:T(8,128)S(1)} %shard_map.59.base_ref, bf16[16,250,384]{2,1,0:T(8,128)(2,1)} %shard_map.58.h_ref, bf16[384,384]{1,0:T(8,128)(2,1)S(1)} %copy-done.4, ...), custom_call_target="tpu_custom_call" | custom-call | flops 589824000 | bytes 2359296 | tf_op jit(solution)/shard_map/pallas_call | solution.py:206
  277.2 3.5 %shard_map.61 = f32[250,384]{1,0:T(8,128)S(1)} custom-call(s32[8]{0:T(128)S(1)} %stack.62.owners_ref, f32[16]{0:T(128)S(1)} %get-tuple-element.80.gamma_ref, f32[250,384]{1,0:T(8,128)S(1)} %shard_map.60.base_ref, bf16[16,250,384]{2,1,0:T(8,128)(2,1)} %shard_map.58.h_ref, bf16[384,384]{1,0:T(8,128)(2,1)S(1)} %copy-done.6, ...), custom_call_target="tpu_custom_call" | custom-call | flops 589824000 | bytes 2359296 | tf_op jit(solution)/shard_map/pallas_call | solution.py:206
  281.2 11.0 %collective-permute-done.33 = f32[250,384]{1,0:T(8,128)S(1)} collective-permute-done((f32[250,384]{1,0:T(8,128)S(1)}, f32[250,384]{1,0:T(8,128)S(1)}, u32[]{:S(2)}, u32[]{:S(2)}) %collective-permute-start.33) | collective-permute-done | bytes 384032 | tf_op jit(solution)/shard_map/ppermute | solution.py:345
  292.2 0.8 fusion.6
  (82 shorter events, 5.8 us)
Async XLA Ops:
  6.5 48.1 %all-gather.10.cloned.1.call-start = ((), (), s32[]{:S(2)}) async-start(), calls=%async_computation.1 | async-start | bytes 3342336 | tf_op jit(solution)/shard_map/all_gather | solution.py:252
  7.3 128.6 %all-gather.12.cloned.1.call-start = ((), (), s32[]{:S(2)}) async-start(), calls=%async_computation.2 | async-start | bytes 3342336 | tf_op jit(solution)/shard_map/all_gather | solution.py:253
  8.0 260.9 %all-gather.8.cloned.1.call-start = ((), (), s32[]{:S(2)}) async-start(), calls=%async_computation | async-start | bytes 5013504 | tf_op jit(solution)/shard_map/all_gather | solution.py:270
  82.8 2.9 collective-permute-start
  83.1 4.6 %collective-permute-start.1 = (bf16[4,384,384]{2,1,0:T(8,128)(2,1)}, bf16[4,384,384]{2,1,0:T(8,128)(2,1)S(1)}, u32[]{:S(2)}, u32[]{:S(2)}) collective-permute-start(bf16[4,384,384]{2,1,0:T(8,128)(2,1)} %get-tuple-element.43), channel_id=1, source_target_pairs={{0,1},{1,0},{2,3},{3,2},{4,5},{5,4},{6,7},{7,6},{8,9},{9,8},{10,11... | collective-permute-start | bytes 3538952 | tf_op jit(solution)/shard_map/ppermute | solution.py:233
  90.3 31.0 %collective-permute-start.5 = (bf16[4,384,384]{2,1,0:T(8,128)(2,1)}, bf16[4,384,384]{2,1,0:T(8,128)(2,1)}, u32[]{:S(2)}, u32[]{:S(2)}) collective-permute-start(bf16[4,384,384]{2,1,0:T(8,128)(2,1)} %add.217), channel_id=1, source_target_pairs={{0,2},{1,3},{2,0},{3,1},{4,6},{5,7},{6,4},{7,5},{8,10},{9,11},{10,... | collective-permute-start | bytes 3538952 | tf_op jit(solution)/shard_map/ppermute | solution.py:233
  119.7 4.6 %collective-permute-start.6 = (bf16[4,384,384]{2,1,0:T(8,128)(2,1)S(1)}, bf16[4,384,384]{2,1,0:T(8,128)(2,1)}, u32[]{:S(2)}, u32[]{:S(2)}) collective-permute-start(bf16[4,384,384]{2,1,0:T(8,128)(2,1)S(1)} %get-tuple-element.49), channel_id=1, source_target_pairs={{0,1},{1,0},{2,3},{3,2},{4,5},{5,4},{6,7},{7,6},{8,9},{9,8},{10,11... | collective-permute-start | bytes 3538952 | tf_op jit(solution)/shard_map/ppermute | solution.py:233
  119.7 4.9 %collective-permute-start.7 = (bf16[4,384,384]{2,1,0:T(8,128)(2,1)}, bf16[4,384,384]{2,1,0:T(8,128)(2,1)}, u32[]{:S(2)}, u32[]{:S(2)}) collective-permute-start(bf16[4,384,384]{2,1,0:T(8,128)(2,1)} %get-tuple-element.50), channel_id=1, source_target_pairs={{0,1},{1,0},{2,3},{3,2},{4,5},{5,4},{6,7},{7,6},{8,9},{9,8},{10,11... | collective-permute-start | bytes 3538952 | tf_op jit(solution)/shard_map/ppermute | solution.py:233
  120.5 12.7 %collective-permute-start.2 = (f32[32]{0:T(128)S(1)}, f32[32]{0:T(128)S(1)}, u32[]{:S(2)}, u32[]{:S(2)}) collective-permute-start(f32[32]{0:T(128)S(1)} %maximum_reduce_fusion), channel_id=1, source_target_pairs={{0,1},{1,0},{2,3},{3,2},{4,5},{5,4},{6,7},{7,6},{8,9},{9,8},{10,11... | collective-permute-start | bytes 392 | tf_op jit(solution)/shard_map/ppermute | solution.py:233
  120.6 13.9 %collective-permute-start.3 = (f32[32]{0:T(128)S(1)}, f32[32]{0:T(128)S(1)}, u32[]{:S(2)}, u32[]{:S(2)}) collective-permute-start(f32[32]{0:T(128)S(1)} %maximum_reduce_fusion), channel_id=1, source_target_pairs={{0,2},{1,3},{2,0},{3,1},{4,6},{5,7},{6,4},{7,5},{8,10},{9,11},{10,... | collective-permute-start | bytes 392 | tf_op jit(solution)/shard_map/ppermute | solution.py:233
  121.3 43.3 %collective-permute-start.4 = (f32[32]{0:T(128)S(1)}, f32[32]{0:T(128)S(1)}, u32[]{:S(2)}, u32[]{:S(2)}) collective-permute-start(f32[32]{0:T(128)S(1)} %maximum_reduce_fusion), channel_id=1, source_target_pairs={{0,3},{1,2},{2,1},{3,0},{4,7},{5,6},{6,5},{7,4},{8,11},{9,10},{10,... | collective-permute-start | bytes 392 | tf_op jit(solution)/shard_map/ppermute | solution.py:233
  126.5 4.1 %copy-start.9 = (bf16[4,384,384]{2,1,0:T(8,128)(2,1)}, bf16[4,384,384]{2,1,0:T(8,128)(2,1)S(1)}, u32[]{:S(2)}) copy-start(bf16[4,384,384]{2,1,0:T(8,128)(2,1)S(1)} %add.218) | copy-start | bytes 3538948
  126.6 38.0 %collective-permute-start.11 = (bf16[384,384]{1,0:T(8,128)(2,1)S(1)}, bf16[384,384]{1,0:T(8,128)(2,1)}, u32[]{:S(2)}, u32[]{:S(2)}) collective-permute-start(bf16[384,384]{1,0:T(8,128)(2,1)S(1)} %get-tuple-element.78), channel_id=1, source_target_pairs={{0,4},{1,5},{2,6},{3,7},{4,8},{5,9},{6,10},{7,11},{8,12},{9,13},{1... | collective-permute-start | bytes 884744 | tf_op jit(solution)/shard_map/ppermute | solution.py:236
  127.7 36.9 %collective-permute-start.12 = (bf16[384,384]{1,0:T(8,128)(2,1)S(1)}, bf16[384,384]{1,0:T(8,128)(2,1)}, u32[]{:S(2)}, u32[]{:S(2)}) collective-permute-start(bf16[384,384]{1,0:T(8,128)(2,1)S(1)} %get-tuple-element.77), channel_id=1, source_target_pairs={{0,8},{1,9},{2,10},{3,11},{4,12},{5,13},{6,14},{7,15},{8,0},{9,1},... | collective-permute-start | bytes 884744 | tf_op jit(solution)/shard_map/ppermute | solution.py:236
  128.9 1.7 copy-start.10
  133.2 31.4 %collective-permute-start.13 = (bf16[384,384]{1,0:T(8,128)(2,1)S(1)}, bf16[384,384]{1,0:T(8,128)(2,1)}, u32[]{:S(2)}, u32[]{:S(2)}) collective-permute-start(bf16[384,384]{1,0:T(8,128)(2,1)S(1)} %get-tuple-element.76), channel_id=1, source_target_pairs={{0,12},{1,13},{2,14},{3,15},{4,0},{5,1},{6,2},{7,3},{8,4},{9,5},{1... | collective-permute-start | bytes 884744 | tf_op jit(solution)/shard_map/ppermute | solution.py:236
  134.5 30.2 %collective-permute-start.14 = (bf16[4,384,384]{2,1,0:T(8,128)(2,1)}, bf16[4,384,384]{2,1,0:T(8,128)(2,1)S(1)}, u32[]{:S(2)}, u32[]{:S(2)}) collective-permute-start(bf16[4,384,384]{2,1,0:T(8,128)(2,1)} %add.229), channel_id=1, source_target_pairs={{0,2},{1,3},{2,0},{3,1},{4,6},{5,7},{6,4},{7,5},{8,10},{9,11},{10,... | collective-permute-start | bytes 3538952 | tf_op jit(solution)/shard_map/ppermute | solution.py:233
  163.0 1.7 copy-start.1
  166.8 8.2 %collective-permute-start.8 = (f32[32]{0:T(128)S(1)}, f32[32]{0:T(128)S(1)}, u32[]{:S(2)}, u32[]{:S(2)}) collective-permute-start(f32[32]{0:T(128)S(1)} %add_add_fusion.1), channel_id=1, source_target_pairs={{0,4},{1,5},{2,6},{3,7},{4,8},{5,9},{6,10},{7,11},{8,12},{9,13},{1... | collective-permute-start | bytes 392 | tf_op jit(solution)/shard_map/ppermute | solution.py:236
  169.5 31.3 %collective-permute-start.9 = (f32[32]{0:T(128)S(1)}, f32[32]{0:T(128)S(1)}, u32[]{:S(2)}, u32[]{:S(2)}) collective-permute-start(f32[32]{0:T(128)S(1)} %add_add_fusion.1), channel_id=1, source_target_pairs={{0,8},{1,9},{2,10},{3,11},{4,12},{5,13},{6,14},{7,15},{8,0},{9,1},... | collective-permute-start | bytes 392 | tf_op jit(solution)/shard_map/ppermute | solution.py:236
  169.5 31.3 %collective-permute-start.10 = (f32[32]{0:T(128)S(1)}, f32[32]{0:T(128)S(1)}, u32[]{:S(2)}, u32[]{:S(2)}) collective-permute-start(f32[32]{0:T(128)S(1)} %add_add_fusion.1), channel_id=1, source_target_pairs={{0,12},{1,13},{2,14},{3,15},{4,0},{5,1},{6,2},{7,3},{8,4},{9,5},{1... | collective-permute-start | bytes 392 | tf_op jit(solution)/shard_map/ppermute | solution.py:236
  170.2 4.8 %copy-start.2 = (bf16[4000,384]{1,0:T(8,128)(2,1)S(1)}, bf16[4000,384]{1,0:T(8,128)(2,1)}, u32[]{:S(2)}) copy-start(bf16[4000,384]{1,0:T(8,128)(2,1)} %copy-done.1) | copy-start | bytes 9216004
  170.6 30.2 %collective-permute-start.15 = (bf16[384,384]{1,0:T(8,128)(2,1)S(1)}, bf16[384,384]{1,0:T(8,128)(2,1)S(1)}, u32[]{:S(2)}, u32[]{:S(2)}) collective-permute-start(bf16[384,384]{1,0:T(8,128)(2,1)S(1)} %get-tuple-element.75), channel_id=1, source_target_pairs={{0,4},{1,5},{2,6},{3,7},{4,8},{5,9},{6,10},{7,11},{8,12},{9,13},{1... | collective-permute-start | bytes 884744 | tf_op jit(solution)/shard_map/ppermute | solution.py:236
  173.9 34.6 %collective-permute-start.16 = (bf16[384,384]{1,0:T(8,128)(2,1)S(1)}, bf16[384,384]{1,0:T(8,128)(2,1)S(1)}, u32[]{:S(2)}, u32[]{:S(2)}) collective-permute-start(bf16[384,384]{1,0:T(8,128)(2,1)S(1)} %get-tuple-element.74), channel_id=1, source_target_pairs={{0,8},{1,9},{2,10},{3,11},{4,12},{5,13},{6,14},{7,15},{8,0},{9,1},... | collective-permute-start | bytes 884744 | tf_op jit(solution)/shard_map/ppermute | solution.py:236
  175.0 33.5 %collective-permute-start.17 = (bf16[384,384]{1,0:T(8,128)(2,1)S(1)}, bf16[384,384]{1,0:T(8,128)(2,1)S(1)}, u32[]{:S(2)}, u32[]{:S(2)}) collective-permute-start(bf16[384,384]{1,0:T(8,128)(2,1)S(1)} %get-tuple-element.73), channel_id=1, source_target_pairs={{0,12},{1,13},{2,14},{3,15},{4,0},{5,1},{6,2},{7,3},{8,4},{9,5},{1... | collective-permute-start | bytes 884744 | tf_op jit(solution)/shard_map/ppermute | solution.py:236
  175.0 93.9 %copy-start = (bf16[16,250,384]{2,1,0:T(8,128)(2,1)S(1)}, bf16[16,250,384]{2,1,0:T(8,128)(2,1)}, u32[]{:S(2)}) copy-start(bf16[16,250,384]{2,1,0:T(8,128)(2,1)} %get-tuple-element.57.h_ref) | copy-start | bytes 9216004
  208.7 17.1 %collective-permute-start.18 = (bf16[384,384]{1,0:T(8,128)(2,1)S(1)}, bf16[384,384]{1,0:T(8,128)(2,1)}, u32[]{:S(2)}, u32[]{:S(2)}) collective-permute-start(bf16[384,384]{1,0:T(8,128)(2,1)S(1)} %fusion.2.rest_0_), channel_id=1, source_target_pairs={{0,4},{1,5},{2,6},{3,7},{4,8},{5,9},{6,10},{7,11},{8,12},{9,13},{1... | collective-permute-start | bytes 884744 | tf_op jit(solution)/shard_map/ppermute | solution.py:236
  208.7 46.0 %collective-permute-start.19 = (bf16[384,384]{1,0:T(8,128)(2,1)S(1)}, bf16[384,384]{1,0:T(8,128)(2,1)}, u32[]{:S(2)}, u32[]{:S(2)}) collective-permute-start(bf16[384,384]{1,0:T(8,128)(2,1)S(1)} %fusion.2.rest_0_), channel_id=1, source_target_pairs={{0,8},{1,9},{2,10},{3,11},{4,12},{5,13},{6,14},{7,15},{8,0},{9,1},... | collective-permute-start | bytes 884744 | tf_op jit(solution)/shard_map/ppermute | solution.py:236
  216.0 39.3 %collective-permute-start.20 = (bf16[384,384]{1,0:T(8,128)(2,1)S(1)}, bf16[384,384]{1,0:T(8,128)(2,1)}, u32[]{:S(2)}, u32[]{:S(2)}) collective-permute-start(bf16[384,384]{1,0:T(8,128)(2,1)S(1)} %fusion.2.rest_0_), channel_id=1, source_target_pairs={{0,12},{1,13},{2,14},{3,15},{4,0},{5,1},{6,2},{7,3},{8,4},{9,5},{1... | collective-permute-start | bytes 884744 | tf_op jit(solution)/shard_map/ppermute | solution.py:236
  218.0 38.8 %collective-permute-start.21 = (bf16[384,384]{1,0:T(8,128)(2,1)S(1)}, bf16[384,384]{1,0:T(8,128)(2,1)S(1)}, u32[]{:S(2)}, u32[]{:S(2)}) collective-permute-start(bf16[384,384]{1,0:T(8,128)(2,1)S(1)} %fusion.2.rest_0_), channel_id=1, source_target_pairs={{0,2},{1,3},{2,0},{3,1},{4,6},{5,7},{6,4},{7,5},{8,10},{9,11},{10,... | collective-permute-start | bytes 884744 | tf_op jit(solution)/shard_map/ppermute | solution.py:233
  219.3 37.5 %collective-permute-start.25 = (bf16[384,384]{1,0:T(8,128)(2,1)S(1)}, bf16[384,384]{1,0:T(8,128)(2,1)S(1)}, u32[]{:S(2)}, u32[]{:S(2)}) collective-permute-start(bf16[384,384]{1,0:T(8,128)(2,1)S(1)} %fusion.2.rest_0_), channel_id=1, source_target_pairs={{0,1},{1,0},{2,3},{3,2},{4,5},{5,4},{6,7},{7,6},{8,9},{9,8},{10,11... | collective-permute-start | bytes 884744 | tf_op jit(solution)/shard_map/ppermute | solution.py:233
  219.3 0.7 copy-start.3
  225.8 32.6 %collective-permute-start.22 = (bf16[384,384]{1,0:T(8,128)(2,1)}, bf16[384,384]{1,0:T(8,128)(2,1)}, u32[]{:S(2)}, u32[]{:S(2)}) collective-permute-start(bf16[384,384]{1,0:T(8,128)(2,1)} %collective-permute-done.18.rest_1_), channel_id=1, source_target_pairs={{0,2},{1,3},{2,0},{3,1},{4,6},{5,7},{6,4},{7,5},{8,10},{9,11},{10,... | collective-permute-start | bytes 884744 | tf_op jit(solution)/shard_map/ppermute | solution.py:233
  254.7 10.3 %collective-permute-start.23 = (bf16[384,384]{1,0:T(8,128)(2,1)}, bf16[384,384]{1,0:T(8,128)(2,1)}, u32[]{:S(2)}, u32[]{:S(2)}) collective-permute-start(bf16[384,384]{1,0:T(8,128)(2,1)} %collective-permute-done.19.rest_2_), channel_id=1, source_target_pairs={{0,2},{1,3},{2,0},{3,1},{4,6},{5,7},{6,4},{7,5},{8,10},{9,11},{10,... | collective-permute-start | bytes 884744 | tf_op jit(solution)/shard_map/ppermute | solution.py:233
  255.3 12.9 %collective-permute-start.24 = (bf16[384,384]{1,0:T(8,128)(2,1)}, bf16[384,384]{1,0:T(8,128)(2,1)}, u32[]{:S(2)}, u32[]{:S(2)}) collective-permute-start(bf16[384,384]{1,0:T(8,128)(2,1)} %collective-permute-done.20.rest_3_), channel_id=1, source_target_pairs={{0,2},{1,3},{2,0},{3,1},{4,6},{5,7},{6,4},{7,5},{8,10},{9,11},{10,... | collective-permute-start | bytes 884744 | tf_op jit(solution)/shard_map/ppermute | solution.py:233
  256.8 0.7 copy-start.7
  256.8 11.4 %collective-permute-start.26 = (bf16[384,384]{1,0:T(8,128)(2,1)}, bf16[384,384]{1,0:T(8,128)(2,1)}, u32[]{:S(2)}, u32[]{:S(2)}) collective-permute-start(bf16[384,384]{1,0:T(8,128)(2,1)} %collective-permute-done.18.rest_1_), channel_id=1, source_target_pairs={{0,1},{1,0},{2,3},{3,2},{4,5},{5,4},{6,7},{7,6},{8,9},{9,8},{10,11... | collective-permute-start | bytes 884744 | tf_op jit(solution)/shard_map/ppermute | solution.py:233
  257.5 0.7 copy-start.5
  258.2 10.5 %collective-permute-start.27 = (bf16[384,384]{1,0:T(8,128)(2,1)}, bf16[384,384]{1,0:T(8,128)(2,1)}, u32[]{:S(2)}, u32[]{:S(2)}) collective-permute-start(bf16[384,384]{1,0:T(8,128)(2,1)} %collective-permute-done.19.rest_2_), channel_id=1, source_target_pairs={{0,1},{1,0},{2,3},{3,2},{4,5},{5,4},{6,7},{7,6},{8,9},{9,8},{10,11... | collective-permute-start | bytes 884744 | tf_op jit(solution)/shard_map/ppermute | solution.py:233
  258.4 18.7 %collective-permute-start.28 = (bf16[384,384]{1,0:T(8,128)(2,1)}, bf16[384,384]{1,0:T(8,128)(2,1)}, u32[]{:S(2)}, u32[]{:S(2)}) collective-permute-start(bf16[384,384]{1,0:T(8,128)(2,1)} %collective-permute-done.20.rest_3_), channel_id=1, source_target_pairs={{0,1},{1,0},{2,3},{3,2},{4,5},{5,4},{6,7},{7,6},{8,9},{9,8},{10,11... | collective-permute-start | bytes 884744 | tf_op jit(solution)/shard_map/ppermute | solution.py:233
  265.0 12.1 %collective-permute-start.29 = (bf16[384,384]{1,0:T(8,128)(2,1)}, bf16[384,384]{1,0:T(8,128)(2,1)}, u32[]{:S(2)}, u32[]{:S(2)}) collective-permute-start(bf16[384,384]{1,0:T(8,128)(2,1)} %copy-done.7), channel_id=1, source_target_pairs={{0,1},{1,0},{2,3},{3,2},{4,5},{5,4},{6,7},{7,6},{8,9},{9,8},{10,11... | collective-permute-start | bytes 884744 | tf_op jit(solution)/shard_map/ppermute | solution.py:233
  268.2 8.9 %collective-permute-start.30 = (bf16[384,384]{1,0:T(8,128)(2,1)}, bf16[384,384]{1,0:T(8,128)(2,1)}, u32[]{:S(2)}, u32[]{:S(2)}) collective-permute-start(bf16[384,384]{1,0:T(8,128)(2,1)} %collective-permute-done.22.rest_5_), channel_id=1, source_target_pairs={{0,1},{1,0},{2,3},{3,2},{4,5},{5,4},{6,7},{7,6},{8,9},{9,8},{10,11... | collective-permute-start | bytes 884744 | tf_op jit(solution)/shard_map/ppermute | solution.py:233
  268.2 8.9 %collective-permute-start.31 = (bf16[384,384]{1,0:T(8,128)(2,1)}, bf16[384,384]{1,0:T(8,128)(2,1)}, u32[]{:S(2)}, u32[]{:S(2)}) collective-permute-start(bf16[384,384]{1,0:T(8,128)(2,1)} %collective-permute-done.23.rest_6_), channel_id=1, source_target_pairs={{0,1},{1,0},{2,3},{3,2},{4,5},{5,4},{6,7},{7,6},{8,9},{9,8},{10,11... | collective-permute-start | bytes 884744 | tf_op jit(solution)/shard_map/ppermute | solution.py:233
  268.7 8.4 %collective-permute-start.32 = (bf16[384,384]{1,0:T(8,128)(2,1)}, bf16[384,384]{1,0:T(8,128)(2,1)}, u32[]{:S(2)}, u32[]{:S(2)}) collective-permute-start(bf16[384,384]{1,0:T(8,128)(2,1)} %collective-permute-done.24.rest_7_), channel_id=1, source_target_pairs={{0,1},{1,0},{2,3},{3,2},{4,5},{5,4},{6,7},{7,6},{8,9},{9,8},{10,11... | collective-permute-start | bytes 884744 | tf_op jit(solution)/shard_map/ppermute | solution.py:233
  268.9 4.7 %copy-start.4 = (bf16[384,384]{1,0:T(8,128)(2,1)S(1)}, bf16[384,384]{1,0:T(8,128)(2,1)}, u32[]{:S(2)}) copy-start(bf16[384,384]{1,0:T(8,128)(2,1)} %copy-done.3) | copy-start | bytes 884740
  268.9 4.7 %copy-start.8 = (bf16[384,384]{1,0:T(8,128)(2,1)S(1)}, bf16[384,384]{1,0:T(8,128)(2,1)}, u32[]{:S(2)}) copy-start(bf16[384,384]{1,0:T(8,128)(2,1)} %copy-done.7) | copy-start | bytes 884740
  273.6 3.5 %copy-start.6 = (bf16[384,384]{1,0:T(8,128)(2,1)S(1)}, bf16[384,384]{1,0:T(8,128)(2,1)}, u32[]{:S(2)}) copy-start(bf16[384,384]{1,0:T(8,128)(2,1)} %copy-done.5) | copy-start | bytes 884740
  280.7 11.5 %collective-permute-start.33 = (f32[250,384]{1,0:T(8,128)S(1)}, f32[250,384]{1,0:T(8,128)S(1)}, u32[]{:S(2)}, u32[]{:S(2)}) collective-permute-start(f32[250,384]{1,0:T(8,128)S(1)} %shard_map.61), channel_id=1, source_target_pairs={{0,16},{16,0},{1,17},{17,1},{2,18},{18,2},{3,19},{19,3},{4,20},{20... | collective-permute-start | bytes 1152008 | tf_op jit(solution)/shard_map/ppermute | solution.py:345
Sparse Core Ops, SparseCore 0:
  9.6 44.9 all-gather.9
  56.9 43.9 all-gather.11
  166.9 87.1 all-gather.7

commit v5 on v4

--- a/solution.py
+++ b/solution.py
@@ -283,11 +283,13 @@
     def in_transit(c):
         return left[c] > 0
 
-    def advance(which, done=()):
+    def advance(which, done=(), chained=False):
         which = [c for c in which if in_transit(c)]
         arrived = after([waiting[c] for c in which], done)
+        sent = ()
         for c, got in zip(which, arrived):
-            waiting[c], marks[c] = flows[c].send(got)
+            waiting[c], marks[c] = flows[c].send(after(got, sent) if chained else got)
+            sent = marks[c]
             left[c] -= 1
 
     marks = {}
@@ -295,55 +297,63 @@
         out = rot_part(
             me, by_rows, whole_r, scale, ct, weighted, after(start, marks), c, paux, fan, nz, cuts
         )
-        first, g = out[:fan], out[fan]
+        first, g = after(out[:fan], waiting), out[fan]
         if c == 0:
             whole_r = out[fan + 1]
         gammas.append(g)
         flows.append(reduce_steps(first, cuts == 1 and c == chunks - 1 > 0))
         got, marks[c] = next(flows[c])
         waiting.append(got)
-        advance(range(c + 1), g)
+        advance(range(c + 1), g, chained=True)
     gamma = jnp.sum(jnp.concatenate(gammas, axis=0), axis=(1, 2))
-    hops = [
-        [functools.partial(swap, bit=d) for d in range(1, fan)],
-        [functools.partial(turn_z, by=d) for d in range(1, nz)],
-    ]
+    gamma = functools.reduce(jnp.add, [swap(gamma, d) for d in range(1, fan)], gamma)
+    far = [turn_z(gamma, d) for d in range(1, nz)]
     for c in range(chunks):
-        hop = hops.pop(0) if hops else []
-        got = [move(gamma) for move in hop]
         out, *extra = occ_part(by_rows, whole_c, scale, after(start, (marks, gamma)), c, paux)
         if extra:
             whole_c = extra[0]
         occ.append(out)
-        for part in after(got, out):
-            gamma = gamma + part
+        if c == 0:
+            gamma = functools.reduce(jnp.add, after(far, out), gamma)
         if any(left):
-            advance(range(chunks), (out, gamma))
-    for hop in hops:
-        gamma = functools.reduce(jnp.add, [move(gamma) for move in hop], gamma)
+            advance(reversed(range(chunks)), (out, gamma), chained=True)
     while any(left):
         advance(range(chunks))
 
-    sigma = jnp.zeros((rows, width), F32)
+    def over_aux(value):
+        bit = 1
+        while bit < parts:
+            value = value + lax.ppermute(value, "aux", [(i, i ^ bit) for i in range(parts)])
+            bit *= 2
+        return value
+
+    early = zero = jnp.zeros((rows, width), F32)
+    late = None
     for c in range(chunks):
         g = gamma[c * paux : (c + 1) * paux]
         if isinstance(waiting[c], jax.Array):
-            sigma = sigma_part(g, sigma, occ[c], waiting[c])
+            early = sigma_part(g, early, occ[c], waiting[c])
             continue
         shards = waiting[c]
         order = [0]
         for bit in reversed(bits):
             order = order + [d ^ bit for d in order]
+        late = zero
         for lo in range(0, fan, fan // ncore):
             some = range(lo, lo + fan // ncore)
             owners = [(z - k) % nz * fan + (index % fan ^ order[d]) for d in some for k in range(nz)]
-            sigma = sigma_shards(
-                jnp.stack(owners).astype(jnp.int32), g, sigma, occ[c], [v for d in some for v in shards[d]]
-            )
-    bit = 1
-    while bit < parts:
-        sigma = sigma + lax.ppermute(sigma, "aux", [(i, i ^ bit) for i in range(parts)])
-        bit *= 2
+            some = [v for d in some for v in shards[d]]
+            late = sigma_shards(jnp.stack(owners).astype(jnp.int32), g, late, occ[c], some)
+    sigma = over_aux(early)
+    if late is not None:
+        late = late.astype(BF16)
+        bit = 1
+        while bit < parts:
+            got = lax.ppermute(late, "aux", [(i, i ^ bit) for i in range(parts)])
+            late = late.astype(F32) + got.astype(F32)
+            bit *= 2
+            late = late.astype(BF16) if bit < parts else late
+        sigma = sigma + late
     return sigma[:, :nint] / math.sqrt(naux * parts * nint)
 
 

time: 301 us -> 306 us (1.017); the launches traced: 300 us -> 301 us
  waiting for transfers between devices: 113 us -> 102 us
  local copies, waits for them, and re-layouts: 6.26 us -> 15.7 us
    unnamed x23 -> x47, local copies, waits for them, and re-layouts: 4.9 us -> 13.5 us
    ppermute x1 -> x2, waiting for transfers between devices: 11 us -> 5.34 us  [the longest x1 5.33 us: body(): got = lax.ppermute(late, 'aux', [(i, i ^ bit) for i in range(parts)])]
    ppermute x21, waiting for transfers between devices: 15.7 us -> 11.4 us  [swap(): return lax.ppermute(value, 'ao', [(i, i ^ bit) for i in range(groups)])]
  transfers between devices with their start and end apart: 37 -> 38, of which waited for: 11 -> 11; matrix products, arithmetic and copies ran while one was open for 5% -> 5% of each run, Pallas kernels for 39% -> 40%
where the time goes in v5:
time: 306 us; the launch traced here: 301 us
  Pallas kernels  120 us (39%)
  waiting for transfers between devices  102 us (33%)
  starting transfers between devices  33.1 us (11%)
  other arithmetic  16.9 us (6%)
  local copies, waits for them, and re-layouts  15.7 us (5%)
  between operations  13.4 us (4%)
    pallas_call x2, Pallas kernels, rot_part(): pl.pallas_call(functools.partial(rot_kernel, paux, fan, nz, cuts), grid_s...  54.9 us
    pallas_call x2, Pallas kernels, occ_part(): pl.pallas_call(functools.partial(occ_kernel, paux), grid=(nscale,), in_sp...  52.9 us
    all_gather x1, waiting for transfers between devices, body(): whole_r = lax.all_gather(rot_coeff, 'ao', axis=0)  43.6 us
    ppermute x12, waiting for transfers between devices, turn_z(): lax.ppermute(value, 'ao', [(i, (i + by * fan) % groups) for i in range(gr...  40.6 us
    ppermute x12, starting transfers between devices, turn_z(): lax.ppermute(value, 'ao', [(i, (i + by * fan) % groups) for i in range(gr...  19.1 us
    unnamed x47, local copies, waits for them, and re-layouts  13.5 us
    ppermute x21, starting transfers between devices, swap(): return lax.ppermute(value, 'ao', [(i, i ^ bit) for i in range(groups)])  11.8 us
    ppermute x21, waiting for transfers between devices, swap(): return lax.ppermute(value, 'ao', [(i, i ^ bit) for i in range(groups)])  11.4 us
  transfers between devices with their start and end apart: 38, of which 11 were waited for; matrix products, arithmetic and copies ran while one was open for 5% of the time, Pallas kernels for 40%

profile of v5, /device:TPU:28, one launch (start us, length us, event | category | flops | bytes accessed | tf_op | source)
XLA Modules:
  0.0 301.4 jit_solution(16862872325471513179)
XLA Ops:
  8.1 1.1 copy.12
  11.0 43.6 %all-gather.10.cloned.1.call-done.m_ref = bf16[16,250,380]{2,1,0:T(8,128)(2,1)} async-done(((bf16[1,250,380]{2,1,0:T(8,128)(2,1)}), bf16[16,250,380]{2,1,0:T(8,128)(2,1)}) %all-gather.10.cloned.1.call-update) | async-done | bytes 3040016 | tf_op jit(solution)/shard_map/all_gather | solution.py:252
  54.6 28.2 %shard_map.55 = (bf16[4,384,384]{2,1,0:T(8,128)(2,1)S(1)}, bf16[4,384,384]{2,1,0:T(8,128)(2,1)S(1)}, bf16[4,384,384]{2,1,0:T(8,128)(2,1)}, bf16[4,384,384]{2,1,0...) custom-call(s32[1]{0:T(128)} %bitcast.me_ref, bf16[250,32,4000]{2,1,0:T(8,128)(2,1)} %bitcast.43, ...), custom_call_target="tpu_custom_call" | custom-call | flops 12288000000 | bytes 32000000 | tf_op jit(solution)/shard_map/pallas_call | solution.py:144
  83.3 2.4 collective-permute-done
  85.7 1.9 collective-permute-done.1
  87.6 1.6 add.211
  89.3 1.5 collective-permute-start.8
  90.7 1.3 add.210
  92.1 26.6 %shard_map.56 = (bf16[4,384,384]{2,1,0:T(8,128)(2,1)S(1)}, bf16[4,384,384]{2,1,0:T(8,128)(2,1)S(1)}, bf16[4,384,384]{2,1,0:T(8,128)(2,1)}, bf16[4,384,384]{2,1,0:T(8,128)(2,1)}, f32[16,1,384]{2,1,0:T(1,128)S(1)}) custom-call(s32[1]{0:T(128)} %bitcast.me_ref, bf16[250,32,4000]{2,1,0:T(8,128)(2,1)} %bitcast.44, bf16[4000,384]{1,0:T(8,128)(2,1)} %get-tuple-element.55.m_ref, ...), custom_call_target="tpu_custom_call" | custom-call | flops 12288000000 | bytes 32000000 | tf_op jit(solution)/shard_map/pallas_call | solution.py:144
  118.7 1.0 copy-done.18
  121.3 1.1 collective-permute-start.4
  122.5 1.7 collective-permute-done.2
  124.3 1.8 collective-permute-start.5
  126.1 1.4 collective-permute-start.6
  127.4 1.1 collective-permute-start.7
  128.6 1.9 add.215
  130.6 2.9 collective-permute-start.12
  133.6 2.7 add.226
  136.9 1.6 add.225
  138.6 1.8 collective-permute-start.14
  140.4 27.1 %shard_map.57 = (bf16[16,250,384]{2,1,0:T(8,128)(2,1)}, bf16[4000,384]{1,0:T(8,128)(2,1)S(1)}) custom-call(bf16[250,32,4000]{2,1,0:T(8,128)(2,1)} %bitcast.45, bf16[16,250,380]{2,1,0:T(8,128)(2,1)} %all-gather.12.cloned.1.call-done.m_ref, f32[10,32,1]{2,1,0:T(8,128)S(1)} %copy.13.scale_ref, f32[8,128]{1,0:T(8,128)S(1)} %broadcast_in_dim.11.tie_ref), custom_call_target="tpu_custom_call" | custom-call | flops 12288000000 | bytes 32000000 | tf_op jit(solution)/shard_map/pallas_call | solution.py:169
  168.3 1.0 copy-done.21
  169.3 1.6 add.232
  172.4 1.9 fusion.5
  174.3 2.1 collective-permute-start.16
  176.4 1.0 collective-permute-start.17
  177.5 1.9 copy-done.2
  179.4 25.8 %shard_map.59.h_ref = bf16[16,250,384]{2,1,0:T(8,128)(2,1)} custom-call(bf16[250,32,4000]{2,1,0:T(8,128)(2,1)} %bitcast.46, bf16[4000,384]{1,0:T(8,128)(2,1)S(1)} %copy-done.2, f32[10,32,1]{2,1,0:T(8,128)S(1)} %copy.13.scale_ref, f32[8,128]{1,0:T(8,128)S(1)} %broadcast_in_dim.11.tie_ref), custom_call_target="tpu_custom_call" | custom-call | flops 12288000000 | bytes 32000000 | tf_op jit(solution)/shard_map/pallas_call | solution.py:169
  205.2 6.0 %collective-permute-done.17 = bf16[384,384]{1,0:T(8,128)(2,1)S(1)} collective-permute-done((bf16[384,384]{1,0:T(8,128)(2,1)}, bf16[384,384]{1,0:T(8,128)(2,1)S(1)}, u32[]{:S(2)}, u32[]{:S(2)}) %collective-permute-start.17) | collective-permute-done | bytes 294944 | tf_op jit(solution)/shard_map/ppermute | solution.py:236
  211.2 1.1 fusion.2.rest_0_
  212.4 4.8 %collective-permute-start.20 = (bf16[384,384]{1,0:T(8,128)(2,1)S(1)}, bf16[384,384]{1,0:T(8,128)(2,1)S(1)}, u32[]{:S(2)}, u32[]{:S(2)}) collective-permute-start(bf16[384,384]{1,0:T(8,128)(2,1)S(1)} %fusion.2.rest_0_), channel_id=1, source_target_pairs={{0,8},{1,9},{2,10},{3,11},{4,12},{5,13},{6,14},{7,15},{8,0},{9,1},... | collective-permute-start | bytes 884744 | tf_op jit(solution)/shard_map/ppermute | solution.py:236
  217.2 1.9 collective-permute-start.21
  219.1 1.4 collective-permute-start.22
  221.3 8.6 %collective-permute-done.19.rest_1_ = bf16[384,384]{1,0:T(8,128)(2,1)S(1)} collective-permute-done((bf16[384,384]{1,0:T(8,128)(2,1)S(1)}, bf16[384,384]{1,0:T(8,128)(2,1)S(1)}, u32[]{:S(2)}, u32[]{:S(2)}) %collective-permute-start.19) | collective-permute-done | bytes 294944 | tf_op jit(solution)/shard_map/ppermute | solution.py:236
  229.9 2.3 collective-permute-start.23
  232.3 25.9 %collective-permute-done.20.rest_2_ = bf16[384,384]{1,0:T(8,128)(2,1)S(1)} collective-permute-done((bf16[384,384]{1,0:T(8,128)(2,1)S(1)}, bf16[384,384]{1,0:T(8,128)(2,1)S(1)}, u32[]{:S(2)}, u32[]{:S(2)}) %collective-permute-start.20) | collective-permute-done | bytes 294944 | tf_op jit(solution)/shard_map/ppermute | solution.py:236
  258.2 1.5 collective-permute-start.24
  262.9 2.1 collective-permute-done.24.rest_6_
  265.0 3.2 %collective-permute-done.25.rest_7_ = bf16[384,384]{1,0:T(8,128)(2,1)} collective-permute-done((bf16[384,384]{1,0:T(8,128)(2,1)}, bf16[384,384]{1,0:T(8,128)(2,1)}, u32[]{:S(2)}, u32[]{:S(2)}) %collective-permute-start.25) | collective-permute-done | bytes 294944 | tf_op jit(solution)/shard_map/ppermute | solution.py:233
  270.3 5.4 %shard_map.58 = f32[250,384]{1,0:T(8,128)} custom-call(f32[16]{0:T(128)S(1)} %get-tuple-element.110.gamma_ref, f32[250,384]{1,0:T(8,128)S(1)} %broadcast_in_dim.12.base_ref, bf16[16,250,384]{2,1,0:T(8,128)(2,1)S(1)} %copy-done, bf16[16,384,384]{2,1,0:T(8,128)(2,1)} %bitcast.47), custom_call_target="tpu_custom_call" | custom-call | flops 1179648000 | bytes 4718592 | tf_op jit(solution)/shard_map/pallas_call | solution.py:188
  276.2 1.0 copy-done.4
  277.1 1.0 copy-done.8
  278.1 1.0 copy-done.10
  279.1 3.4 %shard_map.60.base_ref = f32[250,384]{1,0:T(8,128)S(1)} custom-call(s32[8]{0:T(128)S(1)} %stack.71.owners_ref, f32[16]{0:T(128)S(1)} %get-tuple-element.109.gamma_ref, f32[250,384]{1,0:T(8,128)S(1)} %broadcast_in_dim.12.base_ref, bf16[16,250,384]{2,1,0:T(8,128)(2,1)} %shard_map.59.h_ref, bf16[384,384]{1,0:T(8,128)(2,1)S(1)} %copy-done.4, ...), custom_call_target="tpu_custom_call" | custom-call | flops 589824000 | bytes 2359296 | tf_op jit(solution)/shard_map/pallas_call | solution.py:206
  282.5 3.3 %shard_map.61 = f32[250,384]{1,0:T(8,128)S(1)} custom-call(s32[8]{0:T(128)S(1)} %stack.62.owners_ref, f32[16]{0:T(128)S(1)} %get-tuple-element.109.gamma_ref, f32[250,384]{1,0:T(8,128)S(1)} %shard_map.60.base_ref, bf16[16,250,384]{2,1,0:T(8,128)(2,1)} %shard_map.59.h_ref, bf16[384,384]{1,0:T(8,128)(2,1)S(1)} %copy-done.6, bf16[384,384]{1,0:T(8,128)(2,1)S(1)} %copy-done.12, ...), custom_call_target="tpu_custom_call" | custom-call | flops 589824000 | bytes 2359296 | tf_op jit(solution)/shard_map/pallas_call | solution.py:206
  285.9 1.8 collective-permute-start.34
  287.7 5.3 %collective-permute-done.34 = bf16[250,384]{1,0:T(8,128)(2,1)S(1)} collective-permute-done((bf16[250,384]{1,0:T(8,128)(2,1)S(1)}, bf16[250,384]{1,0:T(8,128)(2,1)S(1)}, u32[]{:S(2)}, u32[]{:S(2)}) %collective-permute-start.34) | collective-permute-done | bytes 192032 | tf_op jit(solution)/shard_map/ppermute | solution.py:352
  293.0 1.9 fusion.7
  (109 shorter events, 15.4 us)
Async XLA Ops:
  6.5 48.1 %all-gather.10.cloned.1.call-start = ((), (), s32[]{:S(2)}) async-start(), calls=%async_computation.1 | async-start | bytes 3342336 | tf_op jit(solution)/shard_map/all_gather | solution.py:252
  7.3 133.2 %all-gather.12.cloned.1.call-start = ((), (), s32[]{:S(2)}) async-start(), calls=%async_computation.2 | async-start | bytes 3342336 | tf_op jit(solution)/shard_map/all_gather | solution.py:253
  8.0 262.2 %all-gather.8.cloned.1.call-start = ((), (), s32[]{:S(2)}) async-start(), calls=%async_computation | async-start | bytes 5013504 | tf_op jit(solution)/shard_map/all_gather | solution.py:270
  82.8 2.9 collective-permute-start
  83.1 4.6 %collective-permute-start.1 = (bf16[4,384,384]{2,1,0:T(8,128)(2,1)}, bf16[4,384,384]{2,1,0:T(8,128)(2,1)S(1)}, u32[]{:S(2)}, u32[]{:S(2)}) collective-permute-start(bf16[4,384,384]{2,1,0:T(8,128)(2,1)} %get-tuple-element.62), channel_id=1, source_target_pairs={{0,1},{1,0},{2,3},{3,2},{4,5},{5,4},{6,7},{7,6},{8,9},{9,8},{10,11... | collective-permute-start | bytes 3538952 | tf_op jit(solution)/shard_map/ppermute | solution.py:233
  89.3 29.4 %collective-permute-start.8 = (bf16[4,384,384]{2,1,0:T(8,128)(2,1)S(1)}, bf16[4,384,384]{2,1,0:T(8,128)(2,1)S(1)}, u32[]{:S(2)}, u32[]{:S(2)}) collective-permute-start(bf16[4,384,384]{2,1,0:T(8,128)(2,1)S(1)} %add.211), channel_id=1, source_target_pairs={{0,2},{1,3},{2,0},{3,1},{4,6},{5,7},{6,4},{7,5},{8,10},{9,11},{10,... | collective-permute-start | bytes 3538952 | tf_op jit(solution)/shard_map/ppermute | solution.py:233
  119.7 8.9 %collective-permute-start.10 = (bf16[4,384,384]{2,1,0:T(8,128)(2,1)}, bf16[4,384,384]{2,1,0:T(8,128)(2,1)}, u32[]{:S(2)}, u32[]{:S(2)}) collective-permute-start(bf16[4,384,384]{2,1,0:T(8,128)(2,1)} %get-tuple-element.75), channel_id=1, source_target_pairs={{0,1},{1,0},{2,3},{3,2},{4,5},{5,4},{6,7},{7,6},{8,9},{9,8},{10,11... | collective-permute-start | bytes 3538952 | tf_op jit(solution)/shard_map/ppermute | solution.py:233
  119.7 8.9 %collective-permute-start.9 = (bf16[4,384,384]{2,1,0:T(8,128)(2,1)S(1)}, bf16[4,384,384]{2,1,0:T(8,128)(2,1)}, u32[]{:S(2)}, u32[]{:S(2)}) collective-permute-start(bf16[4,384,384]{2,1,0:T(8,128)(2,1)S(1)} %get-tuple-element.74), channel_id=1, source_target_pairs={{0,1},{1,0},{2,3},{3,2},{4,5},{5,4},{6,7},{7,6},{8,9},{9,8},{10,11... | collective-permute-start | bytes 3538952 | tf_op jit(solution)/shard_map/ppermute | solution.py:233
  120.6 3.6 %collective-permute-start.2 = (f32[32]{0:T(128)S(1)}, f32[32]{0:T(128)S(1)}, u32[]{:S(2)}, u32[]{:S(2)}) collective-permute-start(f32[32]{0:T(128)S(1)} %maximum_reduce_fusion), channel_id=1, source_target_pairs={{0,1},{1,0},{2,3},{3,2},{4,5},{5,4},{6,7},{7,6},{8,9},{9,8},{10,11... | collective-permute-start | bytes 392 | tf_op jit(solution)/shard_map/ppermute | solution.py:233
  120.6 3.6 %collective-permute-start.3 = (f32[32]{0:T(128)S(1)}, f32[32]{0:T(128)S(1)}, u32[]{:S(2)}, u32[]{:S(2)}) collective-permute-start(f32[32]{0:T(128)S(1)} %maximum_reduce_fusion), channel_id=1, source_target_pairs={{0,2},{1,3},{2,0},{3,1},{4,6},{5,7},{6,4},{7,5},{8,10},{9,11},{10,... | collective-permute-start | bytes 392 | tf_op jit(solution)/shard_map/ppermute | solution.py:233
  121.3 3.0 collective-permute-start.4
  124.3 14.1 %collective-permute-start.5 = (f32[32]{0:T(128)S(1)}, f32[32]{0:T(128)S(1)}, u32[]{:S(2)}, u32[]{:S(2)}) collective-permute-start(f32[32]{0:T(128)S(1)} %add_add_fusion.1), channel_id=1, source_target_pairs={{0,4},{1,5},{2,6},{3,7},{4,8},{5,9},{6,10},{7,11},{8,12},{9,13},{1... | collective-permute-start | bytes 392 | tf_op jit(solution)/shard_map/ppermute | solution.py:236
  126.1 12.5 %collective-permute-start.6 = (f32[32]{0:T(128)S(1)}, f32[32]{0:T(128)S(1)}, u32[]{:S(2)}, u32[]{:S(2)}) collective-permute-start(f32[32]{0:T(128)S(1)} %add_add_fusion.1), channel_id=1, source_target_pairs={{0,8},{1,9},{2,10},{3,11},{4,12},{5,13},{6,14},{7,15},{8,0},{9,1},... | collective-permute-start | bytes 392 | tf_op jit(solution)/shard_map/ppermute | solution.py:236
  127.4 40.0 %collective-permute-start.7 = (f32[32]{0:T(128)S(1)}, f32[32]{0:T(128)S(1)}, u32[]{:S(2)}, u32[]{:S(2)}) collective-permute-start(f32[32]{0:T(128)S(1)} %add_add_fusion.1), channel_id=1, source_target_pairs={{0,12},{1,13},{2,14},{3,15},{4,0},{5,1},{6,2},{7,3},{8,4},{9,5},{1... | collective-permute-start | bytes 392 | tf_op jit(solution)/shard_map/ppermute | solution.py:236
  130.5 5.7 %copy-start.15 = (bf16[4,384,384]{2,1,0:T(8,128)(2,1)}, bf16[4,384,384]{2,1,0:T(8,128)(2,1)S(1)}, u32[]{:S(2)}) copy-start(bf16[4,384,384]{2,1,0:T(8,128)(2,1)S(1)} %add.215) | copy-start | bytes 3538948
  130.5 3.0 %copy-start.17 = (bf16[4,384,384]{2,1,0:T(8,128)(2,1)S(1)}, bf16[4,384,384]{2,1,0:T(8,128)(2,1)}, u32[]{:S(2)}) copy-start(bf16[4,384,384]{2,1,0:T(8,128)(2,1)} %get-tuple-element.81) | copy-start | bytes 3538948
  130.6 36.9 %collective-permute-start.12 = (bf16[384,384]{1,0:T(8,128)(2,1)S(1)}, bf16[384,384]{1,0:T(8,128)(2,1)}, u32[]{:S(2)}, u32[]{:S(2)}) collective-permute-start(bf16[384,384]{1,0:T(8,128)(2,1)S(1)} %get-tuple-element.108), channel_id=1, source_target_pairs={{0,4},{1,5},{2,6},{3,7},{4,8},{5,9},{6,10},{7,11},{8,12},{9,13},{1... | collective-permute-start | bytes 884744 | tf_op jit(solution)/shard_map/ppermute | solution.py:236
  136.2 33.1 %collective-permute-start.11 = (bf16[4,384,384]{2,1,0:T(8,128)(2,1)}, bf16[4,384,384]{2,1,0:T(8,128)(2,1)}, u32[]{:S(2)}, u32[]{:S(2)}) collective-permute-start(bf16[4,384,384]{2,1,0:T(8,128)(2,1)} %add.226), channel_id=1, source_target_pairs={{0,2},{1,3},{2,0},{3,1},{4,6},{5,7},{6,4},{7,5},{8,10},{9,11},{10,... | collective-permute-start | bytes 3538952 | tf_op jit(solution)/shard_map/ppermute | solution.py:233
  138.5 29.1 %collective-permute-start.13 = (bf16[384,384]{1,0:T(8,128)(2,1)S(1)}, bf16[384,384]{1,0:T(8,128)(2,1)S(1)}, u32[]{:S(2)}, u32[]{:S(2)}) collective-permute-start(bf16[384,384]{1,0:T(8,128)(2,1)S(1)} %get-tuple-element.107), channel_id=1, source_target_pairs={{0,8},{1,9},{2,10},{3,11},{4,12},{5,13},{6,14},{7,15},{8,0},{9,1},... | collective-permute-start | bytes 884744 | tf_op jit(solution)/shard_map/ppermute | solution.py:236
  138.6 28.9 %collective-permute-start.14 = (bf16[384,384]{1,0:T(8,128)(2,1)S(1)}, bf16[384,384]{1,0:T(8,128)(2,1)S(1)}, u32[]{:S(2)}, u32[]{:S(2)}) collective-permute-start(bf16[384,384]{1,0:T(8,128)(2,1)S(1)} %get-tuple-element.106), channel_id=1, source_target_pairs={{0,12},{1,13},{2,14},{3,15},{4,0},{5,1},{6,2},{7,3},{8,4},{9,5},{1... | collective-permute-start | bytes 884744 | tf_op jit(solution)/shard_map/ppermute | solution.py:236
  167.5 3.4 %copy-start.1 = (bf16[4000,384]{1,0:T(8,128)(2,1)}, bf16[4000,384]{1,0:T(8,128)(2,1)S(1)}, u32[]{:S(2)}) copy-start(bf16[4000,384]{1,0:T(8,128)(2,1)S(1)} %get-tuple-element.95.m_ref) | copy-start | bytes 9216004
  170.9 3.4 %copy-start.16 = (bf16[4,384,384]{2,1,0:T(8,128)(2,1)}, bf16[4,384,384]{2,1,0:T(8,128)(2,1)S(1)}, u32[]{:S(2)}) copy-start(bf16[4,384,384]{2,1,0:T(8,128)(2,1)S(1)} %add.232) | copy-start | bytes 3538948
  170.9 1.5 copy-start.22
  174.3 30.9 %collective-permute-start.16 = (bf16[384,384]{1,0:T(8,128)(2,1)}, bf16[384,384]{1,0:T(8,128)(2,1)S(1)}, u32[]{:S(2)}, u32[]{:S(2)}) collective-permute-start(bf16[384,384]{1,0:T(8,128)(2,1)} %get-tuple-element.105), channel_id=1, source_target_pairs={{0,4},{1,5},{2,6},{3,7},{4,8},{5,9},{6,10},{7,11},{8,12},{9,13},{1... | collective-permute-start | bytes 884744 | tf_op jit(solution)/shard_map/ppermute | solution.py:236
  176.4 34.8 %collective-permute-start.17 = (bf16[384,384]{1,0:T(8,128)(2,1)}, bf16[384,384]{1,0:T(8,128)(2,1)S(1)}, u32[]{:S(2)}, u32[]{:S(2)}) collective-permute-start(bf16[384,384]{1,0:T(8,128)(2,1)} %get-tuple-element.104), channel_id=1, source_target_pairs={{0,8},{1,9},{2,10},{3,11},{4,12},{5,13},{6,14},{7,15},{8,0},{9,1},... | collective-permute-start | bytes 884744 | tf_op jit(solution)/shard_map/ppermute | solution.py:236
  177.5 33.7 %collective-permute-start.18 = (bf16[384,384]{1,0:T(8,128)(2,1)}, bf16[384,384]{1,0:T(8,128)(2,1)S(1)}, u32[]{:S(2)}, u32[]{:S(2)}) collective-permute-start(bf16[384,384]{1,0:T(8,128)(2,1)} %get-tuple-element.103), channel_id=1, source_target_pairs={{0,12},{1,13},{2,14},{3,15},{4,0},{5,1},{6,2},{7,3},{8,4},{9,5},{1... | collective-permute-start | bytes 884744 | tf_op jit(solution)/shard_map/ppermute | solution.py:236
  177.5 1.9 copy-start.2
  179.4 90.9 %copy-start = (bf16[16,250,384]{2,1,0:T(8,128)(2,1)S(1)}, bf16[16,250,384]{2,1,0:T(8,128)(2,1)}, u32[]{:S(2)}) copy-start(bf16[16,250,384]{2,1,0:T(8,128)(2,1)} %get-tuple-element.84.h_ref) | copy-start | bytes 9216004
  212.3 17.6 %collective-permute-start.19 = (bf16[384,384]{1,0:T(8,128)(2,1)S(1)}, bf16[384,384]{1,0:T(8,128)(2,1)S(1)}, u32[]{:S(2)}, u32[]{:S(2)}) collective-permute-start(bf16[384,384]{1,0:T(8,128)(2,1)S(1)} %fusion.2.rest_0_), channel_id=1, source_target_pairs={{0,4},{1,5},{2,6},{3,7},{4,8},{5,9},{6,10},{7,11},{8,12},{9,13},{1... | collective-permute-start | bytes 884744 | tf_op jit(solution)/shard_map/ppermute | solution.py:236
  212.4 45.8 %collective-permute-start.20 = (bf16[384,384]{1,0:T(8,128)(2,1)S(1)}, bf16[384,384]{1,0:T(8,128)(2,1)S(1)}, u32[]{:S(2)}, u32[]{:S(2)}) collective-permute-start(bf16[384,384]{1,0:T(8,128)(2,1)S(1)} %fusion.2.rest_0_), channel_id=1, source_target_pairs={{0,8},{1,9},{2,10},{3,11},{4,12},{5,13},{6,14},{7,15},{8,0},{9,1},... | collective-permute-start | bytes 884744 | tf_op jit(solution)/shard_map/ppermute | solution.py:236
  217.2 42.5 %collective-permute-start.21 = (bf16[384,384]{1,0:T(8,128)(2,1)S(1)}, bf16[384,384]{1,0:T(8,128)(2,1)}, u32[]{:S(2)}, u32[]{:S(2)}) collective-permute-start(bf16[384,384]{1,0:T(8,128)(2,1)S(1)} %fusion.2.rest_0_), channel_id=1, source_target_pairs={{0,12},{1,13},{2,14},{3,15},{4,0},{5,1},{6,2},{7,3},{8,4},{9,5},{1... | collective-permute-start | bytes 884744 | tf_op jit(solution)/shard_map/ppermute | solution.py:236
  219.1 41.1 %collective-permute-start.22 = (bf16[384,384]{1,0:T(8,128)(2,1)S(1)}, bf16[384,384]{1,0:T(8,128)(2,1)}, u32[]{:S(2)}, u32[]{:S(2)}) collective-permute-start(bf16[384,384]{1,0:T(8,128)(2,1)S(1)} %fusion.2.rest_0_), channel_id=1, source_target_pairs={{0,2},{1,3},{2,0},{3,1},{4,6},{5,7},{6,4},{7,5},{8,10},{9,11},{10,... | collective-permute-start | bytes 884744 | tf_op jit(solution)/shard_map/ppermute | solution.py:233
  220.6 40.4 %collective-permute-start.26 = (bf16[384,384]{1,0:T(8,128)(2,1)S(1)}, bf16[384,384]{1,0:T(8,128)(2,1)S(1)}, u32[]{:S(2)}, u32[]{:S(2)}) collective-permute-start(bf16[384,384]{1,0:T(8,128)(2,1)S(1)} %fusion.2.rest_0_), channel_id=1, source_target_pairs={{0,1},{1,0},{2,3},{3,2},{4,5},{5,4},{6,7},{7,6},{8,9},{9,8},{10,11... | collective-permute-start | bytes 884744 | tf_op jit(solution)/shard_map/ppermute | solution.py:233
  229.9 33.0 %collective-permute-start.23 = (bf16[384,384]{1,0:T(8,128)(2,1)S(1)}, bf16[384,384]{1,0:T(8,128)(2,1)}, u32[]{:S(2)}, u32[]{:S(2)}) collective-permute-start(bf16[384,384]{1,0:T(8,128)(2,1)S(1)} %collective-permute-done.19.rest_1_), channel_id=1, source_target_pairs={{0,2},{1,3},{2,0},{3,1},{4,6},{5,7},{6,4},{7,5},{8,10},{9,11},{10,... | collective-permute-start | bytes 884744 | tf_op jit(solution)/shard_map/ppermute | solution.py:233
  258.2 6.8 %collective-permute-start.24 = (bf16[384,384]{1,0:T(8,128)(2,1)S(1)}, bf16[384,384]{1,0:T(8,128)(2,1)}, u32[]{:S(2)}, u32[]{:S(2)}) collective-permute-start(bf16[384,384]{1,0:T(8,128)(2,1)S(1)} %collective-permute-done.20.rest_2_), channel_id=1, source_target_pairs={{0,2},{1,3},{2,0},{3,1},{4,6},{5,7},{6,4},{7,5},{8,10},{9,11},{10,... | collective-permute-start | bytes 884744 | tf_op jit(solution)/shard_map/ppermute | solution.py:233
  259.7 8.5 %collective-permute-start.25 = (bf16[384,384]{1,0:T(8,128)(2,1)}, bf16[384,384]{1,0:T(8,128)(2,1)}, u32[]{:S(2)}, u32[]{:S(2)}) collective-permute-start(bf16[384,384]{1,0:T(8,128)(2,1)} %collective-permute-done.21.rest_3_), channel_id=1, source_target_pairs={{0,2},{1,3},{2,0},{3,1},{4,6},{5,7},{6,4},{7,5},{8,10},{9,11},{10,... | collective-permute-start | bytes 884744 | tf_op jit(solution)/shard_map/ppermute | solution.py:233
  260.2 8.0 %collective-permute-start.27 = (bf16[384,384]{1,0:T(8,128)(2,1)S(1)}, bf16[384,384]{1,0:T(8,128)(2,1)S(1)}, u32[]{:S(2)}, u32[]{:S(2)}) collective-permute-start(bf16[384,384]{1,0:T(8,128)(2,1)S(1)} %collective-permute-done.19.rest_1_), channel_id=1, source_target_pairs={{0,1},{1,0},{2,3},{3,2},{4,5},{5,4},{6,7},{7,6},{8,9},{9,8},{10,11... | collective-permute-start | bytes 884744 | tf_op jit(solution)/shard_map/ppermute | solution.py:233
  261.7 7.8 %collective-permute-start.28 = (bf16[384,384]{1,0:T(8,128)(2,1)S(1)}, bf16[384,384]{1,0:T(8,128)(2,1)S(1)}, u32[]{:S(2)}, u32[]{:S(2)}) collective-permute-start(bf16[384,384]{1,0:T(8,128)(2,1)S(1)} %collective-permute-done.20.rest_2_), channel_id=1, source_target_pairs={{0,1},{1,0},{2,3},{3,2},{4,5},{5,4},{6,7},{7,6},{8,9},{9,8},{10,11... | collective-permute-start | bytes 884744 | tf_op jit(solution)/shard_map/ppermute | solution.py:233
  262.9 12.7 %collective-permute-start.29 = (bf16[384,384]{1,0:T(8,128)(2,1)}, bf16[384,384]{1,0:T(8,128)(2,1)}, u32[]{:S(2)}, u32[]{:S(2)}) collective-permute-start(bf16[384,384]{1,0:T(8,128)(2,1)} %collective-permute-done.21.rest_3_), channel_id=1, source_target_pairs={{0,1},{1,0},{2,3},{3,2},{4,5},{5,4},{6,7},{7,6},{8,9},{9,8},{10,11... | collective-permute-start | bytes 884744 | tf_op jit(solution)/shard_map/ppermute | solution.py:233
  265.0 17.4 %collective-permute-start.30 = (bf16[384,384]{1,0:T(8,128)(2,1)}, bf16[384,384]{1,0:T(8,128)(2,1)}, u32[]{:S(2)}, u32[]{:S(2)}) collective-permute-start(bf16[384,384]{1,0:T(8,128)(2,1)} %collective-permute-done.22.rest_4_), channel_id=1, source_target_pairs={{0,1},{1,0},{2,3},{3,2},{4,5},{5,4},{6,7},{7,6},{8,9},{9,8},{10,11... | collective-permute-start | bytes 884744 | tf_op jit(solution)/shard_map/ppermute | solution.py:233
  268.2 14.3 %collective-permute-start.31 = (bf16[384,384]{1,0:T(8,128)(2,1)}, bf16[384,384]{1,0:T(8,128)(2,1)}, u32[]{:S(2)}, u32[]{:S(2)}) collective-permute-start(bf16[384,384]{1,0:T(8,128)(2,1)} %collective-permute-done.23.rest_5_), channel_id=1, source_target_pairs={{0,1},{1,0},{2,3},{3,2},{4,5},{5,4},{6,7},{7,6},{8,9},{9,8},{10,11... | collective-permute-start | bytes 884744 | tf_op jit(solution)/shard_map/ppermute | solution.py:233
  268.9 13.6 %collective-permute-start.32 = (bf16[384,384]{1,0:T(8,128)(2,1)}, bf16[384,384]{1,0:T(8,128)(2,1)}, u32[]{:S(2)}, u32[]{:S(2)}) collective-permute-start(bf16[384,384]{1,0:T(8,128)(2,1)} %collective-permute-done.24.rest_6_), channel_id=1, source_target_pairs={{0,1},{1,0},{2,3},{3,2},{4,5},{5,4},{6,7},{7,6},{8,9},{9,8},{10,11... | collective-permute-start | bytes 884744 | tf_op jit(solution)/shard_map/ppermute | solution.py:233
  270.1 12.4 %collective-permute-start.33 = (bf16[384,384]{1,0:T(8,128)(2,1)}, bf16[384,384]{1,0:T(8,128)(2,1)}, u32[]{:S(2)}, u32[]{:S(2)}) collective-permute-start(bf16[384,384]{1,0:T(8,128)(2,1)} %collective-permute-done.25.rest_7_), channel_id=1, source_target_pairs={{0,1},{1,0},{2,3},{3,2},{4,5},{5,4},{6,7},{7,6},{8,9},{9,8},{10,11... | collective-permute-start | bytes 884744 | tf_op jit(solution)/shard_map/ppermute | solution.py:233
  275.7 17.4 %collective-permute-start.15 = (f32[250,384]{1,0:T(8,128)}, f32[250,384]{1,0:T(8,128)S(1)}, u32[]{:S(2)}, u32[]{:S(2)}) collective-permute-start(f32[250,384]{1,0:T(8,128)} %shard_map.58), channel_id=1, source_target_pairs={{0,16},{16,0},{1,17},{17,1},{2,18},{18,2},{3,19},{19,3},{4,20},{20... | collective-permute-start | bytes 1152008 | tf_op jit(solution)/shard_map/ppermute | solution.py:326
  279.0 3.5 %copy-start.6 = (bf16[384,384]{1,0:T(8,128)(2,1)S(1)}, bf16[384,384]{1,0:T(8,128)(2,1)}, u32[]{:S(2)}) copy-start(bf16[384,384]{1,0:T(8,128)(2,1)} %copy-done.5) | copy-start | bytes 884740
  279.0 3.5 %copy-start.12 = (bf16[384,384]{1,0:T(8,128)(2,1)S(1)}, bf16[384,384]{1,0:T(8,128)(2,1)}, u32[]{:S(2)}) copy-start(bf16[384,384]{1,0:T(8,128)(2,1)} %copy-done.11) | copy-start | bytes 884740
  279.1 3.5 %copy-start.14 = (bf16[384,384]{1,0:T(8,128)(2,1)S(1)}, bf16[384,384]{1,0:T(8,128)(2,1)}, u32[]{:S(2)}) copy-start(bf16[384,384]{1,0:T(8,128)(2,1)} %copy-done.13) | copy-start | bytes 884740
  285.9 7.1 %collective-permute-start.34 = (bf16[250,384]{1,0:T(8,128)(2,1)S(1)}, bf16[250,384]{1,0:T(8,128)(2,1)S(1)}, u32[]{:S(2)}, u32[]{:S(2)}) collective-permute-start(bf16[250,384]{1,0:T(8,128)(2,1)S(1)} %convert_element_type.65), channel_id=1, source_target_pairs={{0,16},{16,0},{1,17},{17,1},{2,18},{18,2},{3,19},{19,3},{4,20},{20... | collective-permute-start | bytes 576008 | tf_op jit(solution)/shard_map/ppermute | solution.py:352
  (13 other events, 11.2 us)
Sparse Core Ops, SparseCore 0:
  9.6 44.9 all-gather.9
  56.9 43.9 all-gather.11
  174.5 83.5 all-gather.7

commit v6 on v4

--- a/solution.py
+++ b/solution.py
@@ -235,6 +235,29 @@
     def turn_z(value, by):
         return lax.ppermute(value, "ao", [(i, (i + by * fan) % groups) for i in range(groups)])
 
+    def along_z(value, pairs):
+        return lax.ppermute(
+            value, "ao", [(a * fan + i, b * fan + i) for a, b in pairs for i in range(fan)]
+        )
+
+    def line_z(mine):
+        if nz != 4:
+            return [mine] + [turn_z(mine, d) for d in range(1, nz)]
+        up = along_z(mine, [(0, 1), (1, 2), (2, 3)])
+        down = along_z(mine, [(3, 2), (2, 1), (1, 0)])
+        near, up, down = lax.optimization_barrier((jnp.where(z < 2, down, up), up, down))
+        up2 = along_z(up, [(1, 2), (2, 3)])
+        down2 = along_z(down, [(2, 1), (1, 0)])
+        far = jnp.where(z < 2, down2, up2)
+        last = along_z(far, [(2, 3), (1, 0)])
+        other = jnp.where(z == 1, up, jnp.where(z == 2, down, last))
+        return [mine, near, far, other]
+
+    if nz == 4:
+        from_z = [z, jnp.where(z < 2, z + 1, z - 1), z ^ 2, jnp.where(z % 2 == 0, 3, 0)]
+    else:
+        from_z = [(z - d) % nz for d in range(nz)]
+
     def pick(value, k):
         return lax.dynamic_index_in_dim(value, k % nz, 0, keepdims=False)
 
@@ -270,7 +293,7 @@
             whole = lax.all_gather(total, "ao", axis=0, tiled=True)
             yield whole.reshape(paux, width, width), total
             return
-        shards = [[total] + [turn_z(total, d) for d in range(1, nz)]]
+        shards = [line_z(total)]
         for bit in reversed(bits):
             shards = shards + [[swap(v, bit) for v in column] for column in shards]
         yield shards, total
@@ -336,7 +359,7 @@
             order = order + [d ^ bit for d in order]
         for lo in range(0, fan, fan // ncore):
             some = range(lo, lo + fan // ncore)
-            owners = [(z - k) % nz * fan + (index % fan ^ order[d]) for d in some for k in range(nz)]
+            owners = [k * fan + (index % fan ^ order[d]) for d in some for k in from_z]
             sigma = sigma_shards(
                 jnp.stack(owners).astype(jnp.int32), g, sigma, occ[c], [v for d in some for v in shards[d]]
             )

time: 301 us -> 308 us (1.023); the launches traced: 300 us -> 303 us
  other arithmetic: 14.8 us -> 21.2 us
  starting transfers between devices: 32.9 us -> 28.3 us
    ppermute x0 -> x5, waiting for transfers between devices: none -> 35.9 us  [along_z(): lax.ppermute(value, 'ao', [(a * fan + i, b * fan + i) for a, b in pairs f...]
    ppermute x12 -> x9, waiting for transfers between devices: 40.9 us -> 7.76 us  [turn_z(): lax.ppermute(value, 'ao', [(i, (i + by * fan) % groups) for i in range(gr...]
    ppermute x12 -> x9, starting transfers between devices: 20.6 us -> 11 us  [turn_z(): lax.ppermute(value, 'ao', [(i, (i + by * fan) % groups) for i in range(gr...]
    ppermute x0 -> x5, starting transfers between devices: none -> 6.27 us  [along_z(): lax.ppermute(value, 'ao', [(a * fan + i, b * fan + i) for a, b in pairs f...]
    select_n x0 -> x3, other arithmetic: none -> 3.66 us  [the longest x1 1.72 us: line_z(): other = jnp.where(z == 1, up, jnp.where(z == 2, down, last))]
    unnamed x23 -> x13, local copies, waits for them, and re-layouts: 4.9 us -> 1.79 us
  transfers between devices with their start and end apart: 37 -> 39, of which waited for: 11 -> 13; matrix products, arithmetic and copies ran while one was open for 5% -> 7% of each run, Pallas kernels for 39% -> 38%
where the time goes in v6:
time: 308 us; the launch traced here: 303 us
  Pallas kernels  120 us (39%)
  waiting for transfers between devices  116 us (38%)
  starting transfers between devices  28.3 us (9%)
  other arithmetic  21.2 us (7%)
  between operations  13.4 us (4%)
  local copies, waits for them, and re-layouts  4.18 us (1%)
    pallas_call x2, Pallas kernels, rot_part(): pl.pallas_call(functools.partial(rot_kernel, paux, fan, nz, cuts), grid_s...  55 us
    pallas_call x2, Pallas kernels, occ_part(): pl.pallas_call(functools.partial(occ_kernel, paux), grid=(nscale,), in_sp...  53 us
    all_gather x1, waiting for transfers between devices, body(): whole_r = lax.all_gather(rot_coeff, 'ao', axis=0)  43.6 us
    ppermute x5, waiting for transfers between devices, along_z(): lax.ppermute(value, 'ao', [(a * fan + i, b * fan + i) for a, b in pairs f...  35.9 us
    ppermute x21, waiting for transfers between devices, swap(): return lax.ppermute(value, 'ao', [(i, i ^ bit) for i in range(groups)])  16.4 us
    add x6, other arithmetic, reduce_steps(): live = {d: v + sent[d | bit] for d, v in live.items() if not d & bit}  13.2 us
    ppermute x1, waiting for transfers between devices, body(): lax.ppermute(sigma, 'aux', [(i, i ^ bit) for i in range(parts)])  11.1 us
    ppermute x9, starting transfers between devices, turn_z(): lax.ppermute(value, 'ao', [(i, (i + by * fan) % groups) for i in range(gr...  11 us
  transfers between devices with their start and end apart: 39, of which 13 were waited for; matrix products, arithmetic and copies ran while one was open for 7% of the time, Pallas kernels for 38%

profile of v6, /device:TPU:28, one launch (start us, length us, event | category | flops | bytes accessed | tf_op | source)
XLA Modules:
  0.0 303.0 jit_solution(5389072353791278617)
XLA Ops:
  8.1 1.1 copy.12
  9.1 0.8 copy.13.scale_ref
  10.0 1.0 convert_multiply_fusion
  11.0 43.6 %all-gather.10.cloned.1.call-done.m_ref = bf16[16,250,380]{2,1,0:T(8,128)(2,1)} async-done(((bf16[1,250,380]{2,1,0:T(8,128)(2,1)}), bf16[16,250,380]{2,1,0:T(8,128)(2,1)}) %all-gather.10.cloned.1.call-update) | async-done | bytes 3040016 | tf_op jit(solution)/shard_map/all_gather | solution.py:275
  54.6 28.2 %shard_map.55 = (bf16[4,384,384]{2,1,0:T(8,128)(2,1)S(1)}, bf16[4,384,384]{2,1,0:T(8,128)(2,1)S(1)}, bf16[4,384,384]{2,1,0:T(8,128)(2,1)}, bf16[4,384,384]{2,1,0...) custom-call(s32[1]{0:T(128)} %bitcast.8.me_ref, bf16[250,32,4000]{2,1,0:T(8,128)(2,1)} %bitcast.43, ...), custom_call_target="tpu_custom_call" | custom-call | flops 12288000000 | bytes 32000000 | tf_op jit(solution)/shard_map/pallas_call | solution.py:144
  83.4 2.4 collective-permute-done
  85.7 1.9 collective-permute-done.1
  87.6 2.6 add.195
  90.3 1.4 collective-permute-start.5
  91.7 1.3 add.194
  93.0 26.8 %shard_map.56 = (bf16[4,384,384]{2,1,0:T(8,128)(2,1)S(1)}, bf16[4,384,384]{2,1,0:T(8,128)(2,1)S(1)}, bf16[4,384,384]{2,1,0:T(8,128)(2,1)}, bf16[4,384,384]{2,1,0:T(8,128)(2,1)}, f32[16,1,384]{2,1,0:T(1,128)S(1)}) custom-call(s32[1]{0:T(128)} %bitcast.8.me_ref, bf16[250,32,4000]{2,1,0:T(8,128)(2,1)} %bitcast.44, bf16[4000,384]{1,0:T(8,128)(2,1)} %get-tuple-element.43.m_ref, ...), custom_call_target="tpu_custom_call" | custom-call | flops 12288000000 | bytes 32000000 | tf_op jit(solution)/shard_map/pallas_call | solution.py:144
  121.4 1.2 collective-permute-start.4
  122.6 1.9 collective-permute-done.6
  124.7 1.9 add.196
  126.6 1.1 dynamic-slice_bitcast_fusion.3
  127.7 0.9 collective-permute-start.11
  128.6 1.2 collective-permute-start.12
  129.8 2.8 add.205
  132.6 2.6 add.206
  135.2 1.2 collective-permute-start.13
  136.4 1.4 collective-permute-start.14
  137.8 27.2 %shard_map.57 = (bf16[16,250,384]{2,1,0:T(8,128)(2,1)}, bf16[4000,384]{1,0:T(8,128)(2,1)S(1)}) custom-call(bf16[250,32,4000]{2,1,0:T(8,128)(2,1)} %bitcast.45, bf16[16,250,380]{2,1,0:T(8,128)(2,1)} %all-gather.12.cloned.1.call-done.m_ref, f32[10,32,1]{2,1,0:T(8,128)S(1)} %copy.13.scale_ref, f32[8,128]{1,0:T(8,128)S(1)} %broadcast_in_dim.11.tie_ref), custom_call_target="tpu_custom_call" | custom-call | flops 12288000000 | bytes 32000000 | tf_op jit(solution)/shard_map/pallas_call | solution.py:169
  165.1 2.1 fusion.5
  167.2 2.7 collective-permute-start.8
  170.6 1.9 add.215
  172.6 3.3 %collective-permute-start.15 = (bf16[384,384]{1,0:T(8,128)(2,1)S(1)}, bf16[384,384]{1,0:T(8,128)(2,1)S(1)}, u32[]{:S(2)}, u32[]{:S(2)}) collective-permute-start(bf16[384,384]{1,0:T(8,128)(2,1)S(1)} %get-tuple-element.81), channel_id=1, source_target_pairs={{0,4},{1,5},{2,6},{3,7},{4,8},{5,9},{6,10},{7,11},{8,12},{9,13},{1... | collective-permute-start | bytes 884744 | tf_op jit(solution)/shard_map/ppermute | solution.py:236
  175.9 1.1 collective-permute-start.16
  177.0 25.7 %shard_map.58.h_ref = bf16[16,250,384]{2,1,0:T(8,128)(2,1)} custom-call(bf16[250,32,4000]{2,1,0:T(8,128)(2,1)} %bitcast.46, bf16[4000,384]{1,0:T(8,128)(2,1)S(1)} %get-tuple-element.64.m_ref, f32[10,32,1]{2,1,0:T(8,128)S(1)} %copy.13.scale_ref, f32[8,128]{1,0:T(8,128)S(1)} %broadcast_in_dim.11.tie_ref), custom_call_target="tpu_custom_call" | custom-call | flops 12288000000 | bytes 32000000 | tf_op jit(solution)/shard_map/pallas_call | solution.py:169
  202.8 7.7 %collective-permute-done.16 = bf16[384,384]{1,0:T(8,128)(2,1)S(1)} collective-permute-done((bf16[384,384]{1,0:T(8,128)(2,1)S(1)}, bf16[384,384]{1,0:T(8,128)(2,1)S(1)}, u32[]{:S(2)}, u32[]{:S(2)}) %collective-permute-start.16) | collective-permute-done | bytes 294944 | tf_op jit(solution)/shard_map/ppermute | solution.py:236
  210.7 1.5 collective-permute-start.18
  212.2 1.5 collective-permute-start.19
  213.7 11.5 %collective-permute-done.18 = bf16[384,384]{1,0:T(8,128)(2,1)S(1)} collective-permute-done((bf16[384,384]{1,0:T(8,128)(2,1)S(1)}, bf16[384,384]{1,0:T(8,128)(2,1)S(1)}, u32[]{:S(2)}, u32[]{:S(2)}) %collective-permute-start.18) | collective-permute-done | bytes 294944 | tf_op jit(solution)/shard_map/ppermute | solution.py:239
  225.9 10.5 %collective-permute-done.19 = bf16[384,384]{1,0:T(8,128)(2,1)} collective-permute-done((bf16[384,384]{1,0:T(8,128)(2,1)S(1)}, bf16[384,384]{1,0:T(8,128)(2,1)}, u32[]{:S(2)}, u32[]{:S(2)}) %collective-permute-start.19) | collective-permute-done | bytes 294944 | tf_op jit(solution)/shard_map/ppermute | solution.py:239
  236.4 1.2 broadcast_select_fusion.1.rest_1_
  238.3 1.3 collective-permute-start.21
  240.1 7.8 %collective-permute-done.21 = bf16[384,384]{1,0:T(8,128)(2,1)S(1)} collective-permute-done((bf16[384,384]{1,0:T(8,128)(2,1)}, bf16[384,384]{1,0:T(8,128)(2,1)S(1)}, u32[]{:S(2)}, u32[]{:S(2)}) %collective-permute-start.21) | collective-permute-done | bytes 294944 | tf_op jit(solution)/shard_map/ppermute | solution.py:239
  248.7 1.3 collective-permute-start.22
  250.1 0.9 collective-permute-start.24
  251.5 6.1 %collective-permute-done.22 = bf16[384,384]{1,0:T(8,128)(2,1)} collective-permute-done((bf16[384,384]{1,0:T(8,128)(2,1)}, bf16[384,384]{1,0:T(8,128)(2,1)}, u32[]{:S(2)}, u32[]{:S(2)}) %collective-permute-start.22) | collective-permute-done | bytes 294944 | tf_op jit(solution)/shard_map/ppermute | solution.py:239
  257.6 1.3 collective-permute-start.25
  258.9 1.7 select_select_fusion.rest_3_
  262.2 5.7 %collective-permute-done.25.rest_6_ = bf16[384,384]{1,0:T(8,128)(2,1)} collective-permute-done((bf16[384,384]{1,0:T(8,128)(2,1)}, bf16[384,384]{1,0:T(8,128)(2,1)}, u32[]{:S(2)}, u32[]{:S(2)}) %collective-permute-start.25) | collective-permute-done | bytes 294944 | tf_op jit(solution)/shard_map/ppermute | solution.py:233
  267.9 4.3 %collective-permute-done.26.rest_7_ = bf16[384,384]{1,0:T(8,128)(2,1)} collective-permute-done((bf16[384,384]{1,0:T(8,128)(2,1)}, bf16[384,384]{1,0:T(8,128)(2,1)}, u32[]{:S(2)}, u32[]{:S(2)}) %collective-permute-start.26) | collective-permute-done | bytes 294944 | tf_op jit(solution)/shard_map/ppermute | solution.py:233
  272.4 4.6 %shard_map.59.base_ref = f32[250,384]{1,0:T(8,128)S(1)} custom-call(f32[16]{0:T(128)S(1)} %get-tuple-element.85.gamma_ref, f32[250,384]{1,0:T(8,128)S(1)} %broadcast_in_dim.12.base_ref, bf16[16,250,384]{2,1,0:T(8,128)(2,1)S(1)} %copy-done, bf16[16,384,384]{2,1,0:T(8,128)(2,1)} %bitcast.47), custom_call_target="tpu_custom_call" | custom-call | flops 1179648000 | bytes 4718592 | tf_op jit(solution)/shard_map/pallas_call | solution.py:188
  277.0 3.4 %shard_map.60.base_ref = f32[250,384]{1,0:T(8,128)S(1)} custom-call(s32[8]{0:T(128)S(1)} %stack.71.owners_ref, f32[16]{0:T(128)S(1)} %get-tuple-element.86.gamma_ref, f32[250,384]{1,0:T(8,128)S(1)} %shard_map.59.base_ref, bf16[16,250,384]{2,1,0:T(8,128)(2,1)} %shard_map.58.h_ref, bf16[384,384]{1,0:T(8,128)(2,1)S(1)} %copy-done.2, ...), custom_call_target="tpu_custom_call" | custom-call | flops 589824000 | bytes 2359296 | tf_op jit(solution)/shard_map/pallas_call | solution.py:206
  280.5 3.6 %shard_map.61 = f32[250,384]{1,0:T(8,128)S(1)} custom-call(s32[8]{0:T(128)S(1)} %stack.62.owners_ref, f32[16]{0:T(128)S(1)} %get-tuple-element.86.gamma_ref, f32[250,384]{1,0:T(8,128)S(1)} %shard_map.60.base_ref, bf16[16,250,384]{2,1,0:T(8,128)(2,1)} %shard_map.58.h_ref, bf16[384,384]{1,0:T(8,128)(2,1)} %collective-permute-done.27.rest_0_, ...), custom_call_target="tpu_custom_call" | custom-call | flops 589824000 | bytes 2359296 | tf_op jit(solution)/shard_map/pallas_call | solution.py:206
  284.5 11.1 %collective-permute-done.35 = f32[250,384]{1,0:T(8,128)S(1)} collective-permute-done((f32[250,384]{1,0:T(8,128)S(1)}, f32[250,384]{1,0:T(8,128)S(1)}, u32[]{:S(2)}, u32[]{:S(2)}) %collective-permute-start.35) | collective-permute-done | bytes 384032 | tf_op jit(solution)/shard_map/ppermute | solution.py:368
  295.7 0.8 fusion.6
  (79 shorter events, 10.4 us)
Async XLA Ops:
  6.5 48.1 %all-gather.10.cloned.1.call-start = ((), (), s32[]{:S(2)}) async-start(), calls=%async_computation.1 | async-start | bytes 3342336 | tf_op jit(solution)/shard_map/all_gather | solution.py:275
  7.3 130.6 %all-gather.12.cloned.1.call-start = ((), (), s32[]{:S(2)}) async-start(), calls=%async_computation.2 | async-start | bytes 3342336 | tf_op jit(solution)/shard_map/all_gather | solution.py:276
  8.0 264.3 %all-gather.8.cloned.1.call-start = ((), (), s32[]{:S(2)}) async-start(), calls=%async_computation | async-start | bytes 5013504 | tf_op jit(solution)/shard_map/all_gather | solution.py:293
  82.8 2.9 collective-permute-start
  83.1 4.6 %collective-permute-start.1 = (bf16[4,384,384]{2,1,0:T(8,128)(2,1)}, bf16[4,384,384]{2,1,0:T(8,128)(2,1)S(1)}, u32[]{:S(2)}, u32[]{:S(2)}) collective-permute-start(bf16[4,384,384]{2,1,0:T(8,128)(2,1)} %get-tuple-element.46), channel_id=1, source_target_pairs={{0,1},{1,0},{2,3},{3,2},{4,5},{5,4},{6,7},{7,6},{8,9},{9,8},{10,11... | collective-permute-start | bytes 3538952 | tf_op jit(solution)/shard_map/ppermute | solution.py:233
  90.3 31.1 %collective-permute-start.5 = (bf16[4,384,384]{2,1,0:T(8,128)(2,1)}, bf16[4,384,384]{2,1,0:T(8,128)(2,1)}, u32[]{:S(2)}, u32[]{:S(2)}) collective-permute-start(bf16[4,384,384]{2,1,0:T(8,128)(2,1)} %add.195), channel_id=1, source_target_pairs={{0,2},{1,3},{2,0},{3,1},{4,6},{5,7},{6,4},{7,5},{8,10},{9,11},{10,... | collective-permute-start | bytes 3538952 | tf_op jit(solution)/shard_map/ppermute | solution.py:233
  119.8 4.6 %collective-permute-start.6 = (bf16[4,384,384]{2,1,0:T(8,128)(2,1)S(1)}, bf16[4,384,384]{2,1,0:T(8,128)(2,1)}, u32[]{:S(2)}, u32[]{:S(2)}) collective-permute-start(bf16[4,384,384]{2,1,0:T(8,128)(2,1)S(1)} %get-tuple-element.52), channel_id=1, source_target_pairs={{0,1},{1,0},{2,3},{3,2},{4,5},{5,4},{6,7},{7,6},{8,9},{9,8},{10,11... | collective-permute-start | bytes 3538952 | tf_op jit(solution)/shard_map/ppermute | solution.py:233
  119.8 4.9 %collective-permute-start.7 = (bf16[4,384,384]{2,1,0:T(8,128)(2,1)}, bf16[4,384,384]{2,1,0:T(8,128)(2,1)}, u32[]{:S(2)}, u32[]{:S(2)}) collective-permute-start(bf16[4,384,384]{2,1,0:T(8,128)(2,1)} %get-tuple-element.53), channel_id=1, source_target_pairs={{0,1},{1,0},{2,3},{3,2},{4,5},{5,4},{6,7},{7,6},{8,9},{9,8},{10,11... | collective-permute-start | bytes 3538952 | tf_op jit(solution)/shard_map/ppermute | solution.py:233
  120.6 14.6 %collective-permute-start.2 = (f32[32]{0:T(128)S(1)}, f32[32]{0:T(128)S(1)}, u32[]{:S(2)}, u32[]{:S(2)}) collective-permute-start(f32[32]{0:T(128)S(1)} %maximum_reduce_fusion), channel_id=1, source_target_pairs={{0,1},{1,0},{2,3},{3,2},{4,5},{5,4},{6,7},{7,6},{8,9},{9,8},{10,11... | collective-permute-start | bytes 392 | tf_op jit(solution)/shard_map/ppermute | solution.py:233
  120.7 15.7 %collective-permute-start.3 = (f32[32]{0:T(128)S(1)}, f32[32]{0:T(128)S(1)}, u32[]{:S(2)}, u32[]{:S(2)}) collective-permute-start(f32[32]{0:T(128)S(1)} %maximum_reduce_fusion), channel_id=1, source_target_pairs={{0,2},{1,3},{2,0},{3,1},{4,6},{5,7},{6,4},{7,5},{8,10},{9,11},{10,... | collective-permute-start | bytes 392 | tf_op jit(solution)/shard_map/ppermute | solution.py:233
  121.4 43.7 %collective-permute-start.4 = (f32[32]{0:T(128)S(1)}, f32[32]{0:T(128)S(1)}, u32[]{:S(2)}, u32[]{:S(2)}) collective-permute-start(f32[32]{0:T(128)S(1)} %maximum_reduce_fusion), channel_id=1, source_target_pairs={{0,3},{1,2},{2,1},{3,0},{4,7},{5,6},{6,5},{7,4},{8,11},{9,10},{10,... | collective-permute-start | bytes 392 | tf_op jit(solution)/shard_map/ppermute | solution.py:233
  126.6 6.0 %copy-start.3 = (bf16[4,384,384]{2,1,0:T(8,128)(2,1)}, bf16[4,384,384]{2,1,0:T(8,128)(2,1)S(1)}, u32[]{:S(2)}) copy-start(bf16[4,384,384]{2,1,0:T(8,128)(2,1)S(1)} %add.196) | copy-start | bytes 3538948
  127.7 37.3 %collective-permute-start.11 = (bf16[384,384]{1,0:T(8,128)(2,1)}, bf16[384,384]{1,0:T(8,128)(2,1)}, u32[]{:S(2)}, u32[]{:S(2)}) collective-permute-start(bf16[384,384]{1,0:T(8,128)(2,1)} %get-tuple-element.84), channel_id=1, source_target_pairs={{0,4},{1,5},{2,6},{3,7},{4,8},{5,9},{6,10},{7,11},{8,12},{9,13},{1... | collective-permute-start | bytes 884744 | tf_op jit(solution)/shard_map/ppermute | solution.py:236
  128.6 36.5 %collective-permute-start.12 = (bf16[384,384]{1,0:T(8,128)(2,1)}, bf16[384,384]{1,0:T(8,128)(2,1)}, u32[]{:S(2)}, u32[]{:S(2)}) collective-permute-start(bf16[384,384]{1,0:T(8,128)(2,1)} %get-tuple-element.83), channel_id=1, source_target_pairs={{0,8},{1,9},{2,10},{3,11},{4,12},{5,13},{6,14},{7,15},{8,0},{9,1},... | collective-permute-start | bytes 884744 | tf_op jit(solution)/shard_map/ppermute | solution.py:236
  129.8 2.8 copy-start.4
  135.2 29.9 %collective-permute-start.13 = (bf16[384,384]{1,0:T(8,128)(2,1)}, bf16[384,384]{1,0:T(8,128)(2,1)}, u32[]{:S(2)}, u32[]{:S(2)}) collective-permute-start(bf16[384,384]{1,0:T(8,128)(2,1)} %get-tuple-element.82), channel_id=1, source_target_pairs={{0,12},{1,13},{2,14},{3,15},{4,0},{5,1},{6,2},{7,3},{8,4},{9,5},{1... | collective-permute-start | bytes 884744 | tf_op jit(solution)/shard_map/ppermute | solution.py:236
  136.4 28.7 %collective-permute-start.14 = (bf16[4,384,384]{2,1,0:T(8,128)(2,1)}, bf16[4,384,384]{2,1,0:T(8,128)(2,1)}, u32[]{:S(2)}, u32[]{:S(2)}) collective-permute-start(bf16[4,384,384]{2,1,0:T(8,128)(2,1)} %add.206), channel_id=1, source_target_pairs={{0,2},{1,3},{2,0},{3,1},{4,6},{5,7},{6,4},{7,5},{8,10},{9,11},{10,... | collective-permute-start | bytes 3538952 | tf_op jit(solution)/shard_map/ppermute | solution.py:233
  167.2 9.8 %collective-permute-start.8 = (f32[32]{0:T(128)S(1)}, f32[32]{0:T(128)S(1)}, u32[]{:S(2)}, u32[]{:S(2)}) collective-permute-start(f32[32]{0:T(128)S(1)} %add_add_fusion.1), channel_id=1, source_target_pairs={{0,4},{1,5},{2,6},{3,7},{4,8},{5,9},{6,10},{7,11},{8,12},{9,13},{1... | collective-permute-start | bytes 392 | tf_op jit(solution)/shard_map/ppermute | solution.py:236
  170.0 32.8 %collective-permute-start.9 = (f32[32]{0:T(128)S(1)}, f32[32]{0:T(128)S(1)}, u32[]{:S(2)}, u32[]{:S(2)}) collective-permute-start(f32[32]{0:T(128)S(1)} %add_add_fusion.1), channel_id=1, source_target_pairs={{0,8},{1,9},{2,10},{3,11},{4,12},{5,13},{6,14},{7,15},{8,0},{9,1},... | collective-permute-start | bytes 392 | tf_op jit(solution)/shard_map/ppermute | solution.py:236
  170.0 32.8 %collective-permute-start.10 = (f32[32]{0:T(128)S(1)}, f32[32]{0:T(128)S(1)}, u32[]{:S(2)}, u32[]{:S(2)}) collective-permute-start(f32[32]{0:T(128)S(1)} %add_add_fusion.1), channel_id=1, source_target_pairs={{0,12},{1,13},{2,14},{3,15},{4,0},{5,1},{6,2},{7,3},{8,4},{9,5},{1... | collective-permute-start | bytes 392 | tf_op jit(solution)/shard_map/ppermute | solution.py:236
  172.6 30.1 %collective-permute-start.15 = (bf16[384,384]{1,0:T(8,128)(2,1)S(1)}, bf16[384,384]{1,0:T(8,128)(2,1)S(1)}, u32[]{:S(2)}, u32[]{:S(2)}) collective-permute-start(bf16[384,384]{1,0:T(8,128)(2,1)S(1)} %get-tuple-element.81), channel_id=1, source_target_pairs={{0,4},{1,5},{2,6},{3,7},{4,8},{5,9},{6,10},{7,11},{8,12},{9,13},{1... | collective-permute-start | bytes 884744 | tf_op jit(solution)/shard_map/ppermute | solution.py:236
  175.9 34.6 %collective-permute-start.16 = (bf16[384,384]{1,0:T(8,128)(2,1)S(1)}, bf16[384,384]{1,0:T(8,128)(2,1)S(1)}, u32[]{:S(2)}, u32[]{:S(2)}) collective-permute-start(bf16[384,384]{1,0:T(8,128)(2,1)S(1)} %get-tuple-element.80), channel_id=1, source_target_pairs={{0,8},{1,9},{2,10},{3,11},{4,12},{5,13},{6,14},{7,15},{8,0},{9,1},... | collective-permute-start | bytes 884744 | tf_op jit(solution)/shard_map/ppermute | solution.py:236
  177.0 33.5 %collective-permute-start.17 = (bf16[384,384]{1,0:T(8,128)(2,1)S(1)}, bf16[384,384]{1,0:T(8,128)(2,1)S(1)}, u32[]{:S(2)}, u32[]{:S(2)}) collective-permute-start(bf16[384,384]{1,0:T(8,128)(2,1)S(1)} %get-tuple-element.79), channel_id=1, source_target_pairs={{0,12},{1,13},{2,14},{3,15},{4,0},{5,1},{6,2},{7,3},{8,4},{9,5},{1... | collective-permute-start | bytes 884744 | tf_op jit(solution)/shard_map/ppermute | solution.py:236
  210.6 14.5 %copy-start.1 = (bf16[384,384]{1,0:T(8,128)(2,1)}, bf16[384,384]{1,0:T(8,128)(2,1)S(1)}, u32[]{:S(2)}) copy-start(bf16[384,384]{1,0:T(8,128)(2,1)S(1)} %fusion.2.rest_0_) | copy-start | bytes 884740
  210.7 14.5 %collective-permute-start.18 = (bf16[384,384]{1,0:T(8,128)(2,1)S(1)}, bf16[384,384]{1,0:T(8,128)(2,1)S(1)}, u32[]{:S(2)}, u32[]{:S(2)}) collective-permute-start(bf16[384,384]{1,0:T(8,128)(2,1)S(1)} %fusion.2.rest_0_), channel_id=1, source_target_pairs={{12,8},{13,9},{14,10},{15,11},{8,4},{9,5},{10,6},{11,7},{4,0},{5,1... | collective-permute-start | bytes 884744 | tf_op jit(solution)/shard_map/ppermute | solution.py:239
  212.2 24.2 %collective-permute-start.19 = (bf16[384,384]{1,0:T(8,128)(2,1)S(1)}, bf16[384,384]{1,0:T(8,128)(2,1)}, u32[]{:S(2)}, u32[]{:S(2)}) collective-permute-start(bf16[384,384]{1,0:T(8,128)(2,1)S(1)} %fusion.2.rest_0_), channel_id=1, source_target_pairs={{0,4},{1,5},{2,6},{3,7},{4,8},{5,9},{6,10},{7,11},{8,12},{9,13},{1... | collective-permute-start | bytes 884744 | tf_op jit(solution)/shard_map/ppermute | solution.py:239
  225.2 0.7 copy-start.5
  236.4 35.9 %copy-start = (bf16[16,250,384]{2,1,0:T(8,128)(2,1)S(1)}, bf16[16,250,384]{2,1,0:T(8,128)(2,1)}, u32[]{:S(2)}) copy-start(bf16[16,250,384]{2,1,0:T(8,128)(2,1)} %get-tuple-element.60.h_ref) | copy-start | bytes 9216004
  237.6 2.5 collective-permute-start.20
  238.3 9.7 %collective-permute-start.21 = (bf16[384,384]{1,0:T(8,128)(2,1)}, bf16[384,384]{1,0:T(8,128)(2,1)S(1)}, u32[]{:S(2)}, u32[]{:S(2)}) collective-permute-start(bf16[384,384]{1,0:T(8,128)(2,1)} %collective-permute-done.19), channel_id=1, source_target_pairs={{4,8},{5,9},{6,10},{7,11},{8,12},{9,13},{10,14},{11,15},{20,24},{2... | collective-permute-start | bytes 884744 | tf_op jit(solution)/shard_map/ppermute | solution.py:239
  239.6 11.6 %collective-permute-start.23 = (bf16[384,384]{1,0:T(8,128)(2,1)}, bf16[384,384]{1,0:T(8,128)(2,1)}, u32[]{:S(2)}, u32[]{:S(2)}) collective-permute-start(bf16[384,384]{1,0:T(8,128)(2,1)} %copy-done.1), channel_id=1, source_target_pairs={{0,2},{1,3},{2,0},{3,1},{4,6},{5,7},{6,4},{7,5},{8,10},{9,11},{10,... | collective-permute-start | bytes 884744 | tf_op jit(solution)/shard_map/ppermute | solution.py:233
  248.7 8.9 %collective-permute-start.22 = (bf16[384,384]{1,0:T(8,128)(2,1)}, bf16[384,384]{1,0:T(8,128)(2,1)}, u32[]{:S(2)}, u32[]{:S(2)}) collective-permute-start(bf16[384,384]{1,0:T(8,128)(2,1)} %broadcast_select_fusion.rest_2_), channel_id=1, source_target_pairs={{8,12},{9,13},{10,14},{11,15},{4,0},{5,1},{6,2},{7,3},{24,28},{25,... | collective-permute-start | bytes 884744 | tf_op jit(solution)/shard_map/ppermute | solution.py:239
  250.0 10.6 %collective-permute-start.27 = (bf16[384,384]{1,0:T(8,128)(2,1)}, bf16[384,384]{1,0:T(8,128)(2,1)}, u32[]{:S(2)}, u32[]{:S(2)}) collective-permute-start(bf16[384,384]{1,0:T(8,128)(2,1)} %copy-done.1), channel_id=1, source_target_pairs={{0,1},{1,0},{2,3},{3,2},{4,5},{5,4},{6,7},{7,6},{8,9},{9,8},{10,11... | collective-permute-start | bytes 884744 | tf_op jit(solution)/shard_map/ppermute | solution.py:233
  250.1 11.5 %collective-permute-start.24 = (bf16[384,384]{1,0:T(8,128)(2,1)S(1)}, bf16[384,384]{1,0:T(8,128)(2,1)}, u32[]{:S(2)}, u32[]{:S(2)}) collective-permute-start(bf16[384,384]{1,0:T(8,128)(2,1)S(1)} %broadcast_select_fusion.1.rest_1_), channel_id=1, source_target_pairs={{0,2},{1,3},{2,0},{3,1},{4,6},{5,7},{6,4},{7,5},{8,10},{9,11},{10,... | collective-permute-start | bytes 884744 | tf_op jit(solution)/shard_map/ppermute | solution.py:233
  251.0 10.6 %collective-permute-start.28 = (bf16[384,384]{1,0:T(8,128)(2,1)S(1)}, bf16[384,384]{1,0:T(8,128)(2,1)}, u32[]{:S(2)}, u32[]{:S(2)}) collective-permute-start(bf16[384,384]{1,0:T(8,128)(2,1)S(1)} %broadcast_select_fusion.1.rest_1_), channel_id=1, source_target_pairs={{0,1},{1,0},{2,3},{3,2},{4,5},{5,4},{6,7},{7,6},{8,9},{9,8},{10,11... | collective-permute-start | bytes 884744 | tf_op jit(solution)/shard_map/ppermute | solution.py:233
  251.2 11.0 %collective-permute-start.31 = (bf16[384,384]{1,0:T(8,128)(2,1)}, bf16[384,384]{1,0:T(8,128)(2,1)}, u32[]{:S(2)}, u32[]{:S(2)}) collective-permute-start(bf16[384,384]{1,0:T(8,128)(2,1)} %collective-permute-done.23.rest_4_), channel_id=1, source_target_pairs={{0,1},{1,0},{2,3},{3,2},{4,5},{5,4},{6,7},{7,6},{8,9},{9,8},{10,11... | collective-permute-start | bytes 884744 | tf_op jit(solution)/shard_map/ppermute | solution.py:233
  257.6 10.3 %collective-permute-start.25 = (bf16[384,384]{1,0:T(8,128)(2,1)}, bf16[384,384]{1,0:T(8,128)(2,1)}, u32[]{:S(2)}, u32[]{:S(2)}) collective-permute-start(bf16[384,384]{1,0:T(8,128)(2,1)} %broadcast_select_fusion.rest_2_), channel_id=1, source_target_pairs={{0,2},{1,3},{2,0},{3,1},{4,6},{5,7},{6,4},{7,5},{8,10},{9,11},{10,... | collective-permute-start | bytes 884744 | tf_op jit(solution)/shard_map/ppermute | solution.py:233
  260.6 11.6 %collective-permute-start.26 = (bf16[384,384]{1,0:T(8,128)(2,1)}, bf16[384,384]{1,0:T(8,128)(2,1)}, u32[]{:S(2)}, u32[]{:S(2)}) collective-permute-start(bf16[384,384]{1,0:T(8,128)(2,1)} %select_select_fusion.rest_3_), channel_id=1, source_target_pairs={{0,2},{1,3},{2,0},{3,1},{4,6},{5,7},{6,4},{7,5},{8,10},{9,11},{10,... | collective-permute-start | bytes 884744 | tf_op jit(solution)/shard_map/ppermute | solution.py:233
  261.6 18.8 %collective-permute-start.29 = (bf16[384,384]{1,0:T(8,128)(2,1)}, bf16[384,384]{1,0:T(8,128)(2,1)}, u32[]{:S(2)}, u32[]{:S(2)}) collective-permute-start(bf16[384,384]{1,0:T(8,128)(2,1)} %broadcast_select_fusion.rest_2_), channel_id=1, source_target_pairs={{0,1},{1,0},{2,3},{3,2},{4,5},{5,4},{6,7},{7,6},{8,9},{9,8},{10,11... | collective-permute-start | bytes 884744 | tf_op jit(solution)/shard_map/ppermute | solution.py:233
  261.7 18.8 %collective-permute-start.32 = (bf16[384,384]{1,0:T(8,128)(2,1)}, bf16[384,384]{1,0:T(8,128)(2,1)}, u32[]{:S(2)}, u32[]{:S(2)}) collective-permute-start(bf16[384,384]{1,0:T(8,128)(2,1)} %collective-permute-done.24.rest_5_), channel_id=1, source_target_pairs={{0,1},{1,0},{2,3},{3,2},{4,5},{5,4},{6,7},{7,6},{8,9},{9,8},{10,11... | collective-permute-start | bytes 884744 | tf_op jit(solution)/shard_map/ppermute | solution.py:233
  262.2 18.3 %collective-permute-start.30 = (bf16[384,384]{1,0:T(8,128)(2,1)}, bf16[384,384]{1,0:T(8,128)(2,1)}, u32[]{:S(2)}, u32[]{:S(2)}) collective-permute-start(bf16[384,384]{1,0:T(8,128)(2,1)} %select_select_fusion.rest_3_), channel_id=1, source_target_pairs={{0,1},{1,0},{2,3},{3,2},{4,5},{5,4},{6,7},{7,6},{8,9},{9,8},{10,11... | collective-permute-start | bytes 884744 | tf_op jit(solution)/shard_map/ppermute | solution.py:233
  267.9 12.5 %collective-permute-start.33 = (bf16[384,384]{1,0:T(8,128)(2,1)}, bf16[384,384]{1,0:T(8,128)(2,1)}, u32[]{:S(2)}, u32[]{:S(2)}) collective-permute-start(bf16[384,384]{1,0:T(8,128)(2,1)} %collective-permute-done.25.rest_6_), channel_id=1, source_target_pairs={{0,1},{1,0},{2,3},{3,2},{4,5},{5,4},{6,7},{7,6},{8,9},{9,8},{10,11... | collective-permute-start | bytes 884744 | tf_op jit(solution)/shard_map/ppermute | solution.py:233
  272.2 8.2 %collective-permute-start.34 = (bf16[384,384]{1,0:T(8,128)(2,1)}, bf16[384,384]{1,0:T(8,128)(2,1)}, u32[]{:S(2)}, u32[]{:S(2)}) collective-permute-start(bf16[384,384]{1,0:T(8,128)(2,1)} %collective-permute-done.26.rest_7_), channel_id=1, source_target_pairs={{0,1},{1,0},{2,3},{3,2},{4,5},{5,4},{6,7},{7,6},{8,9},{9,8},{10,11... | collective-permute-start | bytes 884744 | tf_op jit(solution)/shard_map/ppermute | solution.py:233
  272.4 4.6 %copy-start.2 = (bf16[384,384]{1,0:T(8,128)(2,1)S(1)}, bf16[384,384]{1,0:T(8,128)(2,1)}, u32[]{:S(2)}) copy-start(bf16[384,384]{1,0:T(8,128)(2,1)} %copy-done.1) | copy-start | bytes 884740
  284.1 11.6 %collective-permute-start.35 = (f32[250,384]{1,0:T(8,128)S(1)}, f32[250,384]{1,0:T(8,128)S(1)}, u32[]{:S(2)}, u32[]{:S(2)}) collective-permute-start(f32[250,384]{1,0:T(8,128)S(1)} %shard_map.61), channel_id=1, source_target_pairs={{0,16},{16,0},{1,17},{17,1},{2,18},{18,2},{3,19},{19,3},{4,20},{20... | collective-permute-start | bytes 1152008 | tf_op jit(solution)/shard_map/ppermute | solution.py:368
Sparse Core Ops, SparseCore 0:
  9.6 44.9 all-gather.9
  56.9 43.9 all-gather.11
  167.4 71.7 all-gather.7

commit v7 on v4

--- a/solution.py
+++ b/solution.py
@@ -342,7 +342,9 @@
             )
     bit = 1
     while bit < parts:
-        sigma = sigma + lax.ppermute(sigma, "aux", [(i, i ^ bit) for i in range(parts)])
+        mine = lax.optimization_barrier(sigma.astype(BF16))
+        other = lax.ppermute(mine, "aux", [(i, i ^ bit) for i in range(parts)])
+        sigma = mine.astype(F32) + other.astype(F32)
         bit *= 2
     return sigma[:, :nint] / math.sqrt(naux * parts * nint)
 

time: 301 us -> 297 us (0.987)
  waiting for transfers between devices: 113 us -> 108 us
    ppermute x1, waiting for transfers between devices: 11 us -> 6.82 us  [body(): other = lax.ppermute(mine, 'aux', [(i, i ^ bit) for i in range(parts)])]
where the time goes in v7:
time: 297 us; the launch traced here: 295 us
  Pallas kernels  119 us (40%)
  waiting for transfers between devices  108 us (36%)
  starting transfers between devices  32.9 us (11%)
  other arithmetic  14.9 us (5%)
  between operations  13.5 us (5%)
  local copies, waits for them, and re-layouts  6.26 us (2%)
    pallas_call x2, Pallas kernels, rot_part(): pl.pallas_call(functools.partial(rot_kernel, paux, fan, nz, cuts), grid_s...  54.9 us
    pallas_call x2, Pallas kernels, occ_part(): pl.pallas_call(functools.partial(occ_kernel, paux), grid=(nscale,), in_sp...  53 us
    all_gather x1, waiting for transfers between devices, body(): whole_r = lax.all_gather(rot_coeff, 'ao', axis=0)  43.6 us
    ppermute x12, waiting for transfers between devices, turn_z(): lax.ppermute(value, 'ao', [(i, (i + by * fan) % groups) for i in range(gr...  40.9 us
    ppermute x12, starting transfers between devices, turn_z(): lax.ppermute(value, 'ao', [(i, (i + by * fan) % groups) for i in range(gr...  20.6 us
    ppermute x21, waiting for transfers between devices, swap(): return lax.ppermute(value, 'ao', [(i, i ^ bit) for i in range(groups)])  15.7 us
    ppermute x21, starting transfers between devices, swap(): return lax.ppermute(value, 'ao', [(i, i ^ bit) for i in range(groups)])  11.7 us
    add x6, other arithmetic, reduce_steps(): live = {d: v + sent[d | bit] for d, v in live.items() if not d & bit}  10.5 us
  transfers between devices with their start and end apart: 37, of which 11 were waited for; matrix products, arithmetic and copies ran while one was open for 5% of the time, Pallas kernels for 39%

profile of v7, /device:TPU:28, one launch (start us, length us, event | category | flops | bytes accessed | tf_op | source)
XLA Modules:
  0.0 295.3 jit_solution(1319275876992628081)
XLA Ops:
  6.5 0.7 all-gather.10.cloned.1.call-update
  7.3 0.7 all-gather.12.cloned.1.call-update
  8.1 1.1 copy.12
  9.1 0.8 copy.13.scale_ref
  10.0 1.0 convert_multiply_fusion
  11.0 43.6 %all-gather.10.cloned.1.call-done.m_ref = bf16[16,250,380]{2,1,0:T(8,128)(2,1)} async-done(((bf16[1,250,380]{2,1,0:T(8,128)(2,1)}), bf16[16,250,380]{2,1,0:T(8,128)(2,1)}) %all-gather.10.cloned.1.call-update) | async-done | bytes 3040016 | tf_op jit(solution)/shard_map/all_gather | solution.py:252
  54.6 28.2 %shard_map.55 = (bf16[4,384,384]{2,1,0:T(8,128)(2,1)S(1)}, bf16[4,384,384]{2,1,0:T(8,128)(2,1)S(1)}, bf16[4,384,384]{2,1,0:T(8,128)(2,1)}, bf16[4,384,384]{2,1,0...) custom-call(s32[1]{0:T(128)} %bitcast.8.me_ref, bf16[250,32,4000]{2,1,0:T(8,128)(2,1)} %bitcast.43, ...), custom_call_target="tpu_custom_call" | custom-call | flops 12288000000 | bytes 32000000 | tf_op jit(solution)/shard_map/pallas_call | solution.py:144
  83.3 2.4 collective-permute-done
  85.7 1.9 collective-permute-done.1
  87.6 2.7 add.217
  90.3 1.4 collective-permute-start.5
  91.7 1.3 add.216
  93.0 26.7 %shard_map.56 = (bf16[4,384,384]{2,1,0:T(8,128)(2,1)S(1)}, bf16[4,384,384]{2,1,0:T(8,128)(2,1)S(1)}, bf16[4,384,384]{2,1,0:T(8,128)(2,1)}, bf16[4,384,384]{2,1,0:T(8,128)(2,1)}, f32[16,1,384]{2,1,0:T(1,128)S(1)}) custom-call(s32[1]{0:T(128)} %bitcast.8.me_ref, bf16[250,32,4000]{2,1,0:T(8,128)(2,1)} %bitcast.44, bf16[4000,384]{1,0:T(8,128)(2,1)} %get-tuple-element.40.m_ref, ...), custom_call_target="tpu_custom_call" | custom-call | flops 12288000000 | bytes 32000000 | tf_op jit(solution)/shard_map/pallas_call | solution.py:144
  120.6 0.7 collective-permute-start.3
  121.3 1.2 collective-permute-start.4
  122.5 1.9 collective-permute-done.6
  124.6 1.9 add.218
  126.6 1.1 collective-permute-start.11
  127.7 1.2 collective-permute-start.12
  128.9 1.7 add.228
  130.7 2.6 add.229
  133.2 1.2 collective-permute-start.13
  134.5 1.4 collective-permute-start.14
  135.9 27.1 %shard_map.57 = (bf16[16,250,384]{2,1,0:T(8,128)(2,1)}, bf16[4000,384]{1,0:T(8,128)(2,1)S(1)}) custom-call(bf16[250,32,4000]{2,1,0:T(8,128)(2,1)} %bitcast.45, bf16[16,250,380]{2,1,0:T(8,128)(2,1)} %all-gather.12.cloned.1.call-done.m_ref, f32[10,32,1]{2,1,0:T(8,128)S(1)} %copy.13.scale_ref, f32[8,128]{1,0:T(8,128)S(1)} %broadcast_in_dim.11.tie_ref), custom_call_target="tpu_custom_call" | custom-call | flops 12288000000 | bytes 32000000 | tf_op jit(solution)/shard_map/pallas_call | solution.py:169
  163.0 1.7 copy-done.1
  164.7 2.1 fusion.5
  166.8 2.7 collective-permute-start.8
  170.6 3.2 %collective-permute-start.15 = (bf16[384,384]{1,0:T(8,128)(2,1)S(1)}, bf16[384,384]{1,0:T(8,128)(2,1)S(1)}, u32[]{:S(2)}, u32[]{:S(2)}) collective-permute-start(bf16[384,384]{1,0:T(8,128)(2,1)S(1)} %get-tuple-element.75), channel_id=1, source_target_pairs={{0,4},{1,5},{2,6},{3,7},{4,8},{5,9},{6,10},{7,11},{8,12},{9,13},{1... | collective-permute-start | bytes 884744 | tf_op jit(solution)/shard_map/ppermute | solution.py:236
  173.9 1.1 collective-permute-start.16
  175.0 25.8 %shard_map.58.h_ref = bf16[16,250,384]{2,1,0:T(8,128)(2,1)} custom-call(bf16[250,32,4000]{2,1,0:T(8,128)(2,1)} %bitcast.46, bf16[4000,384]{1,0:T(8,128)(2,1)S(1)} %copy-done.2, f32[10,32,1]{2,1,0:T(8,128)S(1)} %copy.13.scale_ref, f32[8,128]{1,0:T(8,128)S(1)} %broadcast_in_dim.11.tie_ref), custom_call_target="tpu_custom_call" | custom-call | flops 12288000000 | bytes 32000000 | tf_op jit(solution)/shard_map/pallas_call | solution.py:169
  200.9 7.6 %collective-permute-done.16 = bf16[384,384]{1,0:T(8,128)(2,1)S(1)} collective-permute-done((bf16[384,384]{1,0:T(8,128)(2,1)S(1)}, bf16[384,384]{1,0:T(8,128)(2,1)S(1)}, u32[]{:S(2)}, u32[]{:S(2)}) %collective-permute-start.16) | collective-permute-done | bytes 294944 | tf_op jit(solution)/shard_map/ppermute | solution.py:236
  208.7 7.3 %collective-permute-start.19 = (bf16[384,384]{1,0:T(8,128)(2,1)S(1)}, bf16[384,384]{1,0:T(8,128)(2,1)}, u32[]{:S(2)}, u32[]{:S(2)}) collective-permute-start(bf16[384,384]{1,0:T(8,128)(2,1)S(1)} %fusion.2.rest_0_), channel_id=1, source_target_pairs={{0,8},{1,9},{2,10},{3,11},{4,12},{5,13},{6,14},{7,15},{8,0},{9,1},... | collective-permute-start | bytes 884744 | tf_op jit(solution)/shard_map/ppermute | solution.py:236
  216.0 1.9 collective-permute-start.20
  218.0 1.3 collective-permute-start.21
  219.3 0.7 copy-done.3
  220.0 5.8 %collective-permute-done.18.rest_1_ = bf16[384,384]{1,0:T(8,128)(2,1)} collective-permute-done((bf16[384,384]{1,0:T(8,128)(2,1)S(1)}, bf16[384,384]{1,0:T(8,128)(2,1)}, u32[]{:S(2)}, u32[]{:S(2)}) %collective-permute-start.18) | collective-permute-done | bytes 294944 | tf_op jit(solution)/shard_map/ppermute | solution.py:236
  225.8 1.6 collective-permute-start.22
  227.4 27.4 %collective-permute-done.19.rest_2_ = bf16[384,384]{1,0:T(8,128)(2,1)} collective-permute-done((bf16[384,384]{1,0:T(8,128)(2,1)S(1)}, bf16[384,384]{1,0:T(8,128)(2,1)}, u32[]{:S(2)}, u32[]{:S(2)}) %collective-permute-start.19) | collective-permute-done | bytes 294944 | tf_op jit(solution)/shard_map/ppermute | solution.py:236
  255.3 1.5 collective-permute-start.24
  256.8 0.7 copy-done.7
  257.5 0.7 copy-done.5
  259.0 6.0 %collective-permute-done.23.rest_6_ = bf16[384,384]{1,0:T(8,128)(2,1)} collective-permute-done((bf16[384,384]{1,0:T(8,128)(2,1)}, bf16[384,384]{1,0:T(8,128)(2,1)}, u32[]{:S(2)}, u32[]{:S(2)}) %collective-permute-start.23) | collective-permute-done | bytes 294944 | tf_op jit(solution)/shard_map/ppermute | solution.py:233
  265.0 3.2 %collective-permute-done.24.rest_7_ = bf16[384,384]{1,0:T(8,128)(2,1)} collective-permute-done((bf16[384,384]{1,0:T(8,128)(2,1)}, bf16[384,384]{1,0:T(8,128)(2,1)}, u32[]{:S(2)}, u32[]{:S(2)}) %collective-permute-start.24) | collective-permute-done | bytes 294944 | tf_op jit(solution)/shard_map/ppermute | solution.py:233
  268.9 4.7 %shard_map.59.base_ref = f32[250,384]{1,0:T(8,128)S(1)} custom-call(f32[16]{0:T(128)S(1)} %get-tuple-element.79.gamma_ref, f32[250,384]{1,0:T(8,128)S(1)} %broadcast_in_dim.12.base_ref, bf16[16,250,384]{2,1,0:T(8,128)(2,1)S(1)} %copy-done, bf16[16,384,384]{2,1,0:T(8,128)(2,1)} %bitcast.47), custom_call_target="tpu_custom_call" | custom-call | flops 1179648000 | bytes 4718592 | tf_op jit(solution)/shard_map/pallas_call | solution.py:188
  273.6 3.5 %shard_map.60.base_ref = f32[250,384]{1,0:T(8,128)S(1)} custom-call(s32[8]{0:T(128)S(1)} %stack.71.owners_ref, f32[16]{0:T(128)S(1)} %get-tuple-element.80.gamma_ref, f32[250,384]{1,0:T(8,128)S(1)} %shard_map.59.base_ref, bf16[16,250,384]{2,1,0:T(8,128)(2,1)} %shard_map.58.h_ref, bf16[384,384]{1,0:T(8,128)(2,1)S(1)} %copy-done.4, ...), custom_call_target="tpu_custom_call" | custom-call | flops 589824000 | bytes 2359296 | tf_op jit(solution)/shard_map/pallas_call | solution.py:206
  277.2 3.5 %shard_map.61 = f32[250,384]{1,0:T(8,128)S(1)} custom-call(s32[8]{0:T(128)S(1)} %stack.62.owners_ref, f32[16]{0:T(128)S(1)} %get-tuple-element.80.gamma_ref, f32[250,384]{1,0:T(8,128)S(1)} %shard_map.60.base_ref, bf16[16,250,384]{2,1,0:T(8,128)(2,1)} %shard_map.58.h_ref, bf16[384,384]{1,0:T(8,128)(2,1)S(1)} %copy-done.6, ...), custom_call_target="tpu_custom_call" | custom-call | flops 589824000 | bytes 2359296 | tf_op jit(solution)/shard_map/pallas_call | solution.py:206
  281.2 6.8 %collective-permute-done.33 = bf16[250,384]{1,0:T(8,128)(2,1)S(1)} collective-permute-done((bf16[250,384]{1,0:T(8,128)(2,1)S(1)}, bf16[250,384]{1,0:T(8,128)(2,1)S(1)}, u32[]{:S(2)}, u32[]{:S(2)}) %collective-permute-start.33) | collective-permute-done | bytes 192032 | tf_op jit(solution)/shard_map/ppermute | solution.py:346
  288.0 0.8 add_multiply_fusion
  (83 shorter events, 5.8 us)
Async XLA Ops:
  6.5 48.1 %all-gather.10.cloned.1.call-start = ((), (), s32[]{:S(2)}) async-start(), calls=%async_computation.1 | async-start | bytes 3342336 | tf_op jit(solution)/shard_map/all_gather | solution.py:252
  7.3 128.6 %all-gather.12.cloned.1.call-start = ((), (), s32[]{:S(2)}) async-start(), calls=%async_computation.2 | async-start | bytes 3342336 | tf_op jit(solution)/shard_map/all_gather | solution.py:253
  8.0 260.9 %all-gather.8.cloned.1.call-start = ((), (), s32[]{:S(2)}) async-start(), calls=%async_computation | async-start | bytes 5013504 | tf_op jit(solution)/shard_map/all_gather | solution.py:270
  82.8 2.9 collective-permute-start
  83.1 4.6 %collective-permute-start.1 = (bf16[4,384,384]{2,1,0:T(8,128)(2,1)}, bf16[4,384,384]{2,1,0:T(8,128)(2,1)S(1)}, u32[]{:S(2)}, u32[]{:S(2)}) collective-permute-start(bf16[4,384,384]{2,1,0:T(8,128)(2,1)} %get-tuple-element.43), channel_id=1, source_target_pairs={{0,1},{1,0},{2,3},{3,2},{4,5},{5,4},{6,7},{7,6},{8,9},{9,8},{10,11... | collective-permute-start | bytes 3538952 | tf_op jit(solution)/shard_map/ppermute | solution.py:233
  90.3 31.0 %collective-permute-start.5 = (bf16[4,384,384]{2,1,0:T(8,128)(2,1)}, bf16[4,384,384]{2,1,0:T(8,128)(2,1)}, u32[]{:S(2)}, u32[]{:S(2)}) collective-permute-start(bf16[4,384,384]{2,1,0:T(8,128)(2,1)} %add.217), channel_id=1, source_target_pairs={{0,2},{1,3},{2,0},{3,1},{4,6},{5,7},{6,4},{7,5},{8,10},{9,11},{10,... | collective-permute-start | bytes 3538952 | tf_op jit(solution)/shard_map/ppermute | solution.py:233
  119.7 4.6 %collective-permute-start.6 = (bf16[4,384,384]{2,1,0:T(8,128)(2,1)S(1)}, bf16[4,384,384]{2,1,0:T(8,128)(2,1)}, u32[]{:S(2)}, u32[]{:S(2)}) collective-permute-start(bf16[4,384,384]{2,1,0:T(8,128)(2,1)S(1)} %get-tuple-element.49), channel_id=1, source_target_pairs={{0,1},{1,0},{2,3},{3,2},{4,5},{5,4},{6,7},{7,6},{8,9},{9,8},{10,11... | collective-permute-start | bytes 3538952 | tf_op jit(solution)/shard_map/ppermute | solution.py:233
  119.7 4.9 %collective-permute-start.7 = (bf16[4,384,384]{2,1,0:T(8,128)(2,1)}, bf16[4,384,384]{2,1,0:T(8,128)(2,1)}, u32[]{:S(2)}, u32[]{:S(2)}) collective-permute-start(bf16[4,384,384]{2,1,0:T(8,128)(2,1)} %get-tuple-element.50), channel_id=1, source_target_pairs={{0,1},{1,0},{2,3},{3,2},{4,5},{5,4},{6,7},{7,6},{8,9},{9,8},{10,11... | collective-permute-start | bytes 3538952 | tf_op jit(solution)/shard_map/ppermute | solution.py:233
  120.5 12.7 %collective-permute-start.2 = (f32[32]{0:T(128)S(1)}, f32[32]{0:T(128)S(1)}, u32[]{:S(2)}, u32[]{:S(2)}) collective-permute-start(f32[32]{0:T(128)S(1)} %maximum_reduce_fusion), channel_id=1, source_target_pairs={{0,1},{1,0},{2,3},{3,2},{4,5},{5,4},{6,7},{7,6},{8,9},{9,8},{10,11... | collective-permute-start | bytes 392 | tf_op jit(solution)/shard_map/ppermute | solution.py:233
  120.6 13.9 %collective-permute-start.3 = (f32[32]{0:T(128)S(1)}, f32[32]{0:T(128)S(1)}, u32[]{:S(2)}, u32[]{:S(2)}) collective-permute-start(f32[32]{0:T(128)S(1)} %maximum_reduce_fusion), channel_id=1, source_target_pairs={{0,2},{1,3},{2,0},{3,1},{4,6},{5,7},{6,4},{7,5},{8,10},{9,11},{10,... | collective-permute-start | bytes 392 | tf_op jit(solution)/shard_map/ppermute | solution.py:233
  121.3 43.3 %collective-permute-start.4 = (f32[32]{0:T(128)S(1)}, f32[32]{0:T(128)S(1)}, u32[]{:S(2)}, u32[]{:S(2)}) collective-permute-start(f32[32]{0:T(128)S(1)} %maximum_reduce_fusion), channel_id=1, source_target_pairs={{0,3},{1,2},{2,1},{3,0},{4,7},{5,6},{6,5},{7,4},{8,11},{9,10},{10,... | collective-permute-start | bytes 392 | tf_op jit(solution)/shard_map/ppermute | solution.py:233
  126.5 4.1 %copy-start.9 = (bf16[4,384,384]{2,1,0:T(8,128)(2,1)}, bf16[4,384,384]{2,1,0:T(8,128)(2,1)S(1)}, u32[]{:S(2)}) copy-start(bf16[4,384,384]{2,1,0:T(8,128)(2,1)S(1)} %add.218) | copy-start | bytes 3538948
  126.6 38.0 %collective-permute-start.11 = (bf16[384,384]{1,0:T(8,128)(2,1)S(1)}, bf16[384,384]{1,0:T(8,128)(2,1)}, u32[]{:S(2)}, u32[]{:S(2)}) collective-permute-start(bf16[384,384]{1,0:T(8,128)(2,1)S(1)} %get-tuple-element.78), channel_id=1, source_target_pairs={{0,4},{1,5},{2,6},{3,7},{4,8},{5,9},{6,10},{7,11},{8,12},{9,13},{1... | collective-permute-start | bytes 884744 | tf_op jit(solution)/shard_map/ppermute | solution.py:236
  127.7 36.9 %collective-permute-start.12 = (bf16[384,384]{1,0:T(8,128)(2,1)S(1)}, bf16[384,384]{1,0:T(8,128)(2,1)}, u32[]{:S(2)}, u32[]{:S(2)}) collective-permute-start(bf16[384,384]{1,0:T(8,128)(2,1)S(1)} %get-tuple-element.77), channel_id=1, source_target_pairs={{0,8},{1,9},{2,10},{3,11},{4,12},{5,13},{6,14},{7,15},{8,0},{9,1},... | collective-permute-start | bytes 884744 | tf_op jit(solution)/shard_map/ppermute | solution.py:236
  128.9 1.7 copy-start.10
  133.2 31.4 %collective-permute-start.13 = (bf16[384,384]{1,0:T(8,128)(2,1)S(1)}, bf16[384,384]{1,0:T(8,128)(2,1)}, u32[]{:S(2)}, u32[]{:S(2)}) collective-permute-start(bf16[384,384]{1,0:T(8,128)(2,1)S(1)} %get-tuple-element.76), channel_id=1, source_target_pairs={{0,12},{1,13},{2,14},{3,15},{4,0},{5,1},{6,2},{7,3},{8,4},{9,5},{1... | collective-permute-start | bytes 884744 | tf_op jit(solution)/shard_map/ppermute | solution.py:236
  134.5 30.2 %collective-permute-start.14 = (bf16[4,384,384]{2,1,0:T(8,128)(2,1)}, bf16[4,384,384]{2,1,0:T(8,128)(2,1)S(1)}, u32[]{:S(2)}, u32[]{:S(2)}) collective-permute-start(bf16[4,384,384]{2,1,0:T(8,128)(2,1)} %add.229), channel_id=1, source_target_pairs={{0,2},{1,3},{2,0},{3,1},{4,6},{5,7},{6,4},{7,5},{8,10},{9,11},{10,... | collective-permute-start | bytes 3538952 | tf_op jit(solution)/shard_map/ppermute | solution.py:233
  163.0 1.7 copy-start.1
  166.8 8.2 %collective-permute-start.8 = (f32[32]{0:T(128)S(1)}, f32[32]{0:T(128)S(1)}, u32[]{:S(2)}, u32[]{:S(2)}) collective-permute-start(f32[32]{0:T(128)S(1)} %add_add_fusion.1), channel_id=1, source_target_pairs={{0,4},{1,5},{2,6},{3,7},{4,8},{5,9},{6,10},{7,11},{8,12},{9,13},{1... | collective-permute-start | bytes 392 | tf_op jit(solution)/shard_map/ppermute | solution.py:236
  169.5 31.3 %collective-permute-start.9 = (f32[32]{0:T(128)S(1)}, f32[32]{0:T(128)S(1)}, u32[]{:S(2)}, u32[]{:S(2)}) collective-permute-start(f32[32]{0:T(128)S(1)} %add_add_fusion.1), channel_id=1, source_target_pairs={{0,8},{1,9},{2,10},{3,11},{4,12},{5,13},{6,14},{7,15},{8,0},{9,1},... | collective-permute-start | bytes 392 | tf_op jit(solution)/shard_map/ppermute | solution.py:236
  169.5 31.3 %collective-permute-start.10 = (f32[32]{0:T(128)S(1)}, f32[32]{0:T(128)S(1)}, u32[]{:S(2)}, u32[]{:S(2)}) collective-permute-start(f32[32]{0:T(128)S(1)} %add_add_fusion.1), channel_id=1, source_target_pairs={{0,12},{1,13},{2,14},{3,15},{4,0},{5,1},{6,2},{7,3},{8,4},{9,5},{1... | collective-permute-start | bytes 392 | tf_op jit(solution)/shard_map/ppermute | solution.py:236
  170.2 4.8 %copy-start.2 = (bf16[4000,384]{1,0:T(8,128)(2,1)S(1)}, bf16[4000,384]{1,0:T(8,128)(2,1)}, u32[]{:S(2)}) copy-start(bf16[4000,384]{1,0:T(8,128)(2,1)} %copy-done.1) | copy-start | bytes 9216004
  170.6 30.2 %collective-permute-start.15 = (bf16[384,384]{1,0:T(8,128)(2,1)S(1)}, bf16[384,384]{1,0:T(8,128)(2,1)S(1)}, u32[]{:S(2)}, u32[]{:S(2)}) collective-permute-start(bf16[384,384]{1,0:T(8,128)(2,1)S(1)} %get-tuple-element.75), channel_id=1, source_target_pairs={{0,4},{1,5},{2,6},{3,7},{4,8},{5,9},{6,10},{7,11},{8,12},{9,13},{1... | collective-permute-start | bytes 884744 | tf_op jit(solution)/shard_map/ppermute | solution.py:236
  173.9 34.6 %collective-permute-start.16 = (bf16[384,384]{1,0:T(8,128)(2,1)S(1)}, bf16[384,384]{1,0:T(8,128)(2,1)S(1)}, u32[]{:S(2)}, u32[]{:S(2)}) collective-permute-start(bf16[384,384]{1,0:T(8,128)(2,1)S(1)} %get-tuple-element.74), channel_id=1, source_target_pairs={{0,8},{1,9},{2,10},{3,11},{4,12},{5,13},{6,14},{7,15},{8,0},{9,1},... | collective-permute-start | bytes 884744 | tf_op jit(solution)/shard_map/ppermute | solution.py:236
  175.0 33.5 %collective-permute-start.17 = (bf16[384,384]{1,0:T(8,128)(2,1)S(1)}, bf16[384,384]{1,0:T(8,128)(2,1)S(1)}, u32[]{:S(2)}, u32[]{:S(2)}) collective-permute-start(bf16[384,384]{1,0:T(8,128)(2,1)S(1)} %get-tuple-element.73), channel_id=1, source_target_pairs={{0,12},{1,13},{2,14},{3,15},{4,0},{5,1},{6,2},{7,3},{8,4},{9,5},{1... | collective-permute-start | bytes 884744 | tf_op jit(solution)/shard_map/ppermute | solution.py:236
  175.0 93.9 %copy-start = (bf16[16,250,384]{2,1,0:T(8,128)(2,1)S(1)}, bf16[16,250,384]{2,1,0:T(8,128)(2,1)}, u32[]{:S(2)}) copy-start(bf16[16,250,384]{2,1,0:T(8,128)(2,1)} %get-tuple-element.57.h_ref) | copy-start | bytes 9216004
  208.7 17.1 %collective-permute-start.18 = (bf16[384,384]{1,0:T(8,128)(2,1)S(1)}, bf16[384,384]{1,0:T(8,128)(2,1)}, u32[]{:S(2)}, u32[]{:S(2)}) collective-permute-start(bf16[384,384]{1,0:T(8,128)(2,1)S(1)} %fusion.2.rest_0_), channel_id=1, source_target_pairs={{0,4},{1,5},{2,6},{3,7},{4,8},{5,9},{6,10},{7,11},{8,12},{9,13},{1... | collective-permute-start | bytes 884744 | tf_op jit(solution)/shard_map/ppermute | solution.py:236
  208.7 46.0 %collective-permute-start.19 = (bf16[384,384]{1,0:T(8,128)(2,1)S(1)}, bf16[384,384]{1,0:T(8,128)(2,1)}, u32[]{:S(2)}, u32[]{:S(2)}) collective-permute-start(bf16[384,384]{1,0:T(8,128)(2,1)S(1)} %fusion.2.rest_0_), channel_id=1, source_target_pairs={{0,8},{1,9},{2,10},{3,11},{4,12},{5,13},{6,14},{7,15},{8,0},{9,1},... | collective-permute-start | bytes 884744 | tf_op jit(solution)/shard_map/ppermute | solution.py:236
  216.0 39.3 %collective-permute-start.20 = (bf16[384,384]{1,0:T(8,128)(2,1)S(1)}, bf16[384,384]{1,0:T(8,128)(2,1)}, u32[]{:S(2)}, u32[]{:S(2)}) collective-permute-start(bf16[384,384]{1,0:T(8,128)(2,1)S(1)} %fusion.2.rest_0_), channel_id=1, source_target_pairs={{0,12},{1,13},{2,14},{3,15},{4,0},{5,1},{6,2},{7,3},{8,4},{9,5},{1... | collective-permute-start | bytes 884744 | tf_op jit(solution)/shard_map/ppermute | solution.py:236
  218.0 38.8 %collective-permute-start.21 = (bf16[384,384]{1,0:T(8,128)(2,1)S(1)}, bf16[384,384]{1,0:T(8,128)(2,1)S(1)}, u32[]{:S(2)}, u32[]{:S(2)}) collective-permute-start(bf16[384,384]{1,0:T(8,128)(2,1)S(1)} %fusion.2.rest_0_), channel_id=1, source_target_pairs={{0,2},{1,3},{2,0},{3,1},{4,6},{5,7},{6,4},{7,5},{8,10},{9,11},{10,... | collective-permute-start | bytes 884744 | tf_op jit(solution)/shard_map/ppermute | solution.py:233
  219.3 37.5 %collective-permute-start.25 = (bf16[384,384]{1,0:T(8,128)(2,1)S(1)}, bf16[384,384]{1,0:T(8,128)(2,1)S(1)}, u32[]{:S(2)}, u32[]{:S(2)}) collective-permute-start(bf16[384,384]{1,0:T(8,128)(2,1)S(1)} %fusion.2.rest_0_), channel_id=1, source_target_pairs={{0,1},{1,0},{2,3},{3,2},{4,5},{5,4},{6,7},{7,6},{8,9},{9,8},{10,11... | collective-permute-start | bytes 884744 | tf_op jit(solution)/shard_map/ppermute | solution.py:233
  219.3 0.7 copy-start.3
  225.8 32.6 %collective-permute-start.22 = (bf16[384,384]{1,0:T(8,128)(2,1)}, bf16[384,384]{1,0:T(8,128)(2,1)}, u32[]{:S(2)}, u32[]{:S(2)}) collective-permute-start(bf16[384,384]{1,0:T(8,128)(2,1)} %collective-permute-done.18.rest_1_), channel_id=1, source_target_pairs={{0,2},{1,3},{2,0},{3,1},{4,6},{5,7},{6,4},{7,5},{8,10},{9,11},{10,... | collective-permute-start | bytes 884744 | tf_op jit(solution)/shard_map/ppermute | solution.py:233
  254.7 10.3 %collective-permute-start.23 = (bf16[384,384]{1,0:T(8,128)(2,1)}, bf16[384,384]{1,0:T(8,128)(2,1)}, u32[]{:S(2)}, u32[]{:S(2)}) collective-permute-start(bf16[384,384]{1,0:T(8,128)(2,1)} %collective-permute-done.19.rest_2_), channel_id=1, source_target_pairs={{0,2},{1,3},{2,0},{3,1},{4,6},{5,7},{6,4},{7,5},{8,10},{9,11},{10,... | collective-permute-start | bytes 884744 | tf_op jit(solution)/shard_map/ppermute | solution.py:233
  255.3 12.9 %collective-permute-start.24 = (bf16[384,384]{1,0:T(8,128)(2,1)}, bf16[384,384]{1,0:T(8,128)(2,1)}, u32[]{:S(2)}, u32[]{:S(2)}) collective-permute-start(bf16[384,384]{1,0:T(8,128)(2,1)} %collective-permute-done.20.rest_3_), channel_id=1, source_target_pairs={{0,2},{1,3},{2,0},{3,1},{4,6},{5,7},{6,4},{7,5},{8,10},{9,11},{10,... | collective-permute-start | bytes 884744 | tf_op jit(solution)/shard_map/ppermute | solution.py:233
  256.8 0.7 copy-start.7
  256.8 11.4 %collective-permute-start.26 = (bf16[384,384]{1,0:T(8,128)(2,1)}, bf16[384,384]{1,0:T(8,128)(2,1)}, u32[]{:S(2)}, u32[]{:S(2)}) collective-permute-start(bf16[384,384]{1,0:T(8,128)(2,1)} %collective-permute-done.18.rest_1_), channel_id=1, source_target_pairs={{0,1},{1,0},{2,3},{3,2},{4,5},{5,4},{6,7},{7,6},{8,9},{9,8},{10,11... | collective-permute-start | bytes 884744 | tf_op jit(solution)/shard_map/ppermute | solution.py:233
  257.5 0.7 copy-start.5
  258.2 10.5 %collective-permute-start.27 = (bf16[384,384]{1,0:T(8,128)(2,1)}, bf16[384,384]{1,0:T(8,128)(2,1)}, u32[]{:S(2)}, u32[]{:S(2)}) collective-permute-start(bf16[384,384]{1,0:T(8,128)(2,1)} %collective-permute-done.19.rest_2_), channel_id=1, source_target_pairs={{0,1},{1,0},{2,3},{3,2},{4,5},{5,4},{6,7},{7,6},{8,9},{9,8},{10,11... | collective-permute-start | bytes 884744 | tf_op jit(solution)/shard_map/ppermute | solution.py:233
  258.4 18.7 %collective-permute-start.28 = (bf16[384,384]{1,0:T(8,128)(2,1)}, bf16[384,384]{1,0:T(8,128)(2,1)}, u32[]{:S(2)}, u32[]{:S(2)}) collective-permute-start(bf16[384,384]{1,0:T(8,128)(2,1)} %collective-permute-done.20.rest_3_), channel_id=1, source_target_pairs={{0,1},{1,0},{2,3},{3,2},{4,5},{5,4},{6,7},{7,6},{8,9},{9,8},{10,11... | collective-permute-start | bytes 884744 | tf_op jit(solution)/shard_map/ppermute | solution.py:233
  265.0 12.1 %collective-permute-start.29 = (bf16[384,384]{1,0:T(8,128)(2,1)}, bf16[384,384]{1,0:T(8,128)(2,1)}, u32[]{:S(2)}, u32[]{:S(2)}) collective-permute-start(bf16[384,384]{1,0:T(8,128)(2,1)} %copy-done.7), channel_id=1, source_target_pairs={{0,1},{1,0},{2,3},{3,2},{4,5},{5,4},{6,7},{7,6},{8,9},{9,8},{10,11... | collective-permute-start | bytes 884744 | tf_op jit(solution)/shard_map/ppermute | solution.py:233
  268.2 8.9 %collective-permute-start.30 = (bf16[384,384]{1,0:T(8,128)(2,1)}, bf16[384,384]{1,0:T(8,128)(2,1)}, u32[]{:S(2)}, u32[]{:S(2)}) collective-permute-start(bf16[384,384]{1,0:T(8,128)(2,1)} %collective-permute-done.22.rest_5_), channel_id=1, source_target_pairs={{0,1},{1,0},{2,3},{3,2},{4,5},{5,4},{6,7},{7,6},{8,9},{9,8},{10,11... | collective-permute-start | bytes 884744 | tf_op jit(solution)/shard_map/ppermute | solution.py:233
  268.2 8.9 %collective-permute-start.31 = (bf16[384,384]{1,0:T(8,128)(2,1)}, bf16[384,384]{1,0:T(8,128)(2,1)}, u32[]{:S(2)}, u32[]{:S(2)}) collective-permute-start(bf16[384,384]{1,0:T(8,128)(2,1)} %collective-permute-done.23.rest_6_), channel_id=1, source_target_pairs={{0,1},{1,0},{2,3},{3,2},{4,5},{5,4},{6,7},{7,6},{8,9},{9,8},{10,11... | collective-permute-start | bytes 884744 | tf_op jit(solution)/shard_map/ppermute | solution.py:233
  268.7 8.4 %collective-permute-start.32 = (bf16[384,384]{1,0:T(8,128)(2,1)}, bf16[384,384]{1,0:T(8,128)(2,1)}, u32[]{:S(2)}, u32[]{:S(2)}) collective-permute-start(bf16[384,384]{1,0:T(8,128)(2,1)} %collective-permute-done.24.rest_7_), channel_id=1, source_target_pairs={{0,1},{1,0},{2,3},{3,2},{4,5},{5,4},{6,7},{7,6},{8,9},{9,8},{10,11... | collective-permute-start | bytes 884744 | tf_op jit(solution)/shard_map/ppermute | solution.py:233
  268.9 4.7 %copy-start.4 = (bf16[384,384]{1,0:T(8,128)(2,1)S(1)}, bf16[384,384]{1,0:T(8,128)(2,1)}, u32[]{:S(2)}) copy-start(bf16[384,384]{1,0:T(8,128)(2,1)} %copy-done.3) | copy-start | bytes 884740
  268.9 4.7 %copy-start.8 = (bf16[384,384]{1,0:T(8,128)(2,1)S(1)}, bf16[384,384]{1,0:T(8,128)(2,1)}, u32[]{:S(2)}) copy-start(bf16[384,384]{1,0:T(8,128)(2,1)} %copy-done.7) | copy-start | bytes 884740
  273.6 3.5 %copy-start.6 = (bf16[384,384]{1,0:T(8,128)(2,1)S(1)}, bf16[384,384]{1,0:T(8,128)(2,1)}, u32[]{:S(2)}) copy-start(bf16[384,384]{1,0:T(8,128)(2,1)} %copy-done.5) | copy-start | bytes 884740
  280.7 7.3 %collective-permute-start.33 = (bf16[250,384]{1,0:T(8,128)(2,1)S(1)}, bf16[250,384]{1,0:T(8,128)(2,1)S(1)}, u32[]{:S(2)}, u32[]{:S(2)}) collective-permute-start(bf16[250,384]{1,0:T(8,128)(2,1)S(1)} %convert_element_type.65), channel_id=1, source_target_pairs={{0,16},{16,0},{1,17},{17,1},{2,18},{18,2},{3,19},{19,3},{4,20},{20... | collective-permute-start | bytes 576008 | tf_op jit(solution)/shard_map/ppermute | solution.py:346
Sparse Core Ops, SparseCore 0:
  9.6 44.9 all-gather.9
  56.9 43.9 all-gather.11
  166.9 87.1 all-gather.7

commit v8 on v7

--- a/solution.py
+++ b/solution.py
@@ -257,7 +257,7 @@
         live = dict(enumerate(first))
         for bit in bits:
             sent = {d: swap(v, bit) for d, v in live.items() if d & bit}
-            sent = yield sent, list(live.values())
+            sent = yield sent, [v for d, v in live.items() if d & bit]
             live = {d: v + sent[d | bit] for d, v in live.items() if not d & bit}
         mine = live[0]
         sent = [pick(mine, z + d) for d in range(1, nz)]
@@ -295,7 +295,7 @@
         out = rot_part(
             me, by_rows, whole_r, scale, ct, weighted, after(start, marks), c, paux, fan, nz, cuts
         )
-        first, g = out[:fan], out[fan]
+        first, g = after(out[:fan], waiting), out[fan]
         if c == 0:
             whole_r = out[fan + 1]
         gammas.append(g)

time: 297 us -> 298 us (level)
  waiting for transfers between devices: 108 us -> 114 us
  other arithmetic: 14.9 us -> 10.9 us
  starting transfers between devices: 32.9 us -> 29 us
    ppermute x12, starting transfers between devices: 20.6 us -> 15.1 us  [turn_z(): lax.ppermute(value, 'ao', [(i, (i + by * fan) % groups) for i in range(gr...]
    ppermute x21, waiting for transfers between devices: 15.7 us -> 19.7 us  [swap(): return lax.ppermute(value, 'ao', [(i, i ^ bit) for i in range(groups)])]
    add x6 -> x4, other arithmetic: 10.5 us -> 6.81 us  [reduce_steps(): live = {d: v + sent[d | bit] for d, v in live.items() if not d & bit}]
    unnamed x23 -> x29, local copies, waits for them, and re-layouts: 4.9 us -> 7.55 us
  transfers between devices with their start and end apart: 37 -> 37, of which waited for: 11 -> 12; matrix products, arithmetic and copies ran while one was open for 5% -> 4% of each run, Pallas kernels for 39% -> 39%
where the time goes in v8:
time: 298 us; the launch traced here: 296 us
  Pallas kernels  120 us (40%)
  waiting for transfers between devices  114 us (38%)
  starting transfers between devices  29 us (10%)
  between operations  13.4 us (4%)
  other arithmetic  10.9 us (4%)
  local copies, waits for them, and re-layouts  8.9 us (3%)
    pallas_call x2, Pallas kernels, rot_part(): pl.pallas_call(functools.partial(rot_kernel, paux, fan, nz, cuts), grid_s...  54.7 us
    pallas_call x2, Pallas kernels, occ_part(): pl.pallas_call(functools.partial(occ_kernel, paux), grid=(nscale,), in_sp...  53.1 us
    all_gather x1, waiting for transfers between devices, body(): whole_r = lax.all_gather(rot_coeff, 'ao', axis=0)  43.6 us
    ppermute x12, waiting for transfers between devices, turn_z(): lax.ppermute(value, 'ao', [(i, (i + by * fan) % groups) for i in range(gr...  42.8 us
    ppermute x21, waiting for transfers between devices, swap(): return lax.ppermute(value, 'ao', [(i, i ^ bit) for i in range(groups)])  19.7 us
    ppermute x12, starting transfers between devices, turn_z(): lax.ppermute(value, 'ao', [(i, (i + by * fan) % groups) for i in range(gr...  15.1 us
    ppermute x21, starting transfers between devices, swap(): return lax.ppermute(value, 'ao', [(i, i ^ bit) for i in range(groups)])  13.2 us
    unnamed x29, local copies, waits for them, and re-layouts  7.55 us
  transfers between devices with their start and end apart: 37, of which 12 were waited for; matrix products, arithmetic and copies ran while one was open for 4% of the time, Pallas kernels for 39%

profile of v8, /device:TPU:28, one launch (start us, length us, event | category | flops | bytes accessed | tf_op | source)
XLA Modules:
  0.0 296.0 jit_solution(14615009250471972871)
XLA Ops:
  6.5 0.7 all-gather.10.cloned.1.call-update
  7.3 0.7 all-gather.12.cloned.1.call-update
  8.1 1.1 copy.12
  9.1 0.8 copy.13.scale_ref
  10.0 1.0 convert_multiply_fusion
  11.0 43.6 %all-gather.10.cloned.1.call-done.m_ref = bf16[16,250,380]{2,1,0:T(8,128)(2,1)} async-done(((bf16[1,250,380]{2,1,0:T(8,128)(2,1)}), bf16[16,250,380]{2,1,0:T(8,128)(2,1)}) %all-gather.10.cloned.1.call-update) | async-done | bytes 3040016 | tf_op jit(solution)/shard_map/all_gather | solution.py:252
  54.6 27.9 %shard_map.55 = (bf16[4,384,384]{2,1,0:T(8,128)(2,1)S(1)}, bf16[4,384,384]{2,1,0:T(8,128)(2,1)S(1)}, bf16[4,384,384]{2,1,0:T(8,128)(2,1)}, bf16[4,384,384]{2,1,0...) custom-call(s32[1]{0:T(128)} %bitcast.8.me_ref, bf16[250,32,4000]{2,1,0:T(8,128)(2,1)} %bitcast.43, ...), custom_call_target="tpu_custom_call" | custom-call | flops 12288000000 | bytes 32000000 | tf_op jit(solution)/shard_map/pallas_call | solution.py:144
  83.0 4.2 %collective-permute-done = bf16[4,384,384]{2,1,0:T(8,128)(2,1)S(1)} collective-permute-done((bf16[4,384,384]{2,1,0:T(8,128)(2,1)S(1)}, bf16[4,384,384]{2,1,0:T(8,128)(2,1)S(1)}, u32[]{:S(2)}, u32[]{:S(2)}) %collective-permute-start) | collective-permute-done | bytes 1179680 | tf_op jit(solution)/shard_map/ppermute | solution.py:233
  87.7 0.6 copy-done.10
  88.3 1.6 add.216
  90.4 26.7 %shard_map.56 = (bf16[4,384,384]{2,1,0:T(8,128)(2,1)S(1)}, bf16[4,384,384]{2,1,0:T(8,128)(2,1)}, bf16[4,384,384]{2,1,0:T(8,128)(2,1)}, bf16[4,384,384]{2,1,0:T(8,128)(2,1)}, f32[16,1,384]{2,1,0:T(1,128)S(1)}) custom-call(s32[1]{0:T(128)} %bitcast.8.me_ref, bf16[250,32,4000]{2,1,0:T(8,128)(2,1)} %bitcast.44, bf16[4000,384]{1,0:T(8,128)(2,1)} %get-tuple-element.48.m_ref, ...), custom_call_target="tpu_custom_call" | custom-call | flops 12288000000 | bytes 32000000 | tf_op jit(solution)/shard_map/pallas_call | solution.py:144
  117.1 1.5 collective-permute-done.5
  118.6 1.0 copy-done.12
  120.5 0.6 collective-permute-start.3
  121.1 1.2 collective-permute-start.4
  122.8 1.7 collective-permute-done.7
  124.5 2.9 add.228
  128.2 1.0 copy-done.9
  129.9 2.0 collective-permute-start.12
  132.2 27.2 %shard_map.57 = (bf16[16,250,384]{2,1,0:T(8,128)(2,1)}, bf16[4000,384]{1,0:T(8,128)(2,1)S(1)}) custom-call(bf16[250,32,4000]{2,1,0:T(8,128)(2,1)} %bitcast.45, bf16[16,250,380]{2,1,0:T(8,128)(2,1)} %all-gather.12.cloned.1.call-done.m_ref, f32[10,32,1]{2,1,0:T(8,128)S(1)} %copy.13.scale_ref, f32[8,128]{1,0:T(8,128)S(1)} %broadcast_in_dim.11.tie_ref), custom_call_target="tpu_custom_call" | custom-call | flops 12288000000 | bytes 32000000 | tf_op jit(solution)/shard_map/pallas_call | solution.py:169
  159.5 1.7 copy-done.1
  161.2 1.8 fusion.5
  163.0 1.2 collective-permute-start.10
  164.2 2.7 collective-permute-start.8
  167.2 2.1 add_add_fusion
  169.4 1.5 collective-permute-start.15
  170.9 2.0 collective-permute-start.16
  172.8 1.3 collective-permute-start.17
  174.1 25.9 %shard_map.58.h_ref = bf16[16,250,384]{2,1,0:T(8,128)(2,1)} custom-call(bf16[250,32,4000]{2,1,0:T(8,128)(2,1)} %bitcast.46, bf16[4000,384]{1,0:T(8,128)(2,1)S(1)} %copy-done.2, f32[10,32,1]{2,1,0:T(8,128)S(1)} %copy.13.scale_ref, f32[8,128]{1,0:T(8,128)S(1)} %broadcast_in_dim.11.tie_ref), custom_call_target="tpu_custom_call" | custom-call | flops 12288000000 | bytes 32000000 | tf_op jit(solution)/shard_map/pallas_call | solution.py:169
  200.0 6.3 %collective-permute-done.16 = bf16[384,384]{1,0:T(8,128)(2,1)S(1)} collective-permute-done((bf16[384,384]{1,0:T(8,128)(2,1)S(1)}, bf16[384,384]{1,0:T(8,128)(2,1)S(1)}, u32[]{:S(2)}, u32[]{:S(2)}) %collective-permute-start.16) | collective-permute-done | bytes 294944 | tf_op jit(solution)/shard_map/ppermute | solution.py:236
  206.6 1.3 collective-permute-start.19
  207.8 1.9 collective-permute-start.20
  209.8 4.4 %collective-permute-start.21 = (bf16[384,384]{1,0:T(8,128)(2,1)S(1)}, bf16[384,384]{1,0:T(8,128)(2,1)S(1)}, u32[]{:S(2)}, u32[]{:S(2)}) collective-permute-start(bf16[384,384]{1,0:T(8,128)(2,1)S(1)} %fusion.2.rest_0_), channel_id=1, source_target_pairs={{0,2},{1,3},{2,0},{3,1},{4,6},{5,7},{6,4},{7,5},{8,10},{9,11},{10,... | collective-permute-start | bytes 884744 | tf_op jit(solution)/shard_map/ppermute | solution.py:233
  214.2 0.7 copy-done.3
  214.9 8.9 %collective-permute-done.18.rest_1_ = bf16[384,384]{1,0:T(8,128)(2,1)} collective-permute-done((bf16[384,384]{1,0:T(8,128)(2,1)S(1)}, bf16[384,384]{1,0:T(8,128)(2,1)}, u32[]{:S(2)}, u32[]{:S(2)}) %collective-permute-start.18) | collective-permute-done | bytes 294944 | tf_op jit(solution)/shard_map/ppermute | solution.py:236
  223.8 1.6 collective-permute-start.22
  225.4 27.5 %collective-permute-done.19.rest_2_ = bf16[384,384]{1,0:T(8,128)(2,1)} collective-permute-done((bf16[384,384]{1,0:T(8,128)(2,1)S(1)}, bf16[384,384]{1,0:T(8,128)(2,1)}, u32[]{:S(2)}, u32[]{:S(2)}) %collective-permute-start.19) | collective-permute-done | bytes 294944 | tf_op jit(solution)/shard_map/ppermute | solution.py:236
  253.0 1.9 collective-permute-start.23
  255.0 0.7 copy-done.7
  255.7 0.7 copy-done.5
  257.2 5.9 %collective-permute-done.23.rest_6_ = bf16[384,384]{1,0:T(8,128)(2,1)} collective-permute-done((bf16[384,384]{1,0:T(8,128)(2,1)}, bf16[384,384]{1,0:T(8,128)(2,1)}, u32[]{:S(2)}, u32[]{:S(2)}) %collective-permute-start.23) | collective-permute-done | bytes 294944 | tf_op jit(solution)/shard_map/ppermute | solution.py:233
  263.2 5.5 %collective-permute-done.24.rest_7_ = bf16[384,384]{1,0:T(8,128)(2,1)} collective-permute-done((bf16[384,384]{1,0:T(8,128)(2,1)}, bf16[384,384]{1,0:T(8,128)(2,1)}, u32[]{:S(2)}, u32[]{:S(2)}) %collective-permute-start.24) | collective-permute-done | bytes 294944 | tf_op jit(solution)/shard_map/ppermute | solution.py:233
  269.4 4.7 %shard_map.59.base_ref = f32[250,384]{1,0:T(8,128)S(1)} custom-call(f32[16]{0:T(128)S(1)} %get-tuple-element.95.gamma_ref, f32[250,384]{1,0:T(8,128)S(1)} %broadcast_in_dim.12.base_ref, bf16[16,250,384]{2,1,0:T(8,128)(2,1)S(1)} %copy-done, bf16[16,384,384]{2,1,0:T(8,128)(2,1)} %bitcast.47), custom_call_target="tpu_custom_call" | custom-call | flops 1179648000 | bytes 4718592 | tf_op jit(solution)/shard_map/pallas_call | solution.py:188
  274.1 3.5 %shard_map.60.base_ref = f32[250,384]{1,0:T(8,128)S(1)} custom-call(s32[8]{0:T(128)S(1)} %stack.71.owners_ref, f32[16]{0:T(128)S(1)} %get-tuple-element.96.gamma_ref, f32[250,384]{1,0:T(8,128)S(1)} %shard_map.59.base_ref, bf16[16,250,384]{2,1,0:T(8,128)(2,1)} %shard_map.58.h_ref, bf16[384,384]{1,0:T(8,128)(2,1)S(1)} %copy-done.4, ...), custom_call_target="tpu_custom_call" | custom-call | flops 589824000 | bytes 2359296 | tf_op jit(solution)/shard_map/pallas_call | solution.py:206
  277.8 3.6 %shard_map.61 = f32[250,384]{1,0:T(8,128)S(1)} custom-call(s32[8]{0:T(128)S(1)} %stack.62.owners_ref, f32[16]{0:T(128)S(1)} %get-tuple-element.96.gamma_ref, f32[250,384]{1,0:T(8,128)S(1)} %shard_map.60.base_ref, bf16[16,250,384]{2,1,0:T(8,128)(2,1)} %shard_map.58.h_ref, bf16[384,384]{1,0:T(8,128)(2,1)S(1)} %copy-done.6, ...), custom_call_target="tpu_custom_call" | custom-call | flops 589824000 | bytes 2359296 | tf_op jit(solution)/shard_map/pallas_call | solution.py:206
  281.4 0.6 collective-permute-start.33
  282.0 6.7 %collective-permute-done.33 = bf16[250,384]{1,0:T(8,128)(2,1)S(1)} collective-permute-done((bf16[250,384]{1,0:T(8,128)(2,1)S(1)}, bf16[250,384]{1,0:T(8,128)(2,1)S(1)}, u32[]{:S(2)}, u32[]{:S(2)}) %collective-permute-start.33) | collective-permute-done | bytes 192032 | tf_op jit(solution)/shard_map/ppermute | solution.py:346
  288.7 0.8 add_multiply_fusion
  (87 shorter events, 7.1 us)
Async XLA Ops:
  6.5 48.1 %all-gather.10.cloned.1.call-start = ((), (), s32[]{:S(2)}) async-start(), calls=%async_computation.1 | async-start | bytes 3342336 | tf_op jit(solution)/shard_map/all_gather | solution.py:252
  7.3 125.0 %all-gather.12.cloned.1.call-start = ((), (), s32[]{:S(2)}) async-start(), calls=%async_computation.2 | async-start | bytes 3342336 | tf_op jit(solution)/shard_map/all_gather | solution.py:253
  8.0 261.3 %all-gather.8.cloned.1.call-start = ((), (), s32[]{:S(2)}) async-start(), calls=%async_computation | async-start | bytes 5013504 | tf_op jit(solution)/shard_map/all_gather | solution.py:270
  82.5 4.7 %collective-permute-start = (bf16[4,384,384]{2,1,0:T(8,128)(2,1)S(1)}, bf16[4,384,384]{2,1,0:T(8,128)(2,1)S(1)}, u32[]{:S(2)}, u32[]{:S(2)}) collective-permute-start(bf16[4,384,384]{2,1,0:T(8,128)(2,1)S(1)} %get-tuple-element.54), channel_id=1, source_target_pairs={{0,1},{1,0},{2,3},{3,2},{4,5},{5,4},{6,7},{7,6},{8,9},{9,8},{10,11... | collective-permute-start | bytes 3538952 | tf_op jit(solution)/shard_map/ppermute | solution.py:233
  82.8 4.9 %collective-permute-start.1 = (bf16[4,384,384]{2,1,0:T(8,128)(2,1)}, bf16[4,384,384]{2,1,0:T(8,128)(2,1)S(1)}, u32[]{:S(2)}, u32[]{:S(2)}) collective-permute-start(bf16[4,384,384]{2,1,0:T(8,128)(2,1)} %get-tuple-element.55), channel_id=1, source_target_pairs={{0,1},{1,0},{2,3},{3,2},{4,5},{5,4},{6,7},{7,6},{8,9},{9,8},{10,11... | collective-permute-start | bytes 3538952 | tf_op jit(solution)/shard_map/ppermute | solution.py:233
  87.3 1.0 copy-start.10
  89.9 28.7 %collective-permute-start.5 = (bf16[4,384,384]{2,1,0:T(8,128)(2,1)S(1)}, bf16[4,384,384]{2,1,0:T(8,128)(2,1)S(1)}, u32[]{:S(2)}, u32[]{:S(2)}) collective-permute-start(bf16[4,384,384]{2,1,0:T(8,128)(2,1)S(1)} %add.216), channel_id=1, source_target_pairs={{0,2},{1,3},{2,0},{3,1},{4,6},{5,7},{6,4},{7,5},{8,10},{9,11},{10,... | collective-permute-start | bytes 3538952 | tf_op jit(solution)/shard_map/ppermute | solution.py:233
  118.6 1.0 copy-start.12
  119.6 3.2 %collective-permute-start.6 = (bf16[4,384,384]{2,1,0:T(8,128)(2,1)}, bf16[4,384,384]{2,1,0:T(8,128)(2,1)}, u32[]{:S(2)}, u32[]{:S(2)}) collective-permute-start(bf16[4,384,384]{2,1,0:T(8,128)(2,1)} %get-tuple-element.65), channel_id=1, source_target_pairs={{0,1},{1,0},{2,3},{3,2},{4,5},{5,4},{6,7},{7,6},{8,9},{9,8},{10,11... | collective-permute-start | bytes 3538952 | tf_op jit(solution)/shard_map/ppermute | solution.py:233
  119.6 4.9 %collective-permute-start.7 = (bf16[4,384,384]{2,1,0:T(8,128)(2,1)}, bf16[4,384,384]{2,1,0:T(8,128)(2,1)}, u32[]{:S(2)}, u32[]{:S(2)}) collective-permute-start(bf16[4,384,384]{2,1,0:T(8,128)(2,1)} %get-tuple-element.66), channel_id=1, source_target_pairs={{0,1},{1,0},{2,3},{3,2},{4,5},{5,4},{6,7},{7,6},{8,9},{9,8},{10,11... | collective-permute-start | bytes 3538952 | tf_op jit(solution)/shard_map/ppermute | solution.py:233
  120.4 7.5 %copy-start.11 = (bf16[4,384,384]{2,1,0:T(8,128)(2,1)S(1)}, bf16[4,384,384]{2,1,0:T(8,128)(2,1)}, u32[]{:S(2)}) copy-start(bf16[4,384,384]{2,1,0:T(8,128)(2,1)} %copy-done.10) | copy-start | bytes 3538948
  120.4 7.5 %copy-start.13 = (bf16[4,384,384]{2,1,0:T(8,128)(2,1)S(1)}, bf16[4,384,384]{2,1,0:T(8,128)(2,1)}, u32[]{:S(2)}) copy-start(bf16[4,384,384]{2,1,0:T(8,128)(2,1)} %copy-done.12) | copy-start | bytes 3538948
  120.4 9.5 %collective-permute-start.2 = (f32[32]{0:T(128)S(1)}, f32[32]{0:T(128)S(1)}, u32[]{:S(2)}, u32[]{:S(2)}) collective-permute-start(f32[32]{0:T(128)S(1)} %maximum_reduce_fusion), channel_id=1, source_target_pairs={{0,1},{1,0},{2,3},{3,2},{4,5},{5,4},{6,7},{7,6},{8,9},{9,8},{10,11... | collective-permute-start | bytes 392 | tf_op jit(solution)/shard_map/ppermute | solution.py:233
  120.5 11.4 %collective-permute-start.3 = (f32[32]{0:T(128)S(1)}, f32[32]{0:T(128)S(1)}, u32[]{:S(2)}, u32[]{:S(2)}) collective-permute-start(f32[32]{0:T(128)S(1)} %maximum_reduce_fusion), channel_id=1, source_target_pairs={{0,2},{1,3},{2,0},{3,1},{4,6},{5,7},{6,4},{7,5},{8,10},{9,11},{10,... | collective-permute-start | bytes 392 | tf_op jit(solution)/shard_map/ppermute | solution.py:233
  121.1 40.0 %collective-permute-start.4 = (f32[32]{0:T(128)S(1)}, f32[32]{0:T(128)S(1)}, u32[]{:S(2)}, u32[]{:S(2)}) collective-permute-start(f32[32]{0:T(128)S(1)} %maximum_reduce_fusion), channel_id=1, source_target_pairs={{0,3},{1,2},{2,1},{3,0},{4,7},{5,6},{6,5},{7,4},{8,11},{9,10},{10,... | collective-permute-start | bytes 392 | tf_op jit(solution)/shard_map/ppermute | solution.py:233
  127.4 33.8 %collective-permute-start.14 = (bf16[4,384,384]{2,1,0:T(8,128)(2,1)}, bf16[4,384,384]{2,1,0:T(8,128)(2,1)}, u32[]{:S(2)}, u32[]{:S(2)}) collective-permute-start(bf16[4,384,384]{2,1,0:T(8,128)(2,1)} %add.228), channel_id=1, source_target_pairs={{0,2},{1,3},{2,0},{3,1},{4,6},{5,7},{6,4},{7,5},{8,10},{9,11},{10,... | collective-permute-start | bytes 3538952 | tf_op jit(solution)/shard_map/ppermute | solution.py:233
  128.2 1.0 copy-start.9
  129.3 31.8 %collective-permute-start.11 = (bf16[384,384]{1,0:T(8,128)(2,1)S(1)}, bf16[384,384]{1,0:T(8,128)(2,1)S(1)}, u32[]{:S(2)}, u32[]{:S(2)}) collective-permute-start(bf16[384,384]{1,0:T(8,128)(2,1)S(1)} %get-tuple-element.94), channel_id=1, source_target_pairs={{0,4},{1,5},{2,6},{3,7},{4,8},{5,9},{6,10},{7,11},{8,12},{9,13},{1... | collective-permute-start | bytes 884744 | tf_op jit(solution)/shard_map/ppermute | solution.py:236
  129.9 31.3 %collective-permute-start.12 = (bf16[384,384]{1,0:T(8,128)(2,1)S(1)}, bf16[384,384]{1,0:T(8,128)(2,1)S(1)}, u32[]{:S(2)}, u32[]{:S(2)}) collective-permute-start(bf16[384,384]{1,0:T(8,128)(2,1)S(1)} %get-tuple-element.93), channel_id=1, source_target_pairs={{0,8},{1,9},{2,10},{3,11},{4,12},{5,13},{6,14},{7,15},{8,0},{9,1},... | collective-permute-start | bytes 884744 | tf_op jit(solution)/shard_map/ppermute | solution.py:236
  131.9 29.3 %collective-permute-start.13 = (bf16[384,384]{1,0:T(8,128)(2,1)S(1)}, bf16[384,384]{1,0:T(8,128)(2,1)S(1)}, u32[]{:S(2)}, u32[]{:S(2)}) collective-permute-start(bf16[384,384]{1,0:T(8,128)(2,1)S(1)} %get-tuple-element.92), channel_id=1, source_target_pairs={{0,12},{1,13},{2,14},{3,15},{4,0},{5,1},{6,2},{7,3},{8,4},{9,5},{1... | collective-permute-start | bytes 884744 | tf_op jit(solution)/shard_map/ppermute | solution.py:236
  159.5 1.7 copy-start.1
  163.0 9.8 %collective-permute-start.10 = (f32[32]{0:T(128)S(1)}, f32[32]{0:T(128)S(1)}, u32[]{:S(2)}, u32[]{:S(2)}) collective-permute-start(f32[32]{0:T(128)S(1)} %add_add_fusion.3), channel_id=1, source_target_pairs={{0,12},{1,13},{2,14},{3,15},{4,0},{5,1},{6,2},{7,3},{8,4},{9,5},{1... | collective-permute-start | bytes 392 | tf_op jit(solution)/shard_map/ppermute | solution.py:236
  164.2 35.8 %collective-permute-start.8 = (f32[32]{0:T(128)S(1)}, f32[32]{0:T(128)S(1)}, u32[]{:S(2)}, u32[]{:S(2)}) collective-permute-start(f32[32]{0:T(128)S(1)} %add_add_fusion.3), channel_id=1, source_target_pairs={{0,4},{1,5},{2,6},{3,7},{4,8},{5,9},{6,10},{7,11},{8,12},{9,13},{1... | collective-permute-start | bytes 392 | tf_op jit(solution)/shard_map/ppermute | solution.py:236
  166.9 33.1 %collective-permute-start.9 = (f32[32]{0:T(128)S(1)}, f32[32]{0:T(128)S(1)}, u32[]{:S(2)}, u32[]{:S(2)}) collective-permute-start(f32[32]{0:T(128)S(1)} %add_add_fusion.3), channel_id=1, source_target_pairs={{0,8},{1,9},{2,10},{3,11},{4,12},{5,13},{6,14},{7,15},{8,0},{9,1},... | collective-permute-start | bytes 392 | tf_op jit(solution)/shard_map/ppermute | solution.py:236
  167.2 6.9 %copy-start.2 = (bf16[4000,384]{1,0:T(8,128)(2,1)S(1)}, bf16[4000,384]{1,0:T(8,128)(2,1)}, u32[]{:S(2)}) copy-start(bf16[4000,384]{1,0:T(8,128)(2,1)} %copy-done.1) | copy-start | bytes 9216004
  169.4 30.6 %collective-permute-start.15 = (bf16[384,384]{1,0:T(8,128)(2,1)S(1)}, bf16[384,384]{1,0:T(8,128)(2,1)S(1)}, u32[]{:S(2)}, u32[]{:S(2)}) collective-permute-start(bf16[384,384]{1,0:T(8,128)(2,1)S(1)} %get-tuple-element.91), channel_id=1, source_target_pairs={{0,4},{1,5},{2,6},{3,7},{4,8},{5,9},{6,10},{7,11},{8,12},{9,13},{1... | collective-permute-start | bytes 884744 | tf_op jit(solution)/shard_map/ppermute | solution.py:236
  170.9 35.5 %collective-permute-start.16 = (bf16[384,384]{1,0:T(8,128)(2,1)S(1)}, bf16[384,384]{1,0:T(8,128)(2,1)S(1)}, u32[]{:S(2)}, u32[]{:S(2)}) collective-permute-start(bf16[384,384]{1,0:T(8,128)(2,1)S(1)} %get-tuple-element.90), channel_id=1, source_target_pairs={{0,8},{1,9},{2,10},{3,11},{4,12},{5,13},{6,14},{7,15},{8,0},{9,1},... | collective-permute-start | bytes 884744 | tf_op jit(solution)/shard_map/ppermute | solution.py:236
  172.8 33.5 %collective-permute-start.17 = (bf16[384,384]{1,0:T(8,128)(2,1)S(1)}, bf16[384,384]{1,0:T(8,128)(2,1)S(1)}, u32[]{:S(2)}, u32[]{:S(2)}) collective-permute-start(bf16[384,384]{1,0:T(8,128)(2,1)S(1)} %get-tuple-element.89), channel_id=1, source_target_pairs={{0,12},{1,13},{2,14},{3,15},{4,0},{5,1},{6,2},{7,3},{8,4},{9,5},{1... | collective-permute-start | bytes 884744 | tf_op jit(solution)/shard_map/ppermute | solution.py:236
  174.1 95.2 %copy-start = (bf16[16,250,384]{2,1,0:T(8,128)(2,1)S(1)}, bf16[16,250,384]{2,1,0:T(8,128)(2,1)}, u32[]{:S(2)}) copy-start(bf16[16,250,384]{2,1,0:T(8,128)(2,1)} %get-tuple-element.71.h_ref) | copy-start | bytes 9216004
  206.5 17.3 %collective-permute-start.18 = (bf16[384,384]{1,0:T(8,128)(2,1)S(1)}, bf16[384,384]{1,0:T(8,128)(2,1)}, u32[]{:S(2)}, u32[]{:S(2)}) collective-permute-start(bf16[384,384]{1,0:T(8,128)(2,1)S(1)} %fusion.2.rest_0_), channel_id=1, source_target_pairs={{0,4},{1,5},{2,6},{3,7},{4,8},{5,9},{6,10},{7,11},{8,12},{9,13},{1... | collective-permute-start | bytes 884744 | tf_op jit(solution)/shard_map/ppermute | solution.py:236
  206.6 46.4 %collective-permute-start.19 = (bf16[384,384]{1,0:T(8,128)(2,1)S(1)}, bf16[384,384]{1,0:T(8,128)(2,1)}, u32[]{:S(2)}, u32[]{:S(2)}) collective-permute-start(bf16[384,384]{1,0:T(8,128)(2,1)S(1)} %fusion.2.rest_0_), channel_id=1, source_target_pairs={{0,8},{1,9},{2,10},{3,11},{4,12},{5,13},{6,14},{7,15},{8,0},{9,1},... | collective-permute-start | bytes 884744 | tf_op jit(solution)/shard_map/ppermute | solution.py:236
  207.8 47.0 %collective-permute-start.20 = (bf16[384,384]{1,0:T(8,128)(2,1)S(1)}, bf16[384,384]{1,0:T(8,128)(2,1)}, u32[]{:S(2)}, u32[]{:S(2)}) collective-permute-start(bf16[384,384]{1,0:T(8,128)(2,1)S(1)} %fusion.2.rest_0_), channel_id=1, source_target_pairs={{0,12},{1,13},{2,14},{3,15},{4,0},{5,1},{6,2},{7,3},{8,4},{9,5},{1... | collective-permute-start | bytes 884744 | tf_op jit(solution)/shard_map/ppermute | solution.py:236
  209.8 45.2 %collective-permute-start.21 = (bf16[384,384]{1,0:T(8,128)(2,1)S(1)}, bf16[384,384]{1,0:T(8,128)(2,1)S(1)}, u32[]{:S(2)}, u32[]{:S(2)}) collective-permute-start(bf16[384,384]{1,0:T(8,128)(2,1)S(1)} %fusion.2.rest_0_), channel_id=1, source_target_pairs={{0,2},{1,3},{2,0},{3,1},{4,6},{5,7},{6,4},{7,5},{8,10},{9,11},{10,... | collective-permute-start | bytes 884744 | tf_op jit(solution)/shard_map/ppermute | solution.py:233
  214.2 40.8 %collective-permute-start.25 = (bf16[384,384]{1,0:T(8,128)(2,1)S(1)}, bf16[384,384]{1,0:T(8,128)(2,1)S(1)}, u32[]{:S(2)}, u32[]{:S(2)}) collective-permute-start(bf16[384,384]{1,0:T(8,128)(2,1)S(1)} %fusion.2.rest_0_), channel_id=1, source_target_pairs={{0,1},{1,0},{2,3},{3,2},{4,5},{5,4},{6,7},{7,6},{8,9},{9,8},{10,11... | collective-permute-start | bytes 884744 | tf_op jit(solution)/shard_map/ppermute | solution.py:233
  223.8 32.8 %collective-permute-start.22 = (bf16[384,384]{1,0:T(8,128)(2,1)}, bf16[384,384]{1,0:T(8,128)(2,1)}, u32[]{:S(2)}, u32[]{:S(2)}) collective-permute-start(bf16[384,384]{1,0:T(8,128)(2,1)} %collective-permute-done.18.rest_1_), channel_id=1, source_target_pairs={{0,2},{1,3},{2,0},{3,1},{4,6},{5,7},{6,4},{7,5},{8,10},{9,11},{10,... | collective-permute-start | bytes 884744 | tf_op jit(solution)/shard_map/ppermute | solution.py:233
  253.0 10.2 %collective-permute-start.23 = (bf16[384,384]{1,0:T(8,128)(2,1)}, bf16[384,384]{1,0:T(8,128)(2,1)}, u32[]{:S(2)}, u32[]{:S(2)}) collective-permute-start(bf16[384,384]{1,0:T(8,128)(2,1)} %collective-permute-done.19.rest_2_), channel_id=1, source_target_pairs={{0,2},{1,3},{2,0},{3,1},{4,6},{5,7},{6,4},{7,5},{8,10},{9,11},{10,... | collective-permute-start | bytes 884744 | tf_op jit(solution)/shard_map/ppermute | solution.py:233
  254.9 13.8 %collective-permute-start.24 = (bf16[384,384]{1,0:T(8,128)(2,1)}, bf16[384,384]{1,0:T(8,128)(2,1)}, u32[]{:S(2)}, u32[]{:S(2)}) collective-permute-start(bf16[384,384]{1,0:T(8,128)(2,1)} %collective-permute-done.20.rest_3_), channel_id=1, source_target_pairs={{0,2},{1,3},{2,0},{3,1},{4,6},{5,7},{6,4},{7,5},{8,10},{9,11},{10,... | collective-permute-start | bytes 884744 | tf_op jit(solution)/shard_map/ppermute | solution.py:233
  255.0 13.6 %collective-permute-start.26 = (bf16[384,384]{1,0:T(8,128)(2,1)}, bf16[384,384]{1,0:T(8,128)(2,1)}, u32[]{:S(2)}, u32[]{:S(2)}) collective-permute-start(bf16[384,384]{1,0:T(8,128)(2,1)} %collective-permute-done.18.rest_1_), channel_id=1, source_target_pairs={{0,1},{1,0},{2,3},{3,2},{4,5},{5,4},{6,7},{7,6},{8,9},{9,8},{10,11... | collective-permute-start | bytes 884744 | tf_op jit(solution)/shard_map/ppermute | solution.py:233
  256.5 12.7 %collective-permute-start.27 = (bf16[384,384]{1,0:T(8,128)(2,1)}, bf16[384,384]{1,0:T(8,128)(2,1)}, u32[]{:S(2)}, u32[]{:S(2)}) collective-permute-start(bf16[384,384]{1,0:T(8,128)(2,1)} %collective-permute-done.19.rest_2_), channel_id=1, source_target_pairs={{0,1},{1,0},{2,3},{3,2},{4,5},{5,4},{6,7},{7,6},{8,9},{9,8},{10,11... | collective-permute-start | bytes 884744 | tf_op jit(solution)/shard_map/ppermute | solution.py:233
  256.6 21.1 %collective-permute-start.28 = (bf16[384,384]{1,0:T(8,128)(2,1)}, bf16[384,384]{1,0:T(8,128)(2,1)}, u32[]{:S(2)}, u32[]{:S(2)}) collective-permute-start(bf16[384,384]{1,0:T(8,128)(2,1)} %collective-permute-done.20.rest_3_), channel_id=1, source_target_pairs={{0,1},{1,0},{2,3},{3,2},{4,5},{5,4},{6,7},{7,6},{8,9},{9,8},{10,11... | collective-permute-start | bytes 884744 | tf_op jit(solution)/shard_map/ppermute | solution.py:233
  263.1 14.6 %collective-permute-start.29 = (bf16[384,384]{1,0:T(8,128)(2,1)}, bf16[384,384]{1,0:T(8,128)(2,1)}, u32[]{:S(2)}, u32[]{:S(2)}) collective-permute-start(bf16[384,384]{1,0:T(8,128)(2,1)} %copy-done.7), channel_id=1, source_target_pairs={{0,1},{1,0},{2,3},{3,2},{4,5},{5,4},{6,7},{7,6},{8,9},{9,8},{10,11... | collective-permute-start | bytes 884744 | tf_op jit(solution)/shard_map/ppermute | solution.py:233
  268.6 9.1 %collective-permute-start.30 = (bf16[384,384]{1,0:T(8,128)(2,1)}, bf16[384,384]{1,0:T(8,128)(2,1)}, u32[]{:S(2)}, u32[]{:S(2)}) collective-permute-start(bf16[384,384]{1,0:T(8,128)(2,1)} %collective-permute-done.22.rest_5_), channel_id=1, source_target_pairs={{0,1},{1,0},{2,3},{3,2},{4,5},{5,4},{6,7},{7,6},{8,9},{9,8},{10,11... | collective-permute-start | bytes 884744 | tf_op jit(solution)/shard_map/ppermute | solution.py:233
  268.6 9.1 %collective-permute-start.31 = (bf16[384,384]{1,0:T(8,128)(2,1)}, bf16[384,384]{1,0:T(8,128)(2,1)}, u32[]{:S(2)}, u32[]{:S(2)}) collective-permute-start(bf16[384,384]{1,0:T(8,128)(2,1)} %collective-permute-done.23.rest_6_), channel_id=1, source_target_pairs={{0,1},{1,0},{2,3},{3,2},{4,5},{5,4},{6,7},{7,6},{8,9},{9,8},{10,11... | collective-permute-start | bytes 884744 | tf_op jit(solution)/shard_map/ppermute | solution.py:233
  269.2 8.6 %collective-permute-start.32 = (bf16[384,384]{1,0:T(8,128)(2,1)}, bf16[384,384]{1,0:T(8,128)(2,1)}, u32[]{:S(2)}, u32[]{:S(2)}) collective-permute-start(bf16[384,384]{1,0:T(8,128)(2,1)} %collective-permute-done.24.rest_7_), channel_id=1, source_target_pairs={{0,1},{1,0},{2,3},{3,2},{4,5},{5,4},{6,7},{7,6},{8,9},{9,8},{10,11... | collective-permute-start | bytes 884744 | tf_op jit(solution)/shard_map/ppermute | solution.py:233
  269.3 4.8 %copy-start.4 = (bf16[384,384]{1,0:T(8,128)(2,1)S(1)}, bf16[384,384]{1,0:T(8,128)(2,1)}, u32[]{:S(2)}) copy-start(bf16[384,384]{1,0:T(8,128)(2,1)} %copy-done.3) | copy-start | bytes 884740
  269.4 4.8 %copy-start.8 = (bf16[384,384]{1,0:T(8,128)(2,1)S(1)}, bf16[384,384]{1,0:T(8,128)(2,1)}, u32[]{:S(2)}) copy-start(bf16[384,384]{1,0:T(8,128)(2,1)} %copy-done.7) | copy-start | bytes 884740
  274.1 3.6 %copy-start.6 = (bf16[384,384]{1,0:T(8,128)(2,1)S(1)}, bf16[384,384]{1,0:T(8,128)(2,1)}, u32[]{:S(2)}) copy-start(bf16[384,384]{1,0:T(8,128)(2,1)} %copy-done.5) | copy-start | bytes 884740
  281.4 7.3 %collective-permute-start.33 = (bf16[250,384]{1,0:T(8,128)(2,1)S(1)}, bf16[250,384]{1,0:T(8,128)(2,1)S(1)}, u32[]{:S(2)}, u32[]{:S(2)}) collective-permute-start(bf16[250,384]{1,0:T(8,128)(2,1)S(1)} %convert_element_type.65), channel_id=1, source_target_pairs={{0,16},{16,0},{1,17},{17,1},{2,18},{18,2},{3,19},{19,3},{4,20},{20... | collective-permute-start | bytes 576008 | tf_op jit(solution)/shard_map/ppermute | solution.py:346
  (3 other events, 2.2 us)
Sparse Core Ops, SparseCore 0:
  9.6 44.9 all-gather.9
  56.9 44.1 all-gather.11
  163.2 88.6 all-gather.7
